TPU v7x, 32 devices: a whole 2x2x4 slice. The times are simulated.
32 devices in a mesh: grp: 2 (over x), freq: 8 (over z, y), src: 2 (over core).
Axes of the slice: x: 2, y: 2, z: 4, core: 2. Of those that a mesh axis runs over, the one named last changes fastest.
Arguments:
- kernel: bfloat16 [4, 64, 320, 8192], P('grp', 'freq', None, 'src'), parts along dimension 0, may hold values from -0.0625 to 0.0625
- data: float32 [4, 64, 320, 8], P('grp', 'freq'), parts along dimension 0, may hold values from -300 to 300
- win_start: int32 [16], P('grp'), parts along dimension 0, may hold values from 0 to 31
- win_end: int32 [16], P('grp'), parts along dimension 0, may hold values from 64 to 128
Outputs:
- estimate: float32 [4, 64, 8, 8192], P('grp', 'freq', None, 'src'), parts along dimension 0
- residual: float32 [4, 64, 320, 8], P('grp', 'freq', 'src'), parts along dimension 0
There are 2 independent parts, one for each index of `grp`. A program takes and returns all parts, laid end to end along the dimension named above; each array names one. Nothing has to cross between parts.
All inputs are finite; a program needn't handle non-finite values.
Results may differ from a plain program's by a relative error of at most 0.006.
Values may be sent and summed in bfloat16 or wider, within the bound.
No kernel may reach another device: no remote copies, remote signals or barrier semaphores. Data moves between devices by JAX's collectives and lax.ppermute only.
A program may use at most 128 MiB of HBM per device.

v0:
```python
import math

import jax
import jax.numpy as jnp
from jax import lax
from jax.sharding import PartitionSpec as P

F = 64
ITERS = 2
NT = 128


def window_mask(starts, ends):
    samples = jnp.arange(NT, dtype=jnp.int32)[:, None]
    inside = (samples >= starts[None, :]) & (samples < ends[None, :])
    return inside.astype(jnp.float32)


def sine_tables():
    samples = jnp.arange(NT, dtype=jnp.int32)[:, None]
    freqs = jnp.arange(F, dtype=jnp.int32)[None, :]
    phase = (samples * freqs % NT).astype(jnp.float32) * (2.0 * math.pi / NT)
    return (jnp.cos(phase), jnp.sin(phase))


def apply_taper(gradient, window):
    cos_table, sin_table = sine_tables()
    norm_scale = F ** (-0.5)
    highest = lax.Precision.HIGHEST
    signal = norm_scale * (
        jnp.einsum("tf,fvs->tvs", cos_table, gradient[0], precision=highest)
        - jnp.einsum("tf,fvs->tvs", sin_table, gradient[1], precision=highest)
    )
    signal = signal * window[:, :, None]
    real_part = norm_scale * jnp.einsum("tf,tvs->fvs", cos_table, signal, precision=highest)
    imag_part = -norm_scale * jnp.einsum("tf,tvs->fvs", sin_table, signal, precision=highest)
    return jnp.stack([real_part, imag_part])


def adjoint(kernel, resid_b):

    def product(left, right):
        return jnp.einsum("frv,frs->fvs", left, right, preferred_element_type=jnp.float32)

    real_part = product(resid_b[0], kernel[0]) + product(resid_b[1], kernel[1])
    imag_part = product(resid_b[1], kernel[0]) - product(resid_b[0], kernel[1])
    return jnp.stack([real_part, imag_part])


def forward(kernel, field_b):

    def product(left, right):
        return jnp.einsum("frs,fvs->frv", left, right, preferred_element_type=jnp.float32)

    real_part = product(kernel[0], field_b[0]) - product(kernel[1], field_b[1])
    imag_part = product(kernel[0], field_b[1]) + product(kernel[1], field_b[0])
    return jnp.stack([real_part, imag_part])


def body(kernel, data, win_start, win_end):
    freq_count = lax.axis_size("freq")
    src_count = lax.axis_size("src")
    receivers = kernel.shape[2]
    points = data.shape[3]
    local_points = points // freq_count
    first_point = lax.axis_index("freq") * local_points
    starts = lax.dynamic_slice_in_dim(win_start, first_point, local_points)
    ends = lax.dynamic_slice_in_dim(win_end, first_point, local_points)
    window = window_mask(starts, ends)
    share_rows = receivers // src_count
    first_row = lax.axis_index("src") * share_rows
    estimate = jnp.zeros((2, kernel.shape[1], points, kernel.shape[3]), jnp.float32)
    residual = data
    resid_share = lax.dynamic_slice_in_dim(data, first_row, share_rows, 2)
    resid_b = data.astype(jnp.bfloat16)
    for iteration in range(ITERS):
        gradient = adjoint(kernel, resid_b)
        regrouped = lax.all_to_all(gradient, "freq", split_axis=2, concat_axis=1, tiled=True)
        direction = lax.all_to_all(
            apply_taper(regrouped, window), "freq", split_axis=1, concat_axis=2, tiled=True
        )
        partial_image = forward(kernel, direction.astype(jnp.bfloat16))
        projected = lax.psum(partial_image, "src")
        image_part = lax.dynamic_slice_in_dim(projected, first_row, share_rows, 2)
        alignment = jnp.sum(gradient * direction)
        curvature = jnp.sum(image_part * image_part)
        alignment, curvature = lax.psum((alignment, curvature), ("freq", "src"))
        step_length = alignment / curvature
        estimate = estimate + step_length * direction
        residual = residual - step_length * projected
        resid_share = lax.dynamic_slice_in_dim(residual, first_row, share_rows, 2)
        resid_b = residual.astype(jnp.bfloat16)
    return (estimate, resid_share)


def solution(mesh):
    in_specs = (P("grp", "freq", None, "src"), P("grp", "freq", None, None), P("grp"), P("grp"))
    out_specs = (P("grp", "freq", None, "src"), P("grp", "freq", "src", None))
    return jax.shard_map(body, mesh=mesh, in_specs=in_specs, out_specs=out_specs, check_vma=False)
```

profile of v0, /device:TPU:0, one launch (start us, length us, event | category | flops | bytes accessed | tf_op | source)
XLA Modules:
  0.0 523.1 jit_solution(10781846412591260246)
XLA Ops:
  8.1 8.4 %fusion.12 = f32[8,8,4096]{2,1,0:T(8,128)S(1)} fusion(bf16[2,8,320,4096]{3,2,1,0:T(8,128)(2,1)} %param.4, bf16[2,8,320,8]{2,3,1,0:T(8,128)(2,1)S(1)} %convert_element_type.34), kind=kOutput, calls=%fused_computation.12 | convolution fusion | flops 167772160 | bytes 22069248 | tf_op jit(solution)/shard_map/frv,frs->fvs/dot_general | solution.py:43
  16.5 8.4 %fusion.14 = f32[8,8,4096]{2,1,0:T(8,128)S(1)} fusion(bf16[2,8,320,4096]{3,2,1,0:T(8,128)(2,1)} %param.4, bf16[2,8,320,8]{2,3,1,0:T(8,128)(2,1)S(1)} %convert_element_type.34), kind=kOutput, calls=%fused_computation.14 | convolution fusion | flops 167772160 | bytes 22069248 | tf_op jit(solution)/shard_map/frv,frs->fvs/dot_general | solution.py:43
  25.0 8.4 %fusion.47 = f32[1,8,8,4096]{3,2,1,0:T(8,128)S(1)} fusion(f32[8,8,4096]{2,1,0:T(8,128)S(1)} %fusion.12, bf16[2,8,320,4096]{3,2,1,0:T(8,128)(2,1)} %param.4, bf16[2,8,320,8]{2,3,1,0:T(8,128)(2,1)S(1)} %convert_element_type.34), kind=kOutput, calls=%fused_computation.47 | convolution fusion | flops 168034304 | bytes 23117824 | tf_op jit(solution)/shard_map/frv,frs->fvs/dot_general | solution.py:43
  33.4 8.4 %fusion.41 = f32[1,8,8,4096]{3,2,1,0:T(8,128)S(1)} fusion(f32[8,8,4096]{2,1,0:T(8,128)S(1)} %fusion.14, bf16[2,8,320,4096]{3,2,1,0:T(8,128)(2,1)} %param.4, bf16[2,8,320,8]{2,3,1,0:T(8,128)(2,1)S(1)} %convert_element_type.34), kind=kOutput, calls=%fused_computation.45 | convolution fusion | flops 168034304 | bytes 23117824 | tf_op jit(solution)/shard_map/frv,frs->fvs/dot_general | solution.py:43
  55.7 45.6 %all-to-all-done = f32[2,8,8,4096]{3,1,0,2:T(8,128)S(1)} async-done(((f32[2,8,8,4096]{3,1,0,2:T(8,128)}), f32[2,8,8,4096]{3,1,0,2:T(8,128)S(1)}, u32[]{:S(2)}, u32[]{:S(2)}) %all-to-all-start) | async-done | bytes 2097184 | tf_op jit(solution)/shard_map/all_to_all | solution.py:78
  117.0 47.4 %all-to-all-done.1 = f32[2,64,1,4096]{3,2,0,1:T(1,128)} async-done(((f32[2,64,1,4096]{3,2,0,1:T(1,128)}), f32[2,64,1,4096]{3,2,0,1:T(1,128)}, u32[]{:S(2)}, u32[]{:S(2)}) %all-to-all-start.1) | async-done | bytes 2097184 | tf_op jit(solution)/shard_map/all_to_all | solution.py:79
  168.7 9.8 %fusion.8 = f32[8,8,320]{2,1,0:T(8,128)S(1)} fusion(bf16[2,8,320,4096]{3,2,1,0:T(8,128)(2,1)} %param.4, bf16[2,8,8,4096]{3,2,1,0:T(8,128)(2,1)S(1)} %bitcast.192), kind=kOutput, calls=%fused_computation.8 | convolution fusion | flops 167772160 | bytes 21577728 | tf_op jit(solution)/shard_map/frs,fvs->frv/dot_general | solution.py:53
  178.5 9.8 %fusion.10 = f32[8,8,320]{2,1,0:T(8,128)S(1)} fusion(bf16[2,8,320,4096]{3,2,1,0:T(8,128)(2,1)} %param.4, bf16[2,8,8,4096]{3,2,1,0:T(8,128)(2,1)S(1)} %bitcast.193), kind=kOutput, calls=%fused_computation.10 | convolution fusion | flops 167772160 | bytes 21577728 | tf_op jit(solution)/shard_map/frs,fvs->frv/dot_general | solution.py:53
  188.2 9.8 %fusion.90 = f32[1,8,320,8]{2,3,1,0:T(8,128)S(1)} fusion(f32[8,8,320]{2,1,0:T(8,128)S(1)} %fusion.8, bf16[2,8,320,4096]{3,2,1,0:T(8,128)(2,1)} %param.4, bf16[2,8,8,4096]{3,2,1,0:T(8,128)(2,1)S(1)} %bitcast.194), kind=kOutput, calls=%fused_computation.88 | convolution fusion | flops 167792640 | bytes 21676032 | tf_op jit(solution)/shard_map/frs,fvs->frv/dot_general | solution.py:53
  198.0 9.8 %fusion.84 = f32[1,8,320,8]{2,3,1,0:T(8,128)S(1)} fusion(f32[8,8,320]{2,1,0:T(8,128)S(1)} %fusion.10, bf16[2,8,320,4096]{3,2,1,0:T(8,128)(2,1)} %param.4, bf16[2,8,8,4096]{3,2,1,0:T(8,128)(2,1)S(1)} %bitcast.195), kind=kOutput, calls=%fused_computation.86 | convolution fusion | flops 167792640 | bytes 21676032 | tf_op jit(solution)/shard_map/frs,fvs->frv/dot_general | solution.py:53
  211.8 14.0 %all-reduce.5.cloned.1.call-done = f32[2,8,320,8]{2,3,1,0:T(8,128)} async-done(((f32[2,8,320,8]{2,3,1,0:T(8,128)}), f32[2,8,320,8]{2,3,1,0:T(8,128)}) %all-reduce.5.cloned.1.call-update) | async-done | bytes 163856 | tf_op jit(solution)/shard_map/psum | solution.py:83
  227.4 34.5 %all-reduce.1 = (f32[]{:T(128)}, f32[]{:T(128)}) all-reduce(f32[]{:T(128)} %fusion.80, f32[]{:T(128)} %multiply_reduce_fusion.1), channel_id=1, replica_groups=mesh['grp'=2,'freq'=8,'src'=2] {'freq','src'}, use_global_device_ids=true, to_apply=%region_1.2 | all-reduce | flops 2 | bytes 16 | tf_op jit(solution)/shard_map/psum | solution.py:87
  264.2 8.4 %fusion.4 = f32[8,8,4096]{2,1,0:T(8,128)S(1)} fusion(bf16[2,8,320,4096]{3,2,1,0:T(8,128)(2,1)} %param.4, bf16[2,8,320,8]{2,3,1,0:T(8,128)(2,1)S(1)} %get-tuple-element.6), kind=kOutput, calls=%fused_computation.4 | convolution fusion | flops 167772160 | bytes 22069248 | tf_op jit(solution)/shard_map/frv,frs->fvs/dot_general | solution.py:43
  272.7 8.4 %fusion.6 = f32[8,8,4096]{2,1,0:T(8,128)S(1)} fusion(bf16[2,8,320,4096]{3,2,1,0:T(8,128)(2,1)} %param.4, bf16[2,8,320,8]{2,3,1,0:T(8,128)(2,1)S(1)} %get-tuple-element.6), kind=kOutput, calls=%fused_computation.6 | convolution fusion | flops 167772160 | bytes 22069248 | tf_op jit(solution)/shard_map/frv,frs->fvs/dot_general | solution.py:43
  281.1 8.4 %fusion.59 = f32[1,8,8,4096]{3,2,1,0:T(8,128)S(1)} fusion(f32[8,8,4096]{2,1,0:T(8,128)S(1)} %fusion.4, bf16[2,8,320,4096]{3,2,1,0:T(8,128)(2,1)} %param.4, bf16[2,8,320,8]{2,3,1,0:T(8,128)(2,1)S(1)} %get-tuple-element.6), kind=kOutput, calls=%fused_computation.51 | convolution fusion | flops 168034304 | bytes 23117824 | tf_op jit(solution)/shard_map/frv,frs->fvs/dot_general | solution.py:43
  289.5 8.4 %fusion.53 = f32[1,8,8,4096]{3,2,1,0:T(8,128)S(1)} fusion(f32[8,8,4096]{2,1,0:T(8,128)S(1)} %fusion.6, bf16[2,8,320,4096]{3,2,1,0:T(8,128)(2,1)} %param.4, bf16[2,8,320,8]{2,3,1,0:T(8,128)(2,1)S(1)} %get-tuple-element.6), kind=kOutput, calls=%fused_computation.49 | convolution fusion | flops 168034304 | bytes 23117824 | tf_op jit(solution)/shard_map/frv,frs->fvs/dot_general | solution.py:43
  300.2 49.5 %all_to_all.66 = f32[2,8,8,4096]{3,1,0,2:T(8,128)S(1)} all-to-all(f32[2,8,8,4096]{3,1,0,2:T(8,128)S(1)} %copy.17), channel_id=1, replica_groups=mesh['grp'=2,'freq'=8,'src'=2] {'freq'}, dimensions={2} | all-to-all | bytes 4194304 | tf_op jit(solution)/shard_map/all_to_all | solution.py:78
  359.4 51.5 %all_to_all.67 = f32[2,64,1,4096]{3,2,0,1:T(1,128)S(1)} all-to-all(f32[2,64,1,4096]{3,2,0,1:T(1,128)S(1)} %copy.19), channel_id=1, replica_groups=mesh['grp'=2,'freq'=8,'src'=2] {'freq'}, dimensions={1} | all-to-all | bytes 4194304 | tf_op jit(solution)/shard_map/all_to_all | solution.py:79
  415.0 9.8 %fusion = f32[8,8,320]{2,1,0:T(8,128)S(1)} fusion(bf16[2,8,320,4096]{3,2,1,0:T(8,128)(2,1)} %param.4, bf16[2,8,8,4096]{3,2,1,0:T(8,128)(2,1)S(1)} %bitcast.196), kind=kOutput, calls=%fused_computation | convolution fusion | flops 167772160 | bytes 21577728 | tf_op jit(solution)/shard_map/frs,fvs->frv/dot_general | solution.py:53
  424.7 9.8 %fusion.2 = f32[8,8,320]{2,1,0:T(8,128)S(1)} fusion(bf16[2,8,320,4096]{3,2,1,0:T(8,128)(2,1)} %param.4, bf16[2,8,8,4096]{3,2,1,0:T(8,128)(2,1)S(1)} %bitcast.197), kind=kOutput, calls=%fused_computation.2 | convolution fusion | flops 167772160 | bytes 21577728 | tf_op jit(solution)/shard_map/frs,fvs->frv/dot_general | solution.py:53
  434.5 9.8 %fusion.102 = f32[1,8,320,8]{2,3,1,0:T(8,128)S(1)} fusion(f32[8,8,320]{2,1,0:T(8,128)S(1)} %fusion, bf16[2,8,320,4096]{3,2,1,0:T(8,128)(2,1)} %param.4, bf16[2,8,8,4096]{3,2,1,0:T(8,128)(2,1)S(1)} %bitcast.198), kind=kOutput, calls=%fused_computation.92 | convolution fusion | flops 167792640 | bytes 21676032 | tf_op jit(solution)/shard_map/frs,fvs->frv/dot_general | solution.py:53
  444.3 10.1 %fusion.96 = f32[1,8,320,8]{2,3,1,0:T(8,128)S(1)} fusion(f32[8,8,320]{2,1,0:T(8,128)S(1)} %fusion.2, bf16[2,8,320,4096]{3,2,1,0:T(8,128)(2,1)} %param.4, bf16[2,8,8,4096]{3,2,1,0:T(8,128)(2,1)S(1)} %bitcast.199), kind=kOutput, calls=%fused_computation.90 | convolution fusion | flops 167792640 | bytes 21676032 | tf_op jit(solution)/shard_map/frs,fvs->frv/dot_general | solution.py:53
  458.7 13.5 %all-reduce.7.cloned.1.call-done = f32[2,8,320,8]{2,3,1,0:T(8,128)} async-done(((f32[2,8,320,8]{2,3,1,0:T(8,128)}), f32[2,8,320,8]{2,3,1,0:T(8,128)}) %all-reduce.7.cloned.1.call-update) | async-done | bytes 163856 | tf_op jit(solution)/shard_map/psum | solution.py:83
  473.8 34.5 %all-reduce = (f32[]{:T(128)}, f32[]{:T(128)}) all-reduce(f32[]{:T(128)} %fusion.78, f32[]{:T(128)} %multiply_reduce_fusion), channel_id=1, replica_groups=mesh['grp'=2,'freq'=8,'src'=2] {'freq','src'}, use_global_device_ids=true, to_apply=%region_6.7 | all-reduce | flops 2 | bytes 16 | tf_op jit(solution)/shard_map/psum | solution.py:87
  (55 shorter events, 69.2 us)
Async XLA Ops:
  41.8 1.0 copy-start.1
  45.4 7.7 %copy-start.5 = (s32[8]{0:T(128)S(1)}, s32[8]{0:T(128)}, u32[]{:S(2)}) copy-start(s32[8]{0:T(128)} %param.7) | copy-start | bytes 100
  45.4 8.3 %copy-start.6 = (s32[8]{0:T(128)S(1)}, s32[8]{0:T(128)}, u32[]{:S(2)}) copy-start(s32[8]{0:T(128)} %param.6) | copy-start | bytes 100
  45.4 55.8 %all-to-all-start = ((f32[2,8,8,4096]{3,1,0,2:T(8,128)}), f32[2,8,8,4096]{3,1,0,2:T(8,128)S(1)}, u32[]{:S(2)}, u32[]{:S(2)}) async-start(f32[2,8,8,4096]{3,1,0,2:T(8,128)} %copy.12), calls=%async_computation | async-start | bytes 4194304 | tf_op jit(solution)/shard_map/all_to_all | solution.py:78
  112.1 52.2 %all-to-all-start.1 = ((f32[2,64,1,4096]{3,2,0,1:T(1,128)}), f32[2,64,1,4096]{3,2,0,1:T(1,128)}, u32[]{:S(2)}, u32[]{:S(2)}) async-start(f32[2,64,1,4096]{3,2,0,1:T(1,128)} %copy.14), calls=%async_computation.1 | async-start | bytes 4194304 | tf_op jit(solution)/shard_map/all_to_all | solution.py:79
  116.5 109.3 %all-reduce.5.cloned.1.call-start = ((), (), s32[]{:S(2)}) async-start(), calls=%async_computation.4 | async-start | bytes 393216 | tf_op jit(solution)/shard_map/psum | solution.py:83
  208.5 54.7 %copy-start.3 = (f32[2,8,320,8]{2,3,1,0:T(8,128)S(1)}, f32[2,8,320,8]{2,3,1,0:T(8,128)}, u32[]{:S(2)}) copy-start(f32[2,8,320,8]{2,3,1,0:T(8,128)} %param.5) | copy-start | bytes 491524
  208.5 263.7 %all-reduce.7.cloned.1.call-start = ((), (), s32[]{:S(2)}) async-start(), calls=%async_computation.5 | async-start | bytes 393216 | tf_op jit(solution)/shard_map/psum | solution.py:83
  298.0 1.0 copy-start.2
  412.5 1.4 copy-start
  509.7 5.3 %copy-start.4 = (f32[2,8,320,8]{2,3,1,0:T(8,128)S(1)}, f32[2,8,320,8]{2,3,1,0:T(8,128)}, u32[]{:S(2)}) copy-start(f32[2,8,320,8]{2,3,1,0:T(8,128)} %all-reduce.7.cloned.1.call-done) | copy-start | bytes 491524
Sparse Core Ops, SparseCore 0:
  208.7 17.1 all-reduce.4
  455.2 16.9 all-reduce.6
where the time goes:
time: 529 us; the launch traced here: 523 us
  blocking collectives  170 us (32%)
  matrix products  160 us (30%)
  waiting for transfers between devices  120 us (23%)
  other arithmetic  21.2 us (4%)
  local copies, waits for them, and re-layouts  21.1 us (4%)
  between operations  17.5 us (3%)
  starting transfers between devices  12.7 us (2%)
    dot_general x8, matrix products, product(): jnp.einsum('frs,fvs->frv', left, right, preferred_element_type=jnp.float32)  78.5 us
    psum x2, blocking collectives, body(): alignment, curvature = lax.psum((alignment, curvature), ('freq', 'src'))  69 us
    dot_general x8, matrix products, product(): jnp.einsum('frv,frs->fvs', left, right, preferred_element_type=jnp.float32)  67.5 us
    all_to_all x1, blocking collectives, body(): lax.all_to_all(apply_taper(regrouped, window), 'freq', split_axis=1, conc...  51.5 us
    all_to_all x1, blocking collectives, body(): lax.all_to_all(gradient, 'freq', split_axis=2, concat_axis=1, tiled=True)  49.5 us
    all_to_all x1, waiting for transfers between devices, body(): lax.all_to_all(apply_taper(regrouped, window), 'freq', split_axis=1, conc...  47.4 us
    all_to_all x1, waiting for transfers between devices, body(): lax.all_to_all(gradient, 'freq', split_axis=2, concat_axis=1, tiled=True)  45.6 us
    psum x2, waiting for transfers between devices, body(): projected = lax.psum(partial_image, 'src')  27.5 us
  transfers between devices with their start and end apart: 4, of which 4 were waited for; matrix products, arithmetic and copies ran while one was open for 2% of the time, Pallas kernels for 0%

commit v1 on v0

v1 whole, which is shorter than its diff:
```python
import functools
import math

import jax
import jax.numpy as jnp
import numpy as np
from jax import lax
from jax.experimental import pallas as pl
from jax.experimental.pallas import tpu as pltpu
from jax.sharding import PartitionSpec as P

ITERS = 2
NT = 128
LANES = 128
BF16 = jnp.bfloat16
F32 = jnp.float32
VMEM_LIMIT = 56 * 2**20
CHUNKS = 2
TILE = 2048
DEPTH = 4


def in_vmem():
    return pl.BlockSpec(memory_space=pltpu.VMEM)


def stream(k_hbm, kbuf, sem, base, steps, fl, step):
    depth, _, _, ts = kbuf.shape
    total = steps * fl

    def copy(i):
        off = pl.multiple_of(base + i // fl * ts, LANES)
        slot = i % depth
        return pltpu.make_async_copy(k_hbm.at[:, i % fl, :, pl.ds(off, ts)], kbuf.at[slot], sem.at[slot])

    for i in range(min(depth - 1, total)):
        copy(i).start()

    def body(i, carry):
        @pl.when(i + depth - 1 < total)
        def _():
            copy(i + depth - 1).start()

        copy(i).wait()
        step(i // fl, i % fl, kbuf.at[i % depth])
        return carry

    lax.fori_loop(0, total, body, 0)


def adjoint_body(l_ref, k_hbm, o_ref, kbuf, sem, scr, *, fl, points, base, steps):
    _, _, receivers, ts = kbuf.shape

    def step(s, f, block):
        out = jnp.dot(l_ref[f], block[...].reshape(2 * receivers, ts), preferred_element_type=F32)
        for c in range(2):
            for j in range(ts // LANES):
                scr[j, pl.ds(c * fl + f, points, stride=2 * fl), :] = out[
                    c * points : (c + 1) * points, j * LANES : (j + 1) * LANES
                ]

        @pl.when(f == fl - 1)
        def _():
            for j in range(ts // LANES):
                o_ref[:, pl.ds(pl.multiple_of(s * ts + j * LANES, LANES), LANES)] = scr[j].astype(BF16)

    stream(k_hbm, kbuf, sem, base, steps, fl, step)


def adjoint(kernel, rows, chunk):
    _, fl, receivers, sources = kernel.shape
    points = rows.shape[1] // 2
    width = sources // CHUNKS
    ts = min(TILE, width)
    return pl.pallas_call(
        functools.partial(adjoint_body, fl=fl, points=points, base=chunk * width, steps=width // ts),
        in_specs=[in_vmem(), pl.BlockSpec(memory_space=pl.ANY)],
        out_specs=in_vmem(),
        out_shape=jax.ShapeDtypeStruct((2 * points * fl, width), BF16),
        scratch_shapes=[
            pltpu.VMEM((DEPTH, 2, receivers, ts), BF16),
            pltpu.SemaphoreType.DMA((DEPTH,)),
            pltpu.VMEM((ts // LANES, 2 * points * fl, LANES), F32),
        ],
        compiler_params=pltpu.CompilerParams(vmem_limit_bytes=VMEM_LIMIT),
        cost_estimate=pl.CostEstimate(
            flops=64 * points * receivers * width * fl, bytes_accessed=4 * fl * receivers * width, transcendentals=0
        ),
        name="adjoint",
    )(rows, kernel)


def forward_body(d_ref, k_hbm, init_ref, al_ref, o_ref, dt_ref, kbuf, sem, dscr, acc, *, fl, points, base, steps):
    _, _, receivers, ts = kbuf.shape
    acc[...] = jnp.zeros(acc.shape, F32)

    def step(s, f, block):
        @pl.when(f == 0)
        def _():
            for j in range(ts // LANES):
                dscr[j] = d_ref[:, pl.ds(pl.multiple_of(s * ts + j * LANES, LANES), LANES)].astype(F32)

        tiles = range(ts // LANES)
        real = jnp.concatenate([dscr[j, pl.ds(f, points, stride=2 * fl), :] for j in tiles], 1)
        imag = jnp.concatenate([dscr[j, pl.ds(fl + f, points, stride=2 * fl), :] for j in tiles], 1)
        at = pl.ds(pl.multiple_of(s * ts, LANES), ts)
        dt_ref[0, f, :, at] = real
        dt_ref[1, f, :, at] = imag
        field = jnp.concatenate([real, imag], 0).astype(BF16)
        acc[f] += lax.dot_general(
            field,
            block[...].reshape(2 * receivers, ts),
            (((1,), (1,)), ((), ())),
            preferred_element_type=F32,
        )

    stream(k_hbm, kbuf, sem, base, steps, fl, step)
    for f in range(fl):
        part = acc[f]
        top = 2 * points * f
        mid = top + points
        end = top + 2 * points
        real = part[:points, :receivers] - part[points:, receivers:]
        imag = part[points:, :receivers] + part[:points, receivers:]
        if init_ref is not None:
            real += init_ref[top:mid]
            imag += init_ref[mid:end]
        o_ref[top:mid] = real
        o_ref[mid:end] = imag
    rest = jnp.zeros((8, receivers - LANES), F32)
    extra = jnp.concatenate([al_ref[...], rest], 1)
    if init_ref is not None:
        extra += init_ref[2 * points * fl :]
    o_ref[2 * points * fl :] = extra


def forward(kernel, field, alignment, init, chunk):
    _, fl, receivers, sources = kernel.shape
    points = field.shape[0] // (2 * fl)
    width = sources // CHUNKS
    ts = min(TILE, width)
    body = functools.partial(forward_body, fl=fl, points=points, base=chunk * width, steps=width // ts)
    args = [field, kernel, alignment]
    if init is None:
        inner = body
        body = lambda d, k, al, *rest: inner(d, k, None, al, *rest)
    else:
        args.insert(2, init)
    specs = [in_vmem(), pl.BlockSpec(memory_space=pl.ANY)] + [in_vmem()] * (len(args) - 2)
    return pl.pallas_call(
        body,
        in_specs=specs,
        out_specs=[in_vmem()] * 2,
        out_shape=[
            jax.ShapeDtypeStruct((2 * points * fl + 8, receivers), F32),
            jax.ShapeDtypeStruct((2, fl, points, width), F32),
        ],
        scratch_shapes=[
            pltpu.VMEM((DEPTH, 2, receivers, ts), BF16),
            pltpu.SemaphoreType.DMA((DEPTH,)),
            pltpu.VMEM((ts // LANES, 2 * points * fl, LANES), F32),
            pltpu.VMEM((fl, 2 * points, 2 * receivers), F32),
        ],
        compiler_params=pltpu.CompilerParams(vmem_limit_bytes=VMEM_LIMIT),
        cost_estimate=pl.CostEstimate(
            flops=64 * points * receivers * width * fl, bytes_accessed=4 * fl * receivers * width, transcendentals=0
        ),
        name="forward",
    )(*args)


def taper_body(t_ref, g_ref, d_ref, al_ref):
    whole = t_ref[...]
    high = whole.astype(BF16)
    rest = whole - high.astype(F32)
    mid = rest.astype(BF16)
    low = (rest - mid.astype(F32)).astype(BF16)
    size, width = g_ref.shape
    step = min(512, width)
    total = jnp.zeros((8, LANES), F32)
    for at in range(0, width, step):
        g = g_ref[:, at : at + step]
        d = jnp.dot(low, g, preferred_element_type=F32)
        d += jnp.dot(mid, g, preferred_element_type=F32)
        d += jnp.dot(high, g, preferred_element_type=F32)
        d_ref[:, at : at + step] = d.astype(BF16)
        product = d * g.astype(F32)
        for j in range(0, step, LANES):
            total += product[:, j : j + LANES].reshape(size // 8, 8, LANES).sum(0)
    al_ref[...] = total


def taper(matrix, gradient):
    size, width = gradient.shape
    return pl.pallas_call(
        taper_body,
        in_specs=[in_vmem()] * 2,
        out_specs=[in_vmem()] * 2,
        out_shape=[jax.ShapeDtypeStruct((size, width), BF16), jax.ShapeDtypeStruct((8, LANES), F32)],
        compiler_params=pltpu.CompilerParams(vmem_limit_bytes=VMEM_LIMIT),
        cost_estimate=pl.CostEstimate(flops=6 * size * size * width, bytes_accessed=4 * size * width, transcendentals=0),
        name="taper",
    )(matrix, gradient)


def wave_table(freqs, fl):
    samples = np.arange(NT)[:, None]
    phase = (samples * np.arange(freqs)[None, :] % NT) * (2.0 * math.pi / NT)
    table = np.stack([np.cos(phase), -np.sin(phase)], 1) * freqs**-0.5
    table = table.reshape(NT, 2, freqs // fl, fl).transpose(0, 2, 1, 3)
    return table.reshape(NT, 2 * freqs).astype(np.float32)


def swap(x):
    return lax.ppermute(x, "src", [(0, 1), (1, 0)])


def total_over(x, axis):
    size = lax.axis_size(axis)
    if size & (size - 1):
        return lax.psum(x, axis)
    hop = 1
    while hop < size:
        x = x + lax.ppermute(x, axis, [(i, i ^ hop) for i in range(size)])
        hop *= 2
    return x


def exchange(x, rows):
    width = x.shape[-1]
    return lax.all_to_all(x.reshape(-1, rows, width), "freq", 0, 0, tiled=True).reshape(-1, width)


def body(kernel, data, win_start, win_end):
    count = lax.axis_size("freq")
    src_count = lax.axis_size("src")
    _, fl, receivers, sources = kernel.shape
    points = data.shape[3]
    own = points // count
    freqs = fl * count
    first = lax.axis_index("freq") * own
    samples = jnp.arange(NT, dtype=jnp.int32)[:, None]
    table = jnp.asarray(wave_table(freqs, fl))
    matrices = []
    for p in range(own):
        start = lax.dynamic_index_in_dim(win_start, first + p, keepdims=False)
        end = lax.dynamic_index_in_dim(win_end, first + p, keepdims=False)
        window = ((samples >= start) & (samples < end)).astype(F32)
        matrices.append(jnp.dot(table.T, window * table, precision=lax.Precision.HIGHEST))

    residual = data.transpose(1, 0, 3, 2).reshape(fl, 2 * points, receivers)
    steps, fields = [], []
    for iteration in range(ITERS):
        rounded = residual.astype(BF16)
        real, imag = rounded[:, :points], rounded[:, points:]
        rows = jnp.concatenate(
            [jnp.concatenate([real, imag], 1), jnp.concatenate([imag, -real], 1)], 2
        )
        image = None
        parts = []
        for chunk in range(CHUNKS):
            gradient = exchange(adjoint(kernel, rows, chunk), 2 * fl)
            width = gradient.shape[-1]
            if own == 1:
                direction, alignment = taper(matrices[0], gradient)
            else:
                blocks = gradient.reshape(count, own, 2 * fl, width)
                done = [taper(matrices[p], blocks[:, p].reshape(-1, width)) for p in range(own)]
                direction = jnp.stack([d.reshape(count, 2 * fl, width) for d, _ in done], 1).reshape(-1, width)
                alignment = sum(a for _, a in done)
            image, part = forward(kernel, exchange(direction, 2 * fl), alignment, image, chunk)
            parts.append(part)
        image = image + (swap(image) if src_count == 2 else lax.psum(image, "src") - image)
        projected = image[:-8].reshape(fl, 2 * points, receivers)
        sums = jnp.stack([jnp.sum(image[-8:]), jnp.sum(projected * projected)])
        sums = total_over(sums, "freq")
        step_length = sums[0] / sums[1]
        residual = residual - step_length * projected
        steps.append(step_length)
        fields.append(parts)
    estimate = jnp.concatenate(
        [sum(s * part for s, part in zip(steps, column)) for column in zip(*fields)], 3
    )
    share = receivers // src_count
    residual = lax.dynamic_slice_in_dim(residual, lax.axis_index("src") * share, share, 2)
    residual = residual.reshape(fl, 2, points, share).transpose(1, 0, 3, 2)
    return estimate, residual


def solution(mesh):
    in_specs = (P("grp", "freq", None, "src"), P("grp", "freq", None, None), P("grp"), P("grp"))
    out_specs = (P("grp", "freq", None, "src"), P("grp", "freq", "src", None))
    return jax.shard_map(body, mesh=mesh, in_specs=in_specs, out_specs=out_specs, check_vma=False)
```

time: 529 us -> 236 us (0.45)
  blocking collectives: 170 us -> 0 us
  matrix products: 160 us -> 0.95 us
  Pallas kernels: 0 us -> 89.4 us
  waiting for transfers between devices: 120 us -> 77.2 us
  starting transfers between devices: 12.7 us -> 39 us
  local copies, waits for them, and re-layouts: 21.1 us -> 5.66 us
  between operations: 17.5 us -> 3.42 us
    dot_general x24 -> x1, matrix products: 160 us -> 0.95 us  [body(): jnp.dot(table.T, window * table, precision=lax.Precision.HIGHEST)]
    all_to_all x2 -> x0, blocking collectives: 101 us -> none  [the longest x1 51.5 us: body(): lax.all_to_all(apply_taper(regrouped, window), 'freq', split_axis=1, conc...]
    pallas_call x0 -> x12, Pallas kernels: none -> 89.4 us  [the longest x4 41 us: forward(): pl.pallas_call(body, in_specs=specs, out_specs=[in_vmem()] * 2, out_shape...]
    psum x2 -> x0, blocking collectives: 69 us -> none  [body(): alignment, curvature = lax.psum((alignment, curvature), ('freq', 'src'))]
    all_to_all x2 -> x8, waiting for transfers between devices: 92.9 us -> 56 us  [exchange(): lax.all_to_all(x.reshape(-1, rows, width), 'freq', 0, 0, tiled=True)]
    psum x2 -> x0, waiting for transfers between devices: 27.5 us -> none  [body(): projected = lax.psum(partial_image, 'src')]
    all_to_all x2 -> x8, starting transfers between devices: 12 us -> 33.5 us  [exchange(): lax.all_to_all(x.reshape(-1, rows, width), 'freq', 0, 0, tiled=True)]
    ppermute x0 -> x8, waiting for transfers between devices: none -> 21.2 us  [the longest x6 17.8 us: total_over(): x = x + lax.ppermute(x, axis, [(i, i ^ hop) for i in range(size)])]
  transfers between devices with their start and end apart: 4 -> 16, of which waited for: 4 -> 16; matrix products, arithmetic and copies ran while one was open for 2% -> 1% of each run, Pallas kernels for 0% -> 21%
where the time goes in v1:
time: 236 us; the launch traced here: 234 us
  Pallas kernels  89.4 us (38%)
  waiting for transfers between devices  77.2 us (33%)
  starting transfers between devices  39 us (17%)
  other arithmetic  18.8 us (8%)
  local copies, waits for them, and re-layouts  5.66 us (2%)
  between operations  3.42 us (1%)
    all_to_all x8, waiting for transfers between devices, exchange(): lax.all_to_all(x.reshape(-1, rows, width), 'freq', 0, 0, tiled=True)  56 us
    pallas_call x4, Pallas kernels, forward(): pl.pallas_call(body, in_specs=specs, out_specs=[in_vmem()] * 2, out_shape...  41 us
    pallas_call x4, Pallas kernels, adjoint(): pl.pallas_call(functools.partial(adjoint_body, fl=fl, points=points, base...  38.6 us
    all_to_all x8, starting transfers between devices, exchange(): lax.all_to_all(x.reshape(-1, rows, width), 'freq', 0, 0, tiled=True)  33.5 us
    ppermute x6, waiting for transfers between devices, total_over(): x = x + lax.ppermute(x, axis, [(i, i ^ hop) for i in range(size)])  17.8 us
    pallas_call x4, Pallas kernels, taper(): pl.pallas_call(taper_body, in_specs=[in_vmem()] * 2, out_specs=[in_vmem()...  9.78 us
    add x6, other arithmetic, total_over(): x = x + lax.ppermute(x, axis, [(i, i ^ hop) for i in range(size)])  5.41 us
    ppermute x6, starting transfers between devices, total_over(): x = x + lax.ppermute(x, axis, [(i, i ^ hop) for i in range(size)])  5.3 us
  transfers between devices with their start and end apart: 16, of which 16 were waited for; matrix products, arithmetic and copies ran while one was open for 1% of the time, Pallas kernels for 21%

profile of v1, /device:TPU:0, one launch (start us, length us, event | category | flops | bytes accessed | tf_op | source)
XLA Modules:
  0.0 234.4 jit_solution(11686023456914849889)
XLA Ops:
  2.4 9.6 %adjoint.5 = bf16[128,2048]{1,0:T(8,128)(2,1)} custom-call(bf16[8,16,640]{2,1,0:T(8,128)(2,1)} %maximum_maximum_fusion.l_ref, bf16[2,8,320,4096]{3,2,1,0:T(8,128)(2,1)} %k_hbm.11), custom_call_target="tpu_custom_call" | custom-call | flops 2684354560 | bytes 20971520 | tf_op jit(solution)/shard_map/adjoint/pallas_call | solution.py:75
  12.0 7.3 %all-to-all-start.2 = ((bf16[8,16,2048]{2,1,0:T(8,128)(2,1)}), bf16[8,16,2048]{2,1,0:T(8,128)(2,1)S(1)}, u32[]{:S(2)}, u32[]{:S(2)}) async-start(bf16[8,16,2048]{2,1,0:T(8,128)(2,1)} %bitcast.46), calls=%async_computation.2 | async-start | bytes 1048576 | tf_op jit(solution)/shard_map/all_to_all | solution.py:231
  19.3 9.7 %adjoint.4 = bf16[128,2048]{1,0:T(8,128)(2,1)} custom-call(bf16[8,16,640]{2,1,0:T(8,128)(2,1)} %maximum_maximum_fusion.l_ref, bf16[2,8,320,4096]{3,2,1,0:T(8,128)(2,1)} %k_hbm.11), custom_call_target="tpu_custom_call" | custom-call | flops 2684354560 | bytes 20971520 | tf_op jit(solution)/shard_map/adjoint/pallas_call | solution.py:75
  29.0 4.8 %all-to-all-done.2 = bf16[8,16,2048]{2,1,0:T(8,128)(2,1)S(1)} async-done(((bf16[8,16,2048]{2,1,0:T(8,128)(2,1)}), bf16[8,16,2048]{2,1,0:T(8,128)(2,1)S(1)}, u32[]{:S(2)}, u32[]{:S(2)}) %all-to-all-start.2) | async-done | bytes 524320 | tf_op jit(solution)/shard_map/all_to_all | solution.py:231
  33.8 3.6 %all-to-all-start = ((bf16[8,16,2048]{2,1,0:T(8,128)(2,1)}), bf16[8,16,2048]{2,1,0:T(8,128)(2,1)S(1)}, u32[]{:S(2)}, u32[]{:S(2)}) async-start(bf16[8,16,2048]{2,1,0:T(8,128)(2,1)} %bitcast.40), calls=%async_computation | async-start | bytes 1048576 | tf_op jit(solution)/shard_map/all_to_all | solution.py:231
  43.3 8.8 %all-to-all-done = bf16[8,16,2048]{2,1,0:T(8,128)(2,1)S(1)} async-done(((bf16[8,16,2048]{2,1,0:T(8,128)(2,1)}), bf16[8,16,2048]{2,1,0:T(8,128)(2,1)S(1)}, u32[]{:S(2)}, u32[]{:S(2)}) %all-to-all-start) | async-done | bytes 524320 | tf_op jit(solution)/shard_map/all_to_all | solution.py:231
  52.1 3.6 %all-to-all-start.3 = ((bf16[8,16,2048]{2,1,0:T(8,128)(2,1)}), bf16[8,16,2048]{2,1,0:T(8,128)(2,1)S(1)}, u32[]{:S(2)}, u32[]{:S(2)}) async-start(bf16[8,16,2048]{2,1,0:T(8,128)(2,1)} %bitcast.57), calls=%async_computation.3 | async-start | bytes 1048576 | tf_op jit(solution)/shard_map/all_to_all | solution.py:231
  58.2 12.2 %all-to-all-done.3 = bf16[8,16,2048]{2,1,0:T(8,128)(2,1)S(1)} async-done(((bf16[8,16,2048]{2,1,0:T(8,128)(2,1)}), bf16[8,16,2048]{2,1,0:T(8,128)(2,1)S(1)}, u32[]{:S(2)}, u32[]{:S(2)}) %all-to-all-start.3) | async-done | bytes 524320 | tf_op jit(solution)/shard_map/all_to_all | solution.py:231
  70.4 3.6 %all-to-all-start.1 = ((bf16[8,16,2048]{2,1,0:T(8,128)(2,1)}), bf16[8,16,2048]{2,1,0:T(8,128)(2,1)S(1)}, u32[]{:S(2)}, u32[]{:S(2)}) async-start(bf16[8,16,2048]{2,1,0:T(8,128)(2,1)} %bitcast.54), calls=%async_computation.1 | async-start | bytes 1048576 | tf_op jit(solution)/shard_map/all_to_all | solution.py:231
  74.0 10.2 %forward.4 = (f32[136,320]{1,0:T(8,128)}, f32[2,8,8,2048]{3,2,1,0:T(8,128)}) custom-call(bf16[128,2048]{1,0:T(8,128)(2,1)} %bitcast.42, bf16[2,8,320,4096]{3,2,1,0:T(8,128)(2,1)} %k_hbm.11, f32[8,128]{1,0:T(8,128)} %get-tuple-element.20.al), custom_call_target="tpu_custom_call" | custom-call | flops 2684354560 | bytes 20971520 | tf_op jit(solution)/shard_map/forward/pallas_call | solution.py:150
  84.2 4.5 %all-to-all-done.1 = bf16[8,16,2048]{2,1,0:T(8,128)(2,1)S(1)} async-done(((bf16[8,16,2048]{2,1,0:T(8,128)(2,1)}), bf16[8,16,2048]{2,1,0:T(8,128)(2,1)S(1)}, u32[]{:S(2)}, u32[]{:S(2)}) %all-to-all-start.1) | async-done | bytes 524320 | tf_op jit(solution)/shard_map/all_to_all | solution.py:231
  89.5 10.3 %forward.5 = (f32[136,320]{1,0:T(8,128)}, f32[2,8,8,2048]{3,2,1,0:T(8,128)}) custom-call(bf16[128,2048]{1,0:T(8,128)(2,1)} %bitcast.43, bf16[2,8,320,4096]{3,2,1,0:T(8,128)(2,1)} %k_hbm.11, f32[136,320]{1,0:T(8,128)} %get-tuple-element.21.init_ref, f32[8,128]{1,0:T(8,128)} %get-tuple-element.22.al_ref), custom_call_target="tpu_custom_call" | custom-call | flops 2684354560 | bytes 20971520 | tf_op jit(solution)/shard_map/forward/pallas_call | solution.py:150
  114.9 4.3 %collective-permute-done.3 = f32[2]{0:T(128)S(1)} collective-permute-done((f32[2]{0:T(128)S(1)}, f32[2]{0:T(128)S(1)}, u32[]{:S(2)}, u32[]{:S(2)}) %collective-permute-start.3) | collective-permute-done | bytes 40 | tf_op jit(solution)/shard_map/ppermute | solution.py:224
  121.9 9.6 %adjoint.7 = bf16[128,2048]{1,0:T(8,128)(2,1)} custom-call(bf16[8,16,640]{2,1,0:T(8,128)(2,1)} %maximum_maximum_fusion.1.l_ref, bf16[2,8,320,4096]{3,2,1,0:T(8,128)(2,1)} %k_hbm.11), custom_call_target="tpu_custom_call" | custom-call | flops 2684354560 | bytes 20971520 | tf_op jit(solution)/shard_map/adjoint/pallas_call | solution.py:75
  131.6 3.6 %all-to-all-start.6 = ((bf16[8,16,2048]{2,1,0:T(8,128)(2,1)}), bf16[8,16,2048]{2,1,0:T(8,128)(2,1)S(1)}, u32[]{:S(2)}, u32[]{:S(2)}) async-start(bf16[8,16,2048]{2,1,0:T(8,128)(2,1)} %bitcast.47), calls=%async_computation.6 | async-start | bytes 1048576 | tf_op jit(solution)/shard_map/all_to_all | solution.py:231
  135.2 9.7 %adjoint.6 = bf16[128,2048]{1,0:T(8,128)(2,1)} custom-call(bf16[8,16,640]{2,1,0:T(8,128)(2,1)} %maximum_maximum_fusion.1.l_ref, bf16[2,8,320,4096]{3,2,1,0:T(8,128)(2,1)} %k_hbm.11), custom_call_target="tpu_custom_call" | custom-call | flops 2684354560 | bytes 20971520 | tf_op jit(solution)/shard_map/adjoint/pallas_call | solution.py:75
  146.6 4.3 %all-to-all-start.4 = ((bf16[8,16,2048]{2,1,0:T(8,128)(2,1)}), bf16[8,16,2048]{2,1,0:T(8,128)(2,1)S(1)}, u32[]{:S(2)}, u32[]{:S(2)}) async-start(bf16[8,16,2048]{2,1,0:T(8,128)(2,1)} %bitcast.45), calls=%async_computation.4 | async-start | bytes 1048576 | tf_op jit(solution)/shard_map/all_to_all | solution.py:231
  153.4 9.7 %all-to-all-done.4 = bf16[8,16,2048]{2,1,0:T(8,128)(2,1)S(1)} async-done(((bf16[8,16,2048]{2,1,0:T(8,128)(2,1)}), bf16[8,16,2048]{2,1,0:T(8,128)(2,1)S(1)}, u32[]{:S(2)}, u32[]{:S(2)}) %all-to-all-start.4) | async-done | bytes 524320 | tf_op jit(solution)/shard_map/all_to_all | solution.py:231
  163.0 3.7 %all-to-all-start.7 = ((bf16[8,16,2048]{2,1,0:T(8,128)(2,1)}), bf16[8,16,2048]{2,1,0:T(8,128)(2,1)S(1)}, u32[]{:S(2)}, u32[]{:S(2)}) async-start(bf16[8,16,2048]{2,1,0:T(8,128)(2,1)} %bitcast.56), calls=%async_computation.7 | async-start | bytes 1048576 | tf_op jit(solution)/shard_map/all_to_all | solution.py:231
  169.2 10.8 %all-to-all-done.7 = bf16[8,16,2048]{2,1,0:T(8,128)(2,1)S(1)} async-done(((bf16[8,16,2048]{2,1,0:T(8,128)(2,1)}), bf16[8,16,2048]{2,1,0:T(8,128)(2,1)S(1)}, u32[]{:S(2)}, u32[]{:S(2)}) %all-to-all-start.7) | async-done | bytes 524320 | tf_op jit(solution)/shard_map/all_to_all | solution.py:231
  180.0 3.7 %all-to-all-start.5 = ((bf16[8,16,2048]{2,1,0:T(8,128)(2,1)}), bf16[8,16,2048]{2,1,0:T(8,128)(2,1)S(1)}, u32[]{:S(2)}, u32[]{:S(2)}) async-start(bf16[8,16,2048]{2,1,0:T(8,128)(2,1)} %bitcast.53), calls=%async_computation.5 | async-start | bytes 1048576 | tf_op jit(solution)/shard_map/all_to_all | solution.py:231
  183.7 10.2 %forward.6 = (f32[136,320]{1,0:T(8,128)}, f32[2,8,8,2048]{3,2,1,0:T(8,128)}) custom-call(bf16[128,2048]{1,0:T(8,128)(2,1)} %bitcast.41, bf16[2,8,320,4096]{3,2,1,0:T(8,128)(2,1)} %k_hbm.11, f32[8,128]{1,0:T(8,128)} %get-tuple-element.27.al), custom_call_target="tpu_custom_call" | custom-call | flops 2684354560 | bytes 20971520 | tf_op jit(solution)/shard_map/forward/pallas_call | solution.py:150
  198.2 10.4 %forward.7 = (f32[136,320]{1,0:T(8,128)}, f32[2,8,8,2048]{3,2,1,0:T(8,128)}) custom-call(bf16[128,2048]{1,0:T(8,128)(2,1)} %bitcast.44, bf16[2,8,320,4096]{3,2,1,0:T(8,128)(2,1)} %k_hbm.11, f32[136,320]{1,0:T(8,128)} %get-tuple-element.28.init_ref, f32[8,128]{1,0:T(8,128)} %get-tuple-element.29.al_ref), custom_call_target="tpu_custom_call" | custom-call | flops 2684354560 | bytes 20971520 | tf_op jit(solution)/shard_map/forward/pallas_call | solution.py:150
  225.0 3.7 %collective-permute-done.7 = f32[2]{0:T(128)S(1)} collective-permute-done((f32[2]{0:T(128)S(1)}, f32[2]{0:T(128)S(1)}, u32[]{:S(2)}, u32[]{:S(2)}) %collective-permute-start.7) | collective-permute-done | bytes 40 | tf_op jit(solution)/shard_map/ppermute | solution.py:224
  (82 shorter events, 59.1 us)
Async XLA Ops:
  12.0 21.8 %all-to-all-start.2 = ((bf16[8,16,2048]{2,1,0:T(8,128)(2,1)}), bf16[8,16,2048]{2,1,0:T(8,128)(2,1)S(1)}, u32[]{:S(2)}, u32[]{:S(2)}) async-start(bf16[8,16,2048]{2,1,0:T(8,128)(2,1)} %bitcast.46), calls=%async_computation.2 | async-start | bytes 1048576 | tf_op jit(solution)/shard_map/all_to_all | solution.py:231
  19.3 18.1 %copy-start.13 = (s32[8]{0:T(128)S(1)}, s32[8]{0:T(128)}, u32[]{:S(2)}) copy-start(s32[8]{0:T(128)} %param.7) | copy-start | bytes 100
  19.3 18.7 %copy-start.14 = (s32[8]{0:T(128)S(1)}, s32[8]{0:T(128)}, u32[]{:S(2)}) copy-start(s32[8]{0:T(128)} %param.8) | copy-start | bytes 100
  19.3 20.6 %copy-start.12 = (f32[128,128]{1,0:T(8,128)S(1)}, f32[128,128]{1,0:T(8,128)}, u32[]{:S(2)}) copy-start(f32[128,128]{1,0:T(8,128)} %constant.25.clone) | copy-start | bytes 196612
  33.8 7.1 %copy-start.9 = (bf16[8,16,2048]{2,1,0:T(8,128)(2,1)}, bf16[8,16,2048]{2,1,0:T(8,128)(2,1)S(1)}, u32[]{:S(2)}) copy-start(bf16[8,16,2048]{2,1,0:T(8,128)(2,1)S(1)} %all-to-all-done.2) | copy-start | bytes 1572868
  33.8 18.3 %all-to-all-start = ((bf16[8,16,2048]{2,1,0:T(8,128)(2,1)}), bf16[8,16,2048]{2,1,0:T(8,128)(2,1)S(1)}, u32[]{:S(2)}, u32[]{:S(2)}) async-start(bf16[8,16,2048]{2,1,0:T(8,128)(2,1)} %bitcast.40), calls=%async_computation | async-start | bytes 1048576 | tf_op jit(solution)/shard_map/all_to_all | solution.py:231
  52.1 18.3 %all-to-all-start.3 = ((bf16[8,16,2048]{2,1,0:T(8,128)(2,1)}), bf16[8,16,2048]{2,1,0:T(8,128)(2,1)S(1)}, u32[]{:S(2)}, u32[]{:S(2)}) async-start(bf16[8,16,2048]{2,1,0:T(8,128)(2,1)} %bitcast.57), calls=%async_computation.3 | async-start | bytes 1048576 | tf_op jit(solution)/shard_map/all_to_all | solution.py:231
  70.4 18.3 %all-to-all-start.1 = ((bf16[8,16,2048]{2,1,0:T(8,128)(2,1)}), bf16[8,16,2048]{2,1,0:T(8,128)(2,1)S(1)}, u32[]{:S(2)}, u32[]{:S(2)}) async-start(bf16[8,16,2048]{2,1,0:T(8,128)(2,1)} %bitcast.54), calls=%async_computation.1 | async-start | bytes 1048576 | tf_op jit(solution)/shard_map/all_to_all | solution.py:231
  99.8 1.7 collective-permute-start
  105.0 3.5 %collective-permute-start.1 = (f32[2]{0:T(128)S(1)}, f32[2]{0:T(128)S(1)}, u32[]{:S(2)}, u32[]{:S(2)}) collective-permute-start(f32[2]{0:T(128)S(1)} %pad_maximum_fusion.1), channel_id=1, source_target_pairs={{0,2},{2,0},{4,6},{6,4},{8,10},{10,8},{12,14},{14,12},{1,3},{3,1},... | collective-permute-start | bytes 32 | tf_op jit(solution)/shard_map/ppermute | solution.py:224
  109.9 3.5 %collective-permute-start.2 = (f32[2]{0:T(128)S(1)}, f32[2]{0:T(128)S(1)}, u32[]{:S(2)}, u32[]{:S(2)}) collective-permute-start(f32[2]{0:T(128)S(1)} %fusion.11), channel_id=1, source_target_pairs={{0,4},{2,6},{4,0},{6,2},{8,12},{10,14},{12,8},{14,10},{1,5},{3,7},... | collective-permute-start | bytes 32 | tf_op jit(solution)/shard_map/ppermute | solution.py:224
  114.7 4.4 %collective-permute-start.3 = (f32[2]{0:T(128)S(1)}, f32[2]{0:T(128)S(1)}, u32[]{:S(2)}, u32[]{:S(2)}) collective-permute-start(f32[2]{0:T(128)S(1)} %fusion.14), channel_id=1, source_target_pairs={{0,8},{2,10},{4,12},{6,14},{8,0},{10,2},{12,4},{14,6},{1,9},{3,11}... | collective-permute-start | bytes 32 | tf_op jit(solution)/shard_map/ppermute | solution.py:224
  131.6 15.0 %all-to-all-start.6 = ((bf16[8,16,2048]{2,1,0:T(8,128)(2,1)}), bf16[8,16,2048]{2,1,0:T(8,128)(2,1)S(1)}, u32[]{:S(2)}, u32[]{:S(2)}) async-start(bf16[8,16,2048]{2,1,0:T(8,128)(2,1)} %bitcast.47), calls=%async_computation.6 | async-start | bytes 1048576 | tf_op jit(solution)/shard_map/all_to_all | solution.py:231
  146.6 4.3 %copy-start.11 = (bf16[8,16,2048]{2,1,0:T(8,128)(2,1)}, bf16[8,16,2048]{2,1,0:T(8,128)(2,1)S(1)}, u32[]{:S(2)}) copy-start(bf16[8,16,2048]{2,1,0:T(8,128)(2,1)S(1)} %all-to-all-done.6) | copy-start | bytes 1572868
  146.6 16.4 %all-to-all-start.4 = ((bf16[8,16,2048]{2,1,0:T(8,128)(2,1)}), bf16[8,16,2048]{2,1,0:T(8,128)(2,1)S(1)}, u32[]{:S(2)}, u32[]{:S(2)}) async-start(bf16[8,16,2048]{2,1,0:T(8,128)(2,1)} %bitcast.45), calls=%async_computation.4 | async-start | bytes 1048576 | tf_op jit(solution)/shard_map/all_to_all | solution.py:231
  163.0 16.9 %all-to-all-start.7 = ((bf16[8,16,2048]{2,1,0:T(8,128)(2,1)}), bf16[8,16,2048]{2,1,0:T(8,128)(2,1)S(1)}, u32[]{:S(2)}, u32[]{:S(2)}) async-start(bf16[8,16,2048]{2,1,0:T(8,128)(2,1)} %bitcast.56), calls=%async_computation.7 | async-start | bytes 1048576 | tf_op jit(solution)/shard_map/all_to_all | solution.py:231
  180.0 17.5 %all-to-all-start.5 = ((bf16[8,16,2048]{2,1,0:T(8,128)(2,1)}), bf16[8,16,2048]{2,1,0:T(8,128)(2,1)S(1)}, u32[]{:S(2)}, u32[]{:S(2)}) async-start(bf16[8,16,2048]{2,1,0:T(8,128)(2,1)} %bitcast.53), calls=%async_computation.5 | async-start | bytes 1048576 | tf_op jit(solution)/shard_map/all_to_all | solution.py:231
  198.2 33.1 %copy-start.6 = (f32[2,8,8,2048]{3,2,1,0:T(8,128)S(1)}, f32[2,8,8,2048]{3,2,1,0:T(8,128)}, u32[]{:S(2)}) copy-start(f32[2,8,8,2048]{3,2,1,0:T(8,128)} %get-tuple-element.32) | copy-start | bytes 3145732
  198.2 33.2 %copy-start.7 = (f32[2,8,8,2048]{3,2,1,0:T(8,128)S(1)}, f32[2,8,8,2048]{3,2,1,0:T(8,128)}, u32[]{:S(2)}) copy-start(f32[2,8,8,2048]{3,2,1,0:T(8,128)} %get-tuple-element.31) | copy-start | bytes 3145732
  208.7 22.7 %copy-start.5 = (f32[2,8,8,2048]{3,2,1,0:T(8,128)S(1)}, f32[2,8,8,2048]{3,2,1,0:T(8,128)}, u32[]{:S(2)}) copy-start(f32[2,8,8,2048]{3,2,1,0:T(8,128)} %get-tuple-element.24) | copy-start | bytes 3145732
  208.7 1.9 collective-permute-start.4
  214.3 3.5 %collective-permute-start.5 = (f32[2]{0:T(128)S(1)}, f32[2]{0:T(128)S(1)}, u32[]{:S(2)}, u32[]{:S(2)}) collective-permute-start(f32[2]{0:T(128)S(1)} %pad_maximum_fusion.2), channel_id=1, source_target_pairs={{0,2},{2,0},{4,6},{6,4},{8,10},{10,8},{12,14},{14,12},{1,3},{3,1},... | collective-permute-start | bytes 32 | tf_op jit(solution)/shard_map/ppermute | solution.py:224
  219.3 3.5 %collective-permute-start.6 = (f32[2]{0:T(128)S(1)}, f32[2]{0:T(128)S(1)}, u32[]{:S(2)}, u32[]{:S(2)}) collective-permute-start(f32[2]{0:T(128)S(1)} %fusion.10), channel_id=1, source_target_pairs={{0,4},{2,6},{4,0},{6,2},{8,12},{10,14},{12,8},{14,10},{1,5},{3,7},... | collective-permute-start | bytes 32 | tf_op jit(solution)/shard_map/ppermute | solution.py:224
  224.2 4.4 %collective-permute-start.7 = (f32[2]{0:T(128)S(1)}, f32[2]{0:T(128)S(1)}, u32[]{:S(2)}, u32[]{:S(2)}) collective-permute-start(f32[2]{0:T(128)S(1)} %fusion.12), channel_id=1, source_target_pairs={{0,8},{2,10},{4,12},{6,14},{8,0},{10,2},{12,4},{14,6},{1,9},{3,11}... | collective-permute-start | bytes 32 | tf_op jit(solution)/shard_map/ppermute | solution.py:224
  (7 other events, 17.2 us)

commit v2 on v1

v2 whole, which is shorter than its diff:
```python
import functools
import math

import jax
import jax.numpy as jnp
import numpy as np
from jax import lax
from jax.experimental import pallas as pl
from jax.experimental.pallas import tpu as pltpu
from jax.sharding import PartitionSpec as P

ITERS = 2
NT = 128
LANES = 128
BF16 = jnp.bfloat16
F32 = jnp.float32
VMEM_LIMIT = 56 * 2**20
PARTS = ((1, "relay"), (1, "relay"))
ADJOINT_TILE = 2048
ADJOINT_DEPTH = 9
FORWARD_TILE = 2048
FORWARD_DEPTH = 9
FORWARD_GROUP = 1
EARLY = False
TIE = 1
TIE2 = True


def in_vmem():
    return pl.BlockSpec(memory_space=pltpu.VMEM)


def tile_of(width, limit):
    return max(t for t in range(LANES, min(limit, width) + 1, LANES) if width % t == 0)


def stream(k_hbm, kbuf, sem, base, steps, step):
    depth, _, group, _, ts = kbuf.shape
    groups = k_hbm.shape[1] // group
    total = steps * groups

    def copy(i):
        off = pl.multiple_of(base + i // groups * ts, LANES)
        slot = i % depth
        source = k_hbm.at[:, pl.ds(i % groups * group, group), :, pl.ds(off, ts)]
        return pltpu.make_async_copy(source, kbuf.at[slot], sem.at[slot])

    for i in range(min(depth - 1, total)):
        copy(i).start()

    def body(i, carry):
        @pl.when(i + depth - 1 < total)
        def _():
            copy(i + depth - 1).start()

        copy(i).wait()
        step(i // groups, i % groups, kbuf.at[i % depth])
        return carry

    lax.fori_loop(0, total, body, 0)


def adjoint_body(turn_ref, l_ref, k_hbm, *refs, points, base, steps):
    *o_refs, kbuf, sem, scr = refs
    _, _, _, receivers, ts = kbuf.shape
    fl = k_hbm.shape[1]
    size = 2 * points * fl // len(o_refs)
    turn = turn_ref[0]

    def step(s, f, block):
        out = jnp.dot(l_ref[f], block[...].reshape(2 * receivers, ts), preferred_element_type=F32)
        for c in range(2):
            for j in range(ts // LANES):
                scr[j, pl.ds(c * fl + f, points, stride=2 * fl), :] = out[
                    c * points : (c + 1) * points, j * LANES : (j + 1) * LANES
                ]

        @pl.when(f == fl - 1)
        def _():
            for k, o_ref in enumerate(o_refs):
                rows = pl.ds(pl.multiple_of((turn ^ k) * size, size), size)
                for j in range(ts // LANES):
                    at = pl.ds(pl.multiple_of(s * ts + j * LANES, LANES), LANES)
                    o_ref[:, at] = scr[j, rows, :].astype(BF16)

    stream(k_hbm, kbuf, sem, base, steps, step)


def adjoint(turn, kernel, rows, base, width, pieces):
    _, fl, receivers, sources = kernel.shape
    points = rows.shape[1] // 2
    ts = tile_of(width, ADJOINT_TILE)
    depth = min(ADJOINT_DEPTH, width // ts * fl)
    return pl.pallas_call(
        functools.partial(adjoint_body, points=points, base=base, steps=width // ts),
        in_specs=[pl.BlockSpec(memory_space=pltpu.SMEM), in_vmem(), pl.BlockSpec(memory_space=pl.ANY)],
        out_specs=[in_vmem()] * pieces,
        out_shape=[jax.ShapeDtypeStruct((2 * points * fl // pieces, width), BF16)] * pieces,
        scratch_shapes=[
            pltpu.VMEM((depth, 2, 1, receivers, ts), BF16),
            pltpu.SemaphoreType.DMA((depth,)),
            pltpu.VMEM((ts // LANES, 2 * points * fl, LANES), F32),
        ],
        compiler_params=pltpu.CompilerParams(vmem_limit_bytes=VMEM_LIMIT),
        cost_estimate=pl.CostEstimate(
            flops=64 * points * receivers * width * fl, bytes_accessed=4 * fl * receivers * width, transcendentals=0
        ),
        name="adjoint",
    )(turn, rows, kernel)


def forward_body(turn_ref, k_hbm, al_ref, init_ref, *refs, pieces, points, base, steps):
    d_refs, (o_ref, kbuf, sem, dscr, acc) = refs[:pieces], refs[pieces:]
    _, _, group, receivers, ts = kbuf.shape
    fl = k_hbm.shape[1]
    size = 2 * points * fl // pieces
    turn = turn_ref[0]
    acc[...] = jnp.zeros(acc.shape, F32)

    def step(s, n, block):
        tiles = range(ts // LANES)

        @pl.when(n == 0)
        def _():
            for k, d_ref in enumerate(d_refs):
                rows = pl.ds(pl.multiple_of((turn ^ k) * size, size), size)
                for j in tiles:
                    at = pl.ds(pl.multiple_of(s * ts + j * LANES, LANES), LANES)
                    dscr[j, rows, :] = d_ref[:, at].astype(F32)

        def part(c, f):
            rows = pl.ds(c * fl + n * group + f, points, stride=2 * fl)
            return jnp.concatenate([dscr[j, rows, :] for j in tiles], 1)

        field = jnp.concatenate([part(c, f) for f in range(group) for c in range(2)], 0).astype(BF16)
        acc[n] += lax.dot_general(
            field,
            block[...].reshape(2 * group * receivers, ts),
            (((1,), (1,)), ((), ())),
            preferred_element_type=F32,
        )

    stream(k_hbm, kbuf, sem, base, steps, step)
    for f in range(fl):
        n, g = divmod(f, group)
        whole = acc[n, 2 * points * g : 2 * points * (g + 1)]
        by_real = whole[:, g * receivers : (g + 1) * receivers]
        by_imag = whole[:, (group + g) * receivers : (group + g + 1) * receivers]
        top = 2 * points * f
        mid = top + points
        end = top + 2 * points
        real = by_real[:points] - by_imag[points:]
        imag = by_real[points:] + by_imag[:points]
        if init_ref is not None:
            real += init_ref[top:mid]
            imag += init_ref[mid:end]
        o_ref[top:mid] = real
        o_ref[mid:end] = imag
    extra = jnp.concatenate([al_ref[...], jnp.zeros((8, receivers - LANES), F32)], 1)
    if init_ref is not None:
        extra += init_ref[2 * points * fl :]
    o_ref[2 * points * fl :] = extra


def forward(turn, kernel, field, alignment, init, base):
    _, fl, receivers, sources = kernel.shape
    pieces = len(field)
    points = field[0].shape[0] * pieces // (2 * fl)
    width = field[0].shape[1]
    ts = tile_of(width, FORWARD_TILE)
    group = FORWARD_GROUP if fl % FORWARD_GROUP == 0 else 1
    depth = min(FORWARD_DEPTH, width // ts * fl // group)
    body = functools.partial(forward_body, pieces=pieces, points=points, base=base, steps=width // ts)
    if init is None:
        inner, start = body, []
        body = lambda turn, k, al, *rest: inner(turn, k, al, None, *rest)
    else:
        start = [init]
    specs = [pl.BlockSpec(memory_space=pltpu.SMEM), pl.BlockSpec(memory_space=pl.ANY), in_vmem()]
    return pl.pallas_call(
        body,
        in_specs=specs + [in_vmem()] * (len(start) + pieces),
        out_specs=in_vmem(),
        out_shape=jax.ShapeDtypeStruct((2 * points * fl + 8, receivers), F32),
        scratch_shapes=[
            pltpu.VMEM((depth, 2, group, receivers, ts), BF16),
            pltpu.SemaphoreType.DMA((depth,)),
            pltpu.VMEM((ts // LANES, 2 * points * fl, LANES), F32),
            pltpu.VMEM((fl // group, 2 * points * group, 2 * receivers * group), F32),
        ],
        compiler_params=pltpu.CompilerParams(vmem_limit_bytes=VMEM_LIMIT),
        cost_estimate=pl.CostEstimate(
            flops=64 * points * receivers * width * fl, bytes_accessed=4 * fl * receivers * width, transcendentals=0
        ),
        name="forward",
    )(turn, kernel, alignment, *start, *field)


def split(whole):
    high = whole.astype(BF16)
    return high, (whole - high.astype(F32)).astype(BF16)


def taper_body(t_ref, *refs, inputs, points, rows):
    g_refs, d_refs, al_ref = refs[:inputs], refs[inputs:-1], refs[-1]
    width = g_refs[0].shape[1]
    step = min(512, width)
    own = len(d_refs) * rows
    total = jnp.zeros((8, LANES), F32)
    for p in range(points):
        high, low = split(t_ref[p])
        places = [
            (ref, slice(at, at + rows)) for ref in g_refs for at in range(p * rows, ref.shape[0], points * rows)
        ]
        for at in range(0, width, step):
            cols = slice(at, at + step)
            g = jnp.concatenate([ref[place, cols] for ref, place in places], 0)
            d = jnp.dot(low, g, preferred_element_type=F32)
            d += jnp.dot(high, g, preferred_element_type=F32)
            for k, ref in enumerate(d_refs):
                ref[p * rows : (p + 1) * rows, cols] = d[k * rows : (k + 1) * rows].astype(BF16)
            product = d * g[:own].astype(F32)
            for j in range(0, step, LANES):
                total += product[:, j : j + LANES].reshape(own // 8, 8, LANES).sum(0)
    al_ref[...] = total


def taper(matrices, blocks, outputs, rows):
    points = matrices.shape[0]
    width = blocks[0].shape[1]
    return pl.pallas_call(
        functools.partial(taper_body, inputs=len(blocks), points=points, rows=rows),
        in_specs=[in_vmem()] * (1 + len(blocks)),
        out_specs=[in_vmem()] * (outputs + 1),
        out_shape=[jax.ShapeDtypeStruct((points * rows, width), BF16)] * outputs
        + [jax.ShapeDtypeStruct((8, LANES), F32)],
        compiler_params=pltpu.CompilerParams(vmem_limit_bytes=VMEM_LIMIT),
        cost_estimate=pl.CostEstimate(
            flops=6 * matrices.size * width, bytes_accessed=8 * points * rows * outputs * width, transcendentals=0
        ),
        name="taper",
    )(matrices, *blocks)


def merge_body(own_ref, got_ref, p_ref, sums_ref):
    size, receivers = p_ref.shape
    projected = own_ref[:size] + got_ref[:size]
    p_ref[...] = projected
    squares = jnp.sum((projected * projected).reshape(size // 8, 8, receivers), 0)
    pad = -receivers % LANES
    if pad:
        squares = jnp.concatenate([squares, jnp.zeros((8, pad), F32)], 1)
    curvature = sum(squares[:, j : j + LANES] for j in range(0, receivers + pad, LANES))
    alignment = own_ref[size:, :LANES] + got_ref[size:, :LANES]
    for at in range(0, sums_ref.shape[0], 16):
        sums_ref[at : at + 8] = alignment
        sums_ref[at + 8 : at + 16] = curvature


def merge(own, got, count):
    size, receivers = own.shape
    return pl.pallas_call(
        merge_body,
        in_specs=[in_vmem()] * 2,
        out_specs=[in_vmem()] * 2,
        out_shape=[jax.ShapeDtypeStruct((size - 8, receivers), F32), jax.ShapeDtypeStruct((16 * count, LANES), F32)],
        name="merge",
    )(own, got)


def step_body(p_ref, r_ref, s_ref, a_ref, new_ref, l_ref, *, fl, points):
    receivers = p_ref.shape[1]
    sums = sum(s_ref[at : at + 16] for at in range(0, s_ref.shape[0], 16))
    length = jnp.sum(sums[0:8], keepdims=True) / jnp.sum(sums[8:16], keepdims=True)
    a_ref[...] = jnp.broadcast_to(length, a_ref.shape)
    new = r_ref[...] - length * p_ref[...]
    new_ref[...] = new
    for f in range(fl):
        block = new[2 * points * f : 2 * points * (f + 1)]
        real, imag = block[:points], block[points:]
        l_ref[f, :, :receivers] = block.astype(BF16)
        l_ref[f, :, receivers:] = jnp.concatenate([imag, -real], 0).astype(BF16)


def advance(projected, residual, sums, fl, points):
    receivers = projected.shape[1]
    return pl.pallas_call(
        functools.partial(step_body, fl=fl, points=points),
        in_specs=[in_vmem()] * 3,
        out_specs=[in_vmem()] * 3,
        out_shape=[
            jax.ShapeDtypeStruct((8, LANES), F32),
            jax.ShapeDtypeStruct(projected.shape, F32),
            jax.ShapeDtypeStruct((fl, 2 * points, 2 * receivers), BF16),
        ],
        name="step",
    )(projected, residual, sums)


def wave_table(freqs, fl):
    samples = np.arange(NT)[:, None]
    phase = (samples * np.arange(freqs)[None, :] % NT) * (2.0 * math.pi / NT)
    table = np.stack([np.cos(phase), -np.sin(phase)], 1) * freqs**-0.5
    table = table.reshape(NT, 2, freqs // fl, fl).transpose(0, 2, 1, 3)
    return table.reshape(NT, 2 * freqs).astype(np.float32)


def swap(x):
    return lax.ppermute(x, "src", [(0, 1), (1, 0)])


def estimate_body(*refs, spans, pieces, fl, points):
    turn_ref, lengths = refs[0], refs[1 : 1 + ITERS]
    fields, (e_ref, scr) = refs[1 + ITERS : -2], refs[-2:]
    lengths = [ref[0:1, 0:1] for ref in lengths]
    at = 0
    for part, ((base, width), count) in enumerate(zip(spans, pieces)):
        size = 2 * points * fl // count
        turn = turn_ref[part]

        def one(i, carry, at=at, base=base, count=count, size=size, turn=turn):
            off = pl.multiple_of(i * LANES, LANES)
            for k in range(count):
                value = sum(
                    lengths[n] * fields[at + n * count + k][:, pl.ds(off, LANES)].astype(F32) for n in range(ITERS)
                )
                scr[i % 2, pl.ds(pl.multiple_of((turn ^ k) * size, size), size), :] = value
            for c in range(2):
                for f in range(fl):
                    out = pl.ds(pl.multiple_of(base + i * LANES, LANES), LANES)
                    e_ref[c, f, :, out] = scr[i % 2, pl.ds(c * fl + f, points, stride=2 * fl), :]
            return carry

        lax.fori_loop(0, width // LANES, one, 0, unroll=2)
        at += ITERS * count


def estimate_of(turns, lengths, fields, spans, fl, points):
    parts = range(len(spans))
    flat = [x for part in parts for field in fields for x in field[part]]
    sources = sum(width for _, width in spans)
    return pl.pallas_call(
        functools.partial(
            estimate_body, spans=spans, pieces=[len(fields[0][part]) for part in parts], fl=fl, points=points
        ),
        in_specs=[pl.BlockSpec(memory_space=pltpu.SMEM)] + [in_vmem()] * (len(lengths) + len(flat)),
        out_specs=in_vmem(),
        out_shape=jax.ShapeDtypeStruct((2, fl, points, sources), F32),
        scratch_shapes=[pltpu.VMEM((2, 2 * points * fl, LANES), F32)],
        compiler_params=pltpu.CompilerParams(vmem_limit_bytes=VMEM_LIMIT),
        name="estimate",
    )(turns, *lengths, *flat)


def then(x, *earlier):
    return lax.optimization_barrier((x, *earlier))[0]


def send(x, hop):
    return lax.ppermute(x, "freq", [(i, i ^ hop) for i in range(lax.axis_size("freq"))])


def exchange(x, rows):
    width = x.shape[-1]
    return lax.all_to_all(x.reshape(-1, rows, width), "freq", 0, 0, tiled=True).reshape(-1, width)


def body(kernel, data, win_start, win_end):
    count = lax.axis_size("freq")
    src_count = lax.axis_size("src")
    _, fl, receivers, sources = kernel.shape
    points = data.shape[3]
    rows = 2 * fl
    me = lax.axis_index("freq")
    own = points // count
    permutes = count & (count - 1) == 0 and rows % 16 == 0 and own == 1
    inner = {"plain": 1, "direct": 1, "relay": 2}
    parts, base = [], 0
    for weight, mode in PARTS:
        width = sources * weight // sum(w for w, _ in PARTS)
        parts.append((base, width, mode if permutes else "plain"))
        base += width

    def turn_of(mode):
        turn = (me // inner[mode]).reshape(1).astype(jnp.int32)
        return jnp.zeros_like(turn) if mode == "plain" else turn

    def pieces_of(mode):
        return 1 if mode == "plain" else count // inner[mode]

    table = jnp.asarray(wave_table(fl * count, fl))
    samples = jnp.arange(NT, dtype=jnp.int32)[None, :]

    def matrices_of(mode):
        size = own * inner[mode]
        first = me // inner[mode] * size
        starts = lax.dynamic_slice_in_dim(win_start, first, size)[:, None]
        ends = lax.dynamic_slice_in_dim(win_end, first, size)[:, None]
        window = ((samples >= starts) & (samples < ends)).astype(F32)
        right = table
        if mode != "plain":
            blocks = table.reshape(NT, count, rows)
            order = [me ^ (k * inner[mode] + y) for y in range(inner[mode]) for k in range(pieces_of(mode))]
            right = jnp.concatenate([lax.dynamic_index_in_dim(blocks, b, 1, keepdims=False) for b in order], 1)
        left = right[:, : right.shape[1] // inner[mode]]
        return jnp.einsum("pta,tb->pab", window[:, :, None] * left, right, precision=lax.Precision.HIGHEST)

    matrices = {mode: matrices_of(mode) for mode in sorted({mode for _, _, mode in parts})}

    def scatter(blocks, mode):
        if mode == "plain":
            return [exchange(blocks[0], rows)]
        return [blocks[0]] + [send(blocks[k], k * inner[mode]) for k in range(1, len(blocks))]

    def pair_up(got, mode):
        if mode != "relay":
            return got
        if EARLY:
            rest = jnp.concatenate(got[1:], 0)
            return [got[0], rest, send(got[0], 1), send(rest, 1)]
        joined = jnp.concatenate(got, 0)
        return [joined, send(joined, 1)]

    def tapered(got, mode):
        if mode != "plain":
            *field, alignment = taper(matrices[mode], got, pieces_of(mode), rows)
            return field, alignment
        if own == 1:
            field, alignment = taper(matrices[mode], got, 1, count * rows)
            return [field], alignment
        width = got[0].shape[-1]
        got = got[0].reshape(count, own, rows, width)
        done = [
            taper(matrices[mode][p : p + 1], [got[:, p].reshape(-1, width)], 1, count * rows) for p in range(own)
        ]
        field = jnp.stack([d.reshape(count, rows, width) for d, _ in done], 1).reshape(-1, width)
        return [field], sum(a for _, a in done)

    residual = data.transpose(1, 0, 3, 2).reshape(2 * fl * points, receivers)
    real, imag = jnp.split(residual.reshape(fl, 2 * points, receivers).astype(BF16), 2, 1)
    lhs = jnp.concatenate([jnp.concatenate([real, imag], 1), jnp.concatenate([imag, -real], 1)], 2)
    lengths, fields = [], []
    for iteration in range(ITERS):
        image = None
        fields.append([])
        gradients, gathered, sent = [], [], []
        after = lhs
        for base, width, mode in parts:
            gradient = adjoint(turn_of(mode), kernel, after, base, width, pieces_of(mode))
            after = then(lhs, gradient[-1])
            gradients.append(gradient)
            if TIE and gathered and mode == "relay":
                gradient = [then(x, gathered[-1][TIE - 1]) for x in gradient]
            gathered.append(pair_up(scatter(gradient, mode), mode))
        for n, (_, _, mode) in enumerate(parts):
            got = gathered[n]
            if n + 1 < len(parts):
                got = [then(got[0], gradients[n + 1][-1])] + got[1:]
            field, alignment = tapered(got, mode)
            if TIE2 and sent and mode == "relay":
                field = [then(x, *sent[-1][1][1:]) for x in field]
            sent.append((field, scatter(field, mode), alignment))
        for n, (base, _, mode) in enumerate(parts):
            _, field, alignment = sent[n]
            if n + 1 < len(parts):
                field = [then(field[0], sent[n + 1][0][-1])] + field[1:]
            image = forward(turn_of(mode), kernel, field, alignment, image, base)
            fields[-1].append(field)
        got = swap(image) if src_count == 2 else lax.psum(image, "src") - image
        projected, sums = merge(image, got, count)
        length, residual, lhs = advance(projected, residual, exchange(sums, 16), fl, points)
        lengths.append(length)
    spans = [(base, width) for base, width, _ in parts]
    turns = jnp.concatenate([turn_of(mode) for _, _, mode in parts])
    estimate = estimate_of(turns, lengths, fields, spans, fl, points)
    share = receivers // src_count
    residual = residual.reshape(fl, 2, points, receivers)
    residual = lax.dynamic_slice_in_dim(residual, lax.axis_index("src") * share, share, 3)
    return estimate, residual.transpose(1, 0, 3, 2)


def solution(mesh):
    in_specs = (P("grp", "freq", None, "src"), P("grp", "freq", None, None), P("grp"), P("grp"))
    out_specs = (P("grp", "freq", None, "src"), P("grp", "freq", "src", None))
    return jax.shard_map(body, mesh=mesh, in_specs=in_specs, out_specs=out_specs, check_vma=False)
```

time: 236 us -> 209 us (0.89)
  waiting for transfers between devices: 77.2 us -> 42.6 us
  other arithmetic: 18.8 us -> 2.57 us
  Pallas kernels: 89.4 us -> 101 us
  starting transfers between devices: 39 us -> 48.7 us
  local copies, waits for them, and re-layouts: 5.66 us -> 12.1 us
    all_to_all x8 -> x2, waiting for transfers between devices: 56 us -> 12.4 us  [exchange(): lax.all_to_all(x.reshape(-1, rows, width), 'freq', 0, 0, tiled=True)]
    ppermute x6 -> x28, starting transfers between devices: 5.3 us -> 41.1 us  [send(): lax.ppermute(x, 'freq', [(i, i ^ hop) for i in range(lax.axis_size('freq'...]
    all_to_all x8 -> x2, starting transfers between devices: 33.5 us -> 7.48 us  [exchange(): lax.all_to_all(x.reshape(-1, rows, width), 'freq', 0, 0, tiled=True)]
    pallas_call x12 -> x17, Pallas kernels: 89.4 us -> 101 us  [the longest x4 41.5 us: forward(): pl.pallas_call(body, in_specs=specs + [in_vmem()] * (len(start) + pieces)...]
    ppermute x6 -> x28, waiting for transfers between devices: 17.8 us -> 26.8 us  [send(): lax.ppermute(x, 'freq', [(i, i ^ hop) for i in range(lax.axis_size('freq'...]
    add x9 -> x0, other arithmetic: 8.99 us -> none  [the longest x6 5.41 us: total_over(): x = x + lax.ppermute(x, axis, [(i, i ^ hop) for i in range(size)])]
    unnamed x31 -> x72, local copies, waits for them, and re-layouts: 3.22 us -> 9.26 us
    another operation x2 -> x0, other arithmetic: 2.7 us -> none  [body(): sums = jnp.stack([jnp.sum(image[-8:]), jnp.sum(projected * projected)])]
  transfers between devices with their start and end apart: 16 -> 32, of which waited for: 16 -> 13; matrix products, arithmetic and copies ran while one was open for 1% -> 2% of each run, Pallas kernels for 21% -> 24%
where the time goes in v2:
time: 209 us
  Pallas kernels  101 us (48%)
  starting transfers between devices  48.7 us (23%)
  waiting for transfers between devices  42.6 us (20%)
  local copies, waits for them, and re-layouts  12.1 us (6%)
  other arithmetic  2.57 us (1%)
    pallas_call x4, Pallas kernels, forward(): pl.pallas_call(body, in_specs=specs + [in_vmem()] * (len(start) + pieces)...  41.5 us
    ppermute x28, starting transfers between devices, send(): lax.ppermute(x, 'freq', [(i, i ^ hop) for i in range(lax.axis_size('freq'...  41.1 us
    pallas_call x4, Pallas kernels, adjoint(): pl.pallas_call(functools.partial(adjoint_body, points=points, base=base,...  37.9 us
    ppermute x28, waiting for transfers between devices, send(): lax.ppermute(x, 'freq', [(i, i ^ hop) for i in range(lax.axis_size('freq'...  26.8 us
    all_to_all x2, waiting for transfers between devices, exchange(): lax.all_to_all(x.reshape(-1, rows, width), 'freq', 0, 0, tiled=True)  12.4 us
    pallas_call x4, Pallas kernels, taper(): pl.pallas_call(functools.partial(taper_body, inputs=len(blocks), points=p...  9.72 us
    unnamed x72, local copies, waits for them, and re-layouts  9.26 us
    all_to_all x2, starting transfers between devices, exchange(): lax.all_to_all(x.reshape(-1, rows, width), 'freq', 0, 0, tiled=True)  7.48 us
  transfers between devices with their start and end apart: 32, of which 13 were waited for; matrix products, arithmetic and copies ran while one was open for 2% of the time, Pallas kernels for 24%

profile of v2, /device:TPU:0, one launch (start us, length us, event | category | flops | bytes accessed | tf_op | source)
XLA Modules:
  0.0 208.7 jit_solution(14403727610632969697)
XLA Ops:
  2.5 9.5 %adjoint.4 = (bf16[32,2048]{1,0:T(8,128)(2,1)}, bf16[32,2048]{1,0:T(8,128)(2,1)}, bf16[32,2048]{1,0:T(8,128)(2,1)}, bf16[32,2048]{1,0:T(8,128)(2,1)}) custom-call(s32[1]{0:T(128)} %bitcast.turn_ref.turn, bf16[8,16,640]{2,1,0:T(8,128)(2,1)} %maximum_maximum_fusion.l_ref, bf16[2,8,320,4096]{3,2,1,0:T(8,128)(2,1)} %k_hbm.11), custom_call_target="tpu_custom_call" | custom-call | flops 2684354560 | bytes 20971520 | tf_op jit(solution)/shard_map/adjoint/pallas_call | solution.py:94
  12.0 3.1 %collective-permute-start = (bf16[32,2048]{1,0:T(8,128)(2,1)}, bf16[32,2048]{1,0:T(8,128)(2,1)S(1)}, u32[]{:S(2)}, u32[]{:S(2)}) collective-permute-start(bf16[32,2048]{1,0:T(8,128)(2,1)} %get-tuple-element.73), channel_id=1, source_target_pairs={{0,4},{2,6},{4,0},{6,2},{8,12},{10,14},{12,8},{14,10},{1,5},{3,7},... | collective-permute-start | bytes 393224 | tf_op jit(solution)/shard_map/ppermute | solution.py:360
  15.1 2.6 %collective-permute-start.1 = (bf16[32,2048]{1,0:T(8,128)(2,1)}, bf16[32,2048]{1,0:T(8,128)(2,1)S(1)}, u32[]{:S(2)}, u32[]{:S(2)}) collective-permute-start(bf16[32,2048]{1,0:T(8,128)(2,1)} %get-tuple-element.74), channel_id=1, source_target_pairs={{0,8},{2,10},{4,12},{6,14},{8,0},{10,2},{12,4},{14,6},{1,9},{3,11}... | collective-permute-start | bytes 393224 | tf_op jit(solution)/shard_map/ppermute | solution.py:360
  18.0 9.5 %adjoint.5 = (bf16[32,2048]{1,0:T(8,128)(2,1)}, bf16[32,2048]{1,0:T(8,128)(2,1)}, bf16[32,2048]{1,0:T(8,128)(2,1)}, bf16[32,2048]{1,0:T(8,128)(2,1)}) custom-call(s32[1]{0:T(128)} %bitcast.turn_ref.turn, bf16[8,16,640]{2,1,0:T(8,128)(2,1)} %maximum_maximum_fusion.l_ref, bf16[2,8,320,4096]{3,2,1,0:T(8,128)(2,1)} %k_hbm.11), custom_call_target="tpu_custom_call" | custom-call | flops 2684354560 | bytes 20971520 | tf_op jit(solution)/shard_map/adjoint/pallas_call | solution.py:94
  36.1 7.3 %collective-permute-done.4 = bf16[32,2048]{1,0:T(8,128)(2,1)S(1)} collective-permute-done((bf16[32,2048]{1,0:T(8,128)(2,1)}, bf16[32,2048]{1,0:T(8,128)(2,1)S(1)}, u32[]{:S(2)}, u32[]{:S(2)}) %collective-permute-start.4) | collective-permute-done | bytes 131104 | tf_op jit(solution)/shard_map/ppermute | solution.py:360
  45.8 2.5 %taper.5 = (bf16[32,2048]{1,0:T(8,128)(2,1)}, bf16[32,2048]{1,0:T(8,128)(2,1)}, bf16[32,2048]{1,0:T(8,128)(2,1)}, bf16[32,2048]{1,0:T(8,128)(2,1)}, f32[8,128]{1,0:T(8,128)}) custom-call(f32[2,64,128]{2,1,0:T(8,128)} %fusion.t_ref, bf16[128,2048]{1,0:T(8,128)(2,1)} %copy-done, bf16[128,2048]{1,0:T(8,128)(2,1)} %copy-done.18), custom_call_target="tpu_custom_call" | custom-call | flops 201326592 | bytes 2097152 | tf_op jit(solution)/shard_map/taper/pallas_call | solution.py:231
  56.6 5.1 %collective-permute-done.9.rest_2_.refs_5_ = bf16[32,2048]{1,0:T(8,128)(2,1)S(1)} collective-permute-done((bf16[32,2048]{1,0:T(8,128)(2,1)}, bf16[32,2048]{1,0:T(8,128)(2,1)S(1)}, u32[]{:S(2)}, u32[]{:S(2)}) %collective-permute-start.9) | collective-permute-done | bytes 131104 | tf_op jit(solution)/shard_map/ppermute | solution.py:360
  66.1 10.3 %forward.4.init_ref = f32[136,320]{1,0:T(8,128)} custom-call(s32[1]{0:T(128)} %bitcast.turn_ref.turn, bf16[2,8,320,4096]{3,2,1,0:T(8,128)(2,1)} %k_hbm.11, f32[8,128]{1,0:T(8,128)} %get-tuple-element.84.al, bf16[32,2048]{1,0:T(8,128)(2,1)} %get-tuple-element.91.rest_0_.refs_3_, bf16[32,2048]{1,0:T(8,128)(2,1)} %copy-done.5, bf16[32,2048]{1,0:T(8,128)(2,1)} %copy-done.6, ...), custom_call_target="tpu_custom_call" | custom-call | flops 2684354560 | bytes 20971520 | tf_op jit(solution)/shard_map/forward/pallas_call | solution.py:180
  77.3 10.4 %forward.5.own_ref = f32[136,320]{1,0:T(8,128)} custom-call(s32[1]{0:T(128)} %bitcast.turn_ref.turn, bf16[2,8,320,4096]{3,2,1,0:T(8,128)(2,1)} %k_hbm.11, f32[8,128]{1,0:T(8,128)} %get-tuple-element.82.al_ref, f32[136,320]{1,0:T(8,128)} %forward.4.init_ref, bf16[32,2048]{1,0:T(8,128)(2,1)} %get-tuple-element.93.refs_0_.refs_11_, bf16[32,2048]{1,0:T(8,128)(2,1)} %copy-done.9, ...), custom_call_target="tpu_custom_call" | custom-call | flops 2684354560 | bytes 20971520 | tf_op jit(solution)/shard_map/forward/pallas_call | solution.py:180
  91.9 4.1 %all-to-all-start = ((f32[8,16,128]{2,1,0:T(8,128)}), f32[8,16,128]{2,1,0:T(8,128)S(1)}, u32[]{:S(2)}, u32[]{:S(2)}) async-start(f32[8,16,128]{2,1,0:T(8,128)} %bitcast.39), calls=%async_computation | async-start | bytes 131072 | tf_op jit(solution)/shard_map/all_to_all | solution.py:365
  96.7 6.2 %all-to-all-done = f32[8,16,128]{2,1,0:T(8,128)S(1)} async-done(((f32[8,16,128]{2,1,0:T(8,128)}), f32[8,16,128]{2,1,0:T(8,128)S(1)}, u32[]{:S(2)}, u32[]{:S(2)}) %all-to-all-start) | async-done | bytes 65568 | tf_op jit(solution)/shard_map/all_to_all | solution.py:365
  105.5 9.5 %adjoint.6 = (bf16[32,2048]{1,0:T(8,128)(2,1)}, bf16[32,2048]{1,0:T(8,128)(2,1)}, bf16[32,2048]{1,0:T(8,128)(2,1)}, bf16[32,2048]{1,0:T(8,128)(2,1)}) custom-call(s32[1]{0:T(128)} %bitcast.turn_ref.turn, bf16[8,16,640]{2,1,0:T(8,128)(2,1)} %get-tuple-element.103.l_ref, bf16[2,8,320,4096]{3,2,1,0:T(8,128)(2,1)} %k_hbm.11), custom_call_target="tpu_custom_call" | custom-call | flops 2684354560 | bytes 20971520 | tf_op jit(solution)/shard_map/adjoint/pallas_call | solution.py:94
  116.0 3.3 %collective-permute-start.16 = (bf16[32,2048]{1,0:T(8,128)(2,1)}, bf16[32,2048]{1,0:T(8,128)(2,1)S(1)}, u32[]{:S(2)}, u32[]{:S(2)}) collective-permute-start(bf16[32,2048]{1,0:T(8,128)(2,1)} %get-tuple-element.107), channel_id=1, source_target_pairs={{0,8},{2,10},{4,12},{6,14},{8,0},{10,2},{12,4},{14,6},{1,9},{3,11}... | collective-permute-start | bytes 393224 | tf_op jit(solution)/shard_map/ppermute | solution.py:360
  119.4 9.4 %adjoint.7 = (bf16[32,2048]{1,0:T(8,128)(2,1)}, bf16[32,2048]{1,0:T(8,128)(2,1)}, bf16[32,2048]{1,0:T(8,128)(2,1)}, bf16[32,2048]{1,0:T(8,128)(2,1)}) custom-call(s32[1]{0:T(128)} %bitcast.turn_ref.turn, bf16[8,16,640]{2,1,0:T(8,128)(2,1)} %get-tuple-element.103.l_ref, bf16[2,8,320,4096]{3,2,1,0:T(8,128)(2,1)} %k_hbm.11), custom_call_target="tpu_custom_call" | custom-call | flops 2684354560 | bytes 20971520 | tf_op jit(solution)/shard_map/adjoint/pallas_call | solution.py:94
  131.0 2.8 %collective-permute-start.20 = (bf16[32,2048]{1,0:T(8,128)(2,1)}, bf16[32,2048]{1,0:T(8,128)(2,1)S(1)}, u32[]{:S(2)}, u32[]{:S(2)}) collective-permute-start(bf16[32,2048]{1,0:T(8,128)(2,1)} %get-tuple-element.114), channel_id=1, source_target_pairs={{0,12},{2,14},{4,8},{6,10},{8,4},{10,6},{12,0},{14,2},{1,13},{3,15... | collective-permute-start | bytes 393224 | tf_op jit(solution)/shard_map/ppermute | solution.py:360
  136.0 4.6 %collective-permute-done.19 = bf16[32,2048]{1,0:T(8,128)(2,1)S(1)} collective-permute-done((bf16[32,2048]{1,0:T(8,128)(2,1)}, bf16[32,2048]{1,0:T(8,128)(2,1)S(1)}, u32[]{:S(2)}, u32[]{:S(2)}) %collective-permute-start.19) | collective-permute-done | bytes 131104 | tf_op jit(solution)/shard_map/ppermute | solution.py:360
  143.1 2.4 %taper.7 = (bf16[32,2048]{1,0:T(8,128)(2,1)}, bf16[32,2048]{1,0:T(8,128)(2,1)}, bf16[32,2048]{1,0:T(8,128)(2,1)}, bf16[32,2048]{1,0:T(8,128)(2,1)}, f32[8,128]{1,0:T(8,128)}) custom-call(f32[2,64,128]{2,1,0:T(8,128)} %fusion.t_ref, bf16[128,2048]{1,0:T(8,128)(2,1)} %copy-done.2, bf16[128,2048]{1,0:T(8,128)(2,1)} %copy-done.19), custom_call_target="tpu_custom_call" | custom-call | flops 201326592 | bytes 2097152 | tf_op jit(solution)/shard_map/taper/pallas_call | solution.py:231
  155.2 4.6 %collective-permute-done.24.rest_2_.refs_9_ = bf16[32,2048]{1,0:T(8,128)(2,1)S(1)} collective-permute-done((bf16[32,2048]{1,0:T(8,128)(2,1)}, bf16[32,2048]{1,0:T(8,128)(2,1)S(1)}, u32[]{:S(2)}, u32[]{:S(2)}) %collective-permute-start.24) | collective-permute-done | bytes 131104 | tf_op jit(solution)/shard_map/ppermute | solution.py:360
  160.1 2.8 %collective-permute-start.26 = (bf16[32,2048]{1,0:T(8,128)(2,1)}, bf16[32,2048]{1,0:T(8,128)(2,1)S(1)}, u32[]{:S(2)}, u32[]{:S(2)}) collective-permute-start(bf16[32,2048]{1,0:T(8,128)(2,1)} %get-tuple-element.128), channel_id=1, source_target_pairs={{0,4},{2,6},{4,0},{6,2},{8,12},{10,14},{12,8},{14,10},{1,5},{3,7},... | collective-permute-start | bytes 393224 | tf_op jit(solution)/shard_map/ppermute | solution.py:360
  164.2 10.3 %forward.6.init_ref = f32[136,320]{1,0:T(8,128)} custom-call(s32[1]{0:T(128)} %bitcast.turn_ref.turn, bf16[2,8,320,4096]{3,2,1,0:T(8,128)(2,1)} %k_hbm.11, f32[8,128]{1,0:T(8,128)} %get-tuple-element.117.al, bf16[32,2048]{1,0:T(8,128)(2,1)} %get-tuple-element.124.rest_0_.refs_7_, bf16[32,2048]{1,0:T(8,128)(2,1)} %copy-done.11, bf16[32,2048]{1,0:T(8,128)(2,1)} %copy-done.12, ...), custom_call_target="tpu_custom_call" | custom-call | flops 2684354560 | bytes 20971520 | tf_op jit(solution)/shard_map/forward/pallas_call | solution.py:180
  175.3 10.4 %forward.7.own_ref = f32[136,320]{1,0:T(8,128)} custom-call(s32[1]{0:T(128)} %bitcast.turn_ref.turn, bf16[2,8,320,4096]{3,2,1,0:T(8,128)(2,1)} %k_hbm.11, f32[8,128]{1,0:T(8,128)} %get-tuple-element.115.al_ref, f32[136,320]{1,0:T(8,128)} %forward.6.init_ref, bf16[32,2048]{1,0:T(8,128)(2,1)} %get-tuple-element.126.refs_0_.refs_15_, ...), custom_call_target="tpu_custom_call" | custom-call | flops 2684354560 | bytes 20971520 | tf_op jit(solution)/shard_map/forward/pallas_call | solution.py:180
  189.9 3.4 %all-to-all-start.1 = ((f32[8,16,128]{2,1,0:T(8,128)}), f32[8,16,128]{2,1,0:T(8,128)S(1)}, u32[]{:S(2)}, u32[]{:S(2)}) async-start(f32[8,16,128]{2,1,0:T(8,128)} %bitcast.38), calls=%async_computation.1 | async-start | bytes 131072 | tf_op jit(solution)/shard_map/all_to_all | solution.py:365
  193.9 6.2 %all-to-all-done.1 = f32[8,16,128]{2,1,0:T(8,128)S(1)} async-done(((f32[8,16,128]{2,1,0:T(8,128)}), f32[8,16,128]{2,1,0:T(8,128)S(1)}, u32[]{:S(2)}, u32[]{:S(2)}) %all-to-all-start.1) | async-done | bytes 65568 | tf_op jit(solution)/shard_map/all_to_all | solution.py:365
  204.3 4.4 %estimate.1 = f32[2,8,8,4096]{3,2,1,0:T(8,128)} custom-call(s32[2]{0:T(128)} %pad_add_fusion.refs_0_, f32[8,128]{1,0:T(8,128)} %get-tuple-element.100.refs_1_, f32[8,128]{1,0:T(8,128)} %get-tuple-element.134.refs_2_, bf16[32,2048]{1,0:T(8,128)(2,1)} %get-tuple-element.91.rest_0_.refs_3_, bf16[32,2048]{1,0:T(8,128)(2,1)} %copy-done.5, ...), custom_call_target="tpu_custom_call" | custom-call | tf_op jit(solution)/shard_map/estimate/pallas_call | solution.py:342
  (147 shorter events, 62.8 us)
Async XLA Ops:
  12.0 15.8 %collective-permute-start = (bf16[32,2048]{1,0:T(8,128)(2,1)}, bf16[32,2048]{1,0:T(8,128)(2,1)S(1)}, u32[]{:S(2)}, u32[]{:S(2)}) collective-permute-start(bf16[32,2048]{1,0:T(8,128)(2,1)} %get-tuple-element.73), channel_id=1, source_target_pairs={{0,4},{2,6},{4,0},{6,2},{8,12},{10,14},{12,8},{14,10},{1,5},{3,7},... | collective-permute-start | bytes 393224 | tf_op jit(solution)/shard_map/ppermute | solution.py:360
  15.1 13.1 %collective-permute-start.1 = (bf16[32,2048]{1,0:T(8,128)(2,1)}, bf16[32,2048]{1,0:T(8,128)(2,1)S(1)}, u32[]{:S(2)}, u32[]{:S(2)}) collective-permute-start(bf16[32,2048]{1,0:T(8,128)(2,1)} %get-tuple-element.74), channel_id=1, source_target_pairs={{0,8},{2,10},{4,12},{6,14},{8,0},{10,2},{12,4},{14,6},{1,9},{3,11}... | collective-permute-start | bytes 393224 | tf_op jit(solution)/shard_map/ppermute | solution.py:360
  17.7 10.6 %collective-permute-start.2 = (bf16[32,2048]{1,0:T(8,128)(2,1)}, bf16[32,2048]{1,0:T(8,128)(2,1)S(1)}, u32[]{:S(2)}, u32[]{:S(2)}) collective-permute-start(bf16[32,2048]{1,0:T(8,128)(2,1)} %get-tuple-element.69), channel_id=1, source_target_pairs={{0,12},{2,14},{4,8},{6,10},{8,4},{10,6},{12,0},{14,2},{1,13},{3,15... | collective-permute-start | bytes 393224 | tf_op jit(solution)/shard_map/ppermute | solution.py:360
  28.3 16.7 %collective-permute-start.7 = (bf16[128,2048]{1,0:T(8,128)(2,1)S(1)}, bf16[128,2048]{1,0:T(8,128)(2,1)S(1)}, u32[]{:S(2)}, u32[]{:S(2)}) collective-permute-start(bf16[128,2048]{1,0:T(8,128)(2,1)S(1)} %constant_dynamic-update-slice_fusion.refs_0_), channel_id=1, source_target_pairs={{0,2},{2,0},{4,6},{6,4},{8,10},{10,8},{12,14},{14,12},{1,3},{3,1},... | collective-permute-start | bytes 1572872 | tf_op jit(solution)/shard_map/ppermute | solution.py:360
  31.8 11.7 %collective-permute-start.4 = (bf16[32,2048]{1,0:T(8,128)(2,1)}, bf16[32,2048]{1,0:T(8,128)(2,1)S(1)}, u32[]{:S(2)}, u32[]{:S(2)}) collective-permute-start(bf16[32,2048]{1,0:T(8,128)(2,1)} %get-tuple-element.79), channel_id=1, source_target_pairs={{0,8},{2,10},{4,12},{6,14},{8,0},{10,2},{12,4},{14,6},{1,9},{3,11}... | collective-permute-start | bytes 393224 | tf_op jit(solution)/shard_map/ppermute | solution.py:360
  43.5 9.8 %collective-permute-start.6 = (bf16[128,2048]{1,0:T(8,128)(2,1)S(1)}, bf16[128,2048]{1,0:T(8,128)(2,1)S(1)}, u32[]{:S(2)}, u32[]{:S(2)}) collective-permute-start(bf16[128,2048]{1,0:T(8,128)(2,1)S(1)} %constant_dynamic-update-slice_fusion.4.refs_0_), channel_id=1, source_target_pairs={{0,2},{2,0},{4,6},{6,4},{8,10},{10,8},{12,14},{14,12},{1,3},{3,1},... | collective-permute-start | bytes 1572872 | tf_op jit(solution)/shard_map/ppermute | solution.py:360
  50.2 11.5 %collective-permute-start.9 = (bf16[32,2048]{1,0:T(8,128)(2,1)}, bf16[32,2048]{1,0:T(8,128)(2,1)S(1)}, u32[]{:S(2)}, u32[]{:S(2)}) collective-permute-start(bf16[32,2048]{1,0:T(8,128)(2,1)} %get-tuple-element.88), channel_id=1, source_target_pairs={{0,8},{2,10},{4,12},{6,14},{8,0},{10,2},{12,4},{14,6},{1,9},{3,11}... | collective-permute-start | bytes 393224 | tf_op jit(solution)/shard_map/ppermute | solution.py:360
  51.5 10.2 %collective-permute-start.10 = (bf16[32,2048]{1,0:T(8,128)(2,1)}, bf16[32,2048]{1,0:T(8,128)(2,1)S(1)}, u32[]{:S(2)}, u32[]{:S(2)}) collective-permute-start(bf16[32,2048]{1,0:T(8,128)(2,1)} %get-tuple-element.89), channel_id=1, source_target_pairs={{0,12},{2,14},{4,8},{6,10},{8,4},{10,6},{12,0},{14,2},{1,13},{3,15... | collective-permute-start | bytes 393224 | tf_op jit(solution)/shard_map/ppermute | solution.py:360
  61.7 14.8 %collective-permute-start.13 = (bf16[32,2048]{1,0:T(8,128)(2,1)}, bf16[32,2048]{1,0:T(8,128)(2,1)S(1)}, u32[]{:S(2)}, u32[]{:S(2)}) collective-permute-start(bf16[32,2048]{1,0:T(8,128)(2,1)} %get-tuple-element.90), channel_id=1, source_target_pairs={{0,12},{2,14},{4,8},{6,10},{8,4},{10,6},{12,0},{14,2},{1,13},{3,15... | collective-permute-start | bytes 393224 | tf_op jit(solution)/shard_map/ppermute | solution.py:360
  63.6 12.9 %collective-permute-start.11 = (bf16[32,2048]{1,0:T(8,128)(2,1)}, bf16[32,2048]{1,0:T(8,128)(2,1)S(1)}, u32[]{:S(2)}, u32[]{:S(2)}) collective-permute-start(bf16[32,2048]{1,0:T(8,128)(2,1)} %get-tuple-element.95), channel_id=1, source_target_pairs={{0,4},{2,6},{4,0},{6,2},{8,12},{10,14},{12,8},{14,10},{1,5},{3,7},... | collective-permute-start | bytes 393224 | tf_op jit(solution)/shard_map/ppermute | solution.py:360
  65.2 11.4 %collective-permute-start.12 = (bf16[32,2048]{1,0:T(8,128)(2,1)}, bf16[32,2048]{1,0:T(8,128)(2,1)S(1)}, u32[]{:S(2)}, u32[]{:S(2)}) collective-permute-start(bf16[32,2048]{1,0:T(8,128)(2,1)} %get-tuple-element.97), channel_id=1, source_target_pairs={{0,8},{2,10},{4,12},{6,14},{8,0},{10,2},{12,4},{14,6},{1,9},{3,11}... | collective-permute-start | bytes 393224 | tf_op jit(solution)/shard_map/ppermute | solution.py:360
  91.9 11.0 %all-to-all-start = ((f32[8,16,128]{2,1,0:T(8,128)}), f32[8,16,128]{2,1,0:T(8,128)S(1)}, u32[]{:S(2)}, u32[]{:S(2)}) async-start(f32[8,16,128]{2,1,0:T(8,128)} %bitcast.39), calls=%async_computation | async-start | bytes 131072 | tf_op jit(solution)/shard_map/all_to_all | solution.py:365
  114.9 14.0 %collective-permute-start.17 = (bf16[32,2048]{1,0:T(8,128)(2,1)}, bf16[32,2048]{1,0:T(8,128)(2,1)S(1)}, u32[]{:S(2)}, u32[]{:S(2)}) collective-permute-start(bf16[32,2048]{1,0:T(8,128)(2,1)} %get-tuple-element.102), channel_id=1, source_target_pairs={{0,12},{2,14},{4,8},{6,10},{8,4},{10,6},{12,0},{14,2},{1,13},{3,15... | collective-permute-start | bytes 393224 | tf_op jit(solution)/shard_map/ppermute | solution.py:360
  115.6 13.3 %collective-permute-start.15 = (bf16[32,2048]{1,0:T(8,128)(2,1)}, bf16[32,2048]{1,0:T(8,128)(2,1)S(1)}, u32[]{:S(2)}, u32[]{:S(2)}) collective-permute-start(bf16[32,2048]{1,0:T(8,128)(2,1)} %get-tuple-element.106), channel_id=1, source_target_pairs={{0,4},{2,6},{4,0},{6,2},{8,12},{10,14},{12,8},{14,10},{1,5},{3,7},... | collective-permute-start | bytes 393224 | tf_op jit(solution)/shard_map/ppermute | solution.py:360
  116.0 12.9 %collective-permute-start.16 = (bf16[32,2048]{1,0:T(8,128)(2,1)}, bf16[32,2048]{1,0:T(8,128)(2,1)S(1)}, u32[]{:S(2)}, u32[]{:S(2)}) collective-permute-start(bf16[32,2048]{1,0:T(8,128)(2,1)} %get-tuple-element.107), channel_id=1, source_target_pairs={{0,8},{2,10},{4,12},{6,14},{8,0},{10,2},{12,4},{14,6},{1,9},{3,11}... | collective-permute-start | bytes 393224 | tf_op jit(solution)/shard_map/ppermute | solution.py:360
  129.0 13.4 %collective-permute-start.22 = (bf16[128,2048]{1,0:T(8,128)(2,1)S(1)}, bf16[128,2048]{1,0:T(8,128)(2,1)S(1)}, u32[]{:S(2)}, u32[]{:S(2)}) collective-permute-start(bf16[128,2048]{1,0:T(8,128)(2,1)S(1)} %constant_dynamic-update-slice_fusion.8.refs_0_), channel_id=1, source_target_pairs={{0,2},{2,0},{4,6},{6,4},{8,10},{10,8},{12,14},{14,12},{1,3},{3,1},... | collective-permute-start | bytes 1572872 | tf_op jit(solution)/shard_map/ppermute | solution.py:360
  129.4 11.2 %collective-permute-start.19 = (bf16[32,2048]{1,0:T(8,128)(2,1)}, bf16[32,2048]{1,0:T(8,128)(2,1)S(1)}, u32[]{:S(2)}, u32[]{:S(2)}) collective-permute-start(bf16[32,2048]{1,0:T(8,128)(2,1)} %get-tuple-element.112), channel_id=1, source_target_pairs={{0,8},{2,10},{4,12},{6,14},{8,0},{10,2},{12,4},{14,6},{1,9},{3,11}... | collective-permute-start | bytes 393224 | tf_op jit(solution)/shard_map/ppermute | solution.py:360
  140.7 11.3 %collective-permute-start.21 = (bf16[128,2048]{1,0:T(8,128)(2,1)S(1)}, bf16[128,2048]{1,0:T(8,128)(2,1)S(1)}, u32[]{:S(2)}, u32[]{:S(2)}) collective-permute-start(bf16[128,2048]{1,0:T(8,128)(2,1)S(1)} %constant_dynamic-update-slice_fusion.12.refs_0_), channel_id=1, source_target_pairs={{0,2},{2,0},{4,6},{6,4},{8,10},{10,8},{12,14},{14,12},{1,3},{3,1},... | collective-permute-start | bytes 1572872 | tf_op jit(solution)/shard_map/ppermute | solution.py:360
  147.5 12.2 %collective-permute-start.24 = (bf16[32,2048]{1,0:T(8,128)(2,1)}, bf16[32,2048]{1,0:T(8,128)(2,1)S(1)}, u32[]{:S(2)}, u32[]{:S(2)}) collective-permute-start(bf16[32,2048]{1,0:T(8,128)(2,1)} %get-tuple-element.121), channel_id=1, source_target_pairs={{0,8},{2,10},{4,12},{6,14},{8,0},{10,2},{12,4},{14,6},{1,9},{3,11}... | collective-permute-start | bytes 393224 | tf_op jit(solution)/shard_map/ppermute | solution.py:360
  148.0 11.8 %collective-permute-start.25 = (bf16[32,2048]{1,0:T(8,128)(2,1)}, bf16[32,2048]{1,0:T(8,128)(2,1)S(1)}, u32[]{:S(2)}, u32[]{:S(2)}) collective-permute-start(bf16[32,2048]{1,0:T(8,128)(2,1)} %get-tuple-element.122), channel_id=1, source_target_pairs={{0,12},{2,14},{4,8},{6,10},{8,4},{10,6},{12,0},{14,2},{1,13},{3,15... | collective-permute-start | bytes 393224 | tf_op jit(solution)/shard_map/ppermute | solution.py:360
  159.8 14.8 %collective-permute-start.28 = (bf16[32,2048]{1,0:T(8,128)(2,1)}, bf16[32,2048]{1,0:T(8,128)(2,1)S(1)}, u32[]{:S(2)}, u32[]{:S(2)}) collective-permute-start(bf16[32,2048]{1,0:T(8,128)(2,1)} %get-tuple-element.123), channel_id=1, source_target_pairs={{0,12},{2,14},{4,8},{6,10},{8,4},{10,6},{12,0},{14,2},{1,13},{3,15... | collective-permute-start | bytes 393224 | tf_op jit(solution)/shard_map/ppermute | solution.py:360
  160.1 14.4 %collective-permute-start.26 = (bf16[32,2048]{1,0:T(8,128)(2,1)}, bf16[32,2048]{1,0:T(8,128)(2,1)S(1)}, u32[]{:S(2)}, u32[]{:S(2)}) collective-permute-start(bf16[32,2048]{1,0:T(8,128)(2,1)} %get-tuple-element.128), channel_id=1, source_target_pairs={{0,4},{2,6},{4,0},{6,2},{8,12},{10,14},{12,8},{14,10},{1,5},{3,7},... | collective-permute-start | bytes 393224 | tf_op jit(solution)/shard_map/ppermute | solution.py:360
  163.0 11.6 %collective-permute-start.27 = (bf16[32,2048]{1,0:T(8,128)(2,1)}, bf16[32,2048]{1,0:T(8,128)(2,1)S(1)}, u32[]{:S(2)}, u32[]{:S(2)}) collective-permute-start(bf16[32,2048]{1,0:T(8,128)(2,1)} %get-tuple-element.130), channel_id=1, source_target_pairs={{0,8},{2,10},{4,12},{6,14},{8,0},{10,2},{12,4},{14,6},{1,9},{3,11}... | collective-permute-start | bytes 393224 | tf_op jit(solution)/shard_map/ppermute | solution.py:360
  189.9 10.2 %all-to-all-start.1 = ((f32[8,16,128]{2,1,0:T(8,128)}), f32[8,16,128]{2,1,0:T(8,128)S(1)}, u32[]{:S(2)}, u32[]{:S(2)}) async-start(f32[8,16,128]{2,1,0:T(8,128)} %bitcast.38), calls=%async_computation.1 | async-start | bytes 131072 | tf_op jit(solution)/shard_map/all_to_all | solution.py:365
  (38 other events, 262.2 us)

commit v3 on v2

--- a/solution.py
+++ b/solution.py
@@ -14,16 +14,13 @@
 LANES = 128
 BF16 = jnp.bfloat16
 F32 = jnp.float32
-VMEM_LIMIT = 56 * 2**20
+VMEM_LIMIT = 32 * 2**20
 PARTS = ((1, "relay"), (1, "relay"))
 ADJOINT_TILE = 2048
 ADJOINT_DEPTH = 9
 FORWARD_TILE = 2048
 FORWARD_DEPTH = 9
 FORWARD_GROUP = 1
-EARLY = False
-TIE = 1
-TIE2 = True
 
 
 def in_vmem():
@@ -270,8 +267,7 @@
 
 def step_body(p_ref, r_ref, s_ref, a_ref, new_ref, l_ref, *, fl, points):
     receivers = p_ref.shape[1]
-    sums = sum(s_ref[at : at + 16] for at in range(0, s_ref.shape[0], 16))
-    length = jnp.sum(sums[0:8], keepdims=True) / jnp.sum(sums[8:16], keepdims=True)
+    length = step_length(s_ref)
     a_ref[...] = jnp.broadcast_to(length, a_ref.shape)
     new = r_ref[...] - length * p_ref[...]
     new_ref[...] = new
@@ -309,47 +305,69 @@
     return lax.ppermute(x, "src", [(0, 1), (1, 0)])
 
 
-def estimate_body(*refs, spans, pieces, fl, points):
-    turn_ref, lengths = refs[0], refs[1 : 1 + ITERS]
-    fields, (e_ref, scr) = refs[1 + ITERS : -2], refs[-2:]
-    lengths = [ref[0:1, 0:1] for ref in lengths]
+def step_length(s_ref):
+    sums = sum(s_ref[at : at + 16] for at in range(0, s_ref.shape[0], 16))
+    return jnp.sum(sums[0:8], keepdims=True) / jnp.sum(sums[8:16], keepdims=True)
+
+
+def finish_body(place_ref, s_ref, p_ref, r_ref, *refs, spans, pieces):
+    earlier, fields, (e_hbm, out_ref, stage, scr, sem) = refs[: ITERS - 1], refs[ITERS - 1 : -5], refs[-5:]
+    _, fl, points, share = out_ref.shape
+    lengths = [ref[0:1, 0:1] for ref in earlier] + [step_length(s_ref)]
+    copies = []
     at = 0
     for part, ((base, width), count) in enumerate(zip(spans, pieces)):
         size = 2 * points * fl // count
-        turn = turn_ref[part]
+        turn = place_ref[1 + part]
 
         def one(i, carry, at=at, base=base, count=count, size=size, turn=turn):
             off = pl.multiple_of(i * LANES, LANES)
+            out = pl.ds(pl.multiple_of(base + i * LANES, LANES), LANES)
             for k in range(count):
-                value = sum(
-                    lengths[n] * fields[at + n * count + k][:, pl.ds(off, LANES)].astype(F32) for n in range(ITERS)
-                )
-                scr[i % 2, pl.ds(pl.multiple_of((turn ^ k) * size, size), size), :] = value
+                values = [fields[at + n * count + k][:, pl.ds(off, LANES)].astype(F32) for n in range(ITERS)]
+                rows = pl.ds(pl.multiple_of((turn ^ k) * size, size), size)
+                scr[i % 2, rows, :] = sum(a * x for a, x in zip(lengths, values))
             for c in range(2):
                 for f in range(fl):
-                    out = pl.ds(pl.multiple_of(base + i * LANES, LANES), LANES)
-                    e_ref[c, f, :, out] = scr[i % 2, pl.ds(c * fl + f, points, stride=2 * fl), :]
+                    stage[c, f, :, out] = scr[i % 2, pl.ds(c * fl + f, points, stride=2 * fl), :]
             return carry
 
         lax.fori_loop(0, width // LANES, one, 0, unroll=2)
+        span = pl.ds(base, width)
+        copies.append(
+            pltpu.make_async_copy(stage.at[:, :, :, span], e_hbm.at[:, :, :, span], sem.at[part])
+        )
+        copies[-1].start()
         at += ITERS * count
-
-
-def estimate_of(turns, lengths, fields, spans, fl, points):
+    residual = r_ref[...] - lengths[-1] * p_ref[...]
+    mine = residual[:, :share]
+    for n in range(1, residual.shape[1] // share):
+        mine = jnp.where(place_ref[0] == n, residual[:, n * share : (n + 1) * share], mine)
+    for c in range(2):
+        for f in range(fl):
+            top = (2 * f + c) * points
+            out_ref[c, f] = mine[top : top + points]
+    for copy in copies:
+        copy.wait()
+
+
+def finish(core, turns, sums, projected, residual, lengths, fields, spans, fl, points, share):
     parts = range(len(spans))
     flat = [x for part in parts for field in fields for x in field[part]]
-    sources = sum(width for _, width in spans)
+    shape = (2, fl, points, sum(width for _, width in spans))
     return pl.pallas_call(
-        functools.partial(
-            estimate_body, spans=spans, pieces=[len(fields[0][part]) for part in parts], fl=fl, points=points
-        ),
-        in_specs=[pl.BlockSpec(memory_space=pltpu.SMEM)] + [in_vmem()] * (len(lengths) + len(flat)),
-        out_specs=in_vmem(),
-        out_shape=jax.ShapeDtypeStruct((2, fl, points, sources), F32),
-        scratch_shapes=[pltpu.VMEM((2, 2 * points * fl, LANES), F32)],
+        functools.partial(finish_body, spans=spans, pieces=[len(fields[0][part]) for part in parts]),
+        in_specs=[pl.BlockSpec(memory_space=pltpu.SMEM)] + [in_vmem()] * (3 + len(lengths) + len(flat)),
+        out_specs=[pl.BlockSpec(memory_space=pl.ANY), in_vmem()],
+        out_shape=[jax.ShapeDtypeStruct(shape, F32), jax.ShapeDtypeStruct((2, fl, points, share), F32)],
+        scratch_shapes=[
+            pltpu.VMEM(shape, F32),
+            pltpu.VMEM((2, 2 * points * fl, LANES), F32),
+            pltpu.SemaphoreType.DMA((len(spans),)),
+        ],
         compiler_params=pltpu.CompilerParams(vmem_limit_bytes=VMEM_LIMIT),
-        name="estimate",
-    )(turns, *lengths, *flat)
+        name="finish",
+    )(jnp.concatenate([core] + turns), sums, projected, residual, *lengths, *flat)
 
 
 def then(x, *earlier):
@@ -415,9 +433,6 @@
     def pair_up(got, mode):
         if mode != "relay":
             return got
-        if EARLY:
-            rest = jnp.concatenate(got[1:], 0)
-            return [got[0], rest, send(got[0], 1), send(rest, 1)]
         joined = jnp.concatenate(got, 0)
         return [joined, send(joined, 1)]
 
@@ -449,15 +464,15 @@
             gradient = adjoint(turn_of(mode), kernel, after, base, width, pieces_of(mode))
             after = then(lhs, gradient[-1])
             gradients.append(gradient)
-            if TIE and gathered and mode == "relay":
-                gradient = [then(x, gathered[-1][TIE - 1]) for x in gradient]
+            if gathered and mode == "relay":
+                gradient = [then(x, gathered[-1][0]) for x in gradient]
             gathered.append(pair_up(scatter(gradient, mode), mode))
         for n, (_, _, mode) in enumerate(parts):
             got = gathered[n]
             if n + 1 < len(parts):
                 got = [then(got[0], gradients[n + 1][-1])] + got[1:]
             field, alignment = tapered(got, mode)
-            if TIE2 and sent and mode == "relay":
+            if sent and mode == "relay":
                 field = [then(x, *sent[-1][1][1:]) for x in field]
             sent.append((field, scatter(field, mode), alignment))
         for n, (base, _, mode) in enumerate(parts):
@@ -468,15 +483,18 @@
             fields[-1].append(field)
         got = swap(image) if src_count == 2 else lax.psum(image, "src") - image
         projected, sums = merge(image, got, count)
-        length, residual, lhs = advance(projected, residual, exchange(sums, 16), fl, points)
-        lengths.append(length)
+        sums = exchange(sums, 16)
+        if iteration + 1 < ITERS:
+            length, residual, lhs = advance(projected, residual, sums, fl, points)
+            lengths.append(length)
     spans = [(base, width) for base, width, _ in parts]
-    turns = jnp.concatenate([turn_of(mode) for _, _, mode in parts])
-    estimate = estimate_of(turns, lengths, fields, spans, fl, points)
+    turns = [turn_of(mode) for _, _, mode in parts]
+    core = lax.axis_index("src").reshape(1).astype(jnp.int32)
     share = receivers // src_count
-    residual = residual.reshape(fl, 2, points, receivers)
-    residual = lax.dynamic_slice_in_dim(residual, lax.axis_index("src") * share, share, 3)
-    return estimate, residual.transpose(1, 0, 3, 2)
+    estimate, residual = finish(
+        core, turns, sums, projected, residual, lengths, fields, spans, fl, points, share
+    )
+    return estimate, residual.transpose(0, 1, 3, 2)
 
 
 def solution(mesh):

time: 209 us -> 186 us (0.89)
  Pallas kernels: 101 us -> 76.2 us
  waiting for transfers between devices: 42.6 us -> 52.2 us
  local copies, waits for them, and re-layouts: 12.1 us -> 5.16 us
    ppermute x28, waiting for transfers between devices: 26.8 us -> 36.2 us  [send(): lax.ppermute(x, 'freq', [(i, i ^ hop) for i in range(lax.axis_size('freq'...]
    pallas_call x4, Pallas kernels: 9.72 us -> 1.76 us  [taper(): pl.pallas_call(functools.partial(taper_body, inputs=len(blocks), points=p...]
    pallas_call x4, Pallas kernels: 41.5 us -> 34.2 us  [forward(): pl.pallas_call(body, in_specs=specs + [in_vmem()] * (len(start) + pieces)...]
    pallas_call x4, Pallas kernels: 37.9 us -> 31 us  [adjoint(): pl.pallas_call(functools.partial(adjoint_body, points=points, base=base,...]
    unnamed x72 -> x38, local copies, waits for them, and re-layouts: 9.26 us -> 3.98 us
  transfers between devices with their start and end apart: 32 -> 32, of which waited for: 13 -> 16; matrix products, arithmetic and copies ran while one was open for 2% -> 1% of each run, Pallas kernels for 24% -> 19%
where the time goes in v3:
time: 186 us
  Pallas kernels  76.2 us (41%)
  waiting for transfers between devices  52.2 us (28%)
  starting transfers between devices  49.6 us (27%)
  local copies, waits for them, and re-layouts  5.16 us (3%)
    ppermute x28, starting transfers between devices, send(): lax.ppermute(x, 'freq', [(i, i ^ hop) for i in range(lax.axis_size('freq'...  41.9 us
    ppermute x28, waiting for transfers between devices, send(): lax.ppermute(x, 'freq', [(i, i ^ hop) for i in range(lax.axis_size('freq'...  36.2 us
    pallas_call x4, Pallas kernels, forward(): pl.pallas_call(body, in_specs=specs + [in_vmem()] * (len(start) + pieces)...  34.2 us
    pallas_call x4, Pallas kernels, adjoint(): pl.pallas_call(functools.partial(adjoint_body, points=points, base=base,...  31 us
    all_to_all x2, waiting for transfers between devices, exchange(): lax.all_to_all(x.reshape(-1, rows, width), 'freq', 0, 0, tiled=True)  13 us
    all_to_all x2, starting transfers between devices, exchange(): lax.all_to_all(x.reshape(-1, rows, width), 'freq', 0, 0, tiled=True)  7.63 us
    unnamed x38, local copies, waits for them, and re-layouts  3.98 us
    pallas_call x1, Pallas kernels, finish(): pl.pallas_call(functools.partial(finish_body, spans=spans, pieces=[len(fi...  3.84 us
  transfers between devices with their start and end apart: 32, of which 16 were waited for; matrix products, arithmetic and copies ran while one was open for 1% of the time, Pallas kernels for 19%

profile of v3, /device:TPU:0, one launch (start us, length us, event | category | flops | bytes accessed | tf_op | source)
XLA Modules:
  0.0 185.8 jit_solution(14925841750855555026)
XLA Ops:
  1.8 7.8 %adjoint.4 = (bf16[32,2048]{1,0:T(8,128)(2,1)S(1)}, bf16[32,2048]{1,0:T(8,128)(2,1)S(1)}, bf16[32,2048]{1,0:T(8,128)(2,1)S(1)}, bf16[32,2048]{1,0:T(8,128)(2,1)S(1)}) custom-call(s32[1]{0:T(128)} %bitcast.1.turn_ref.turn, bf16[8,16,640]{2,1,0:T(8,128)(2,1)S(1)} %maximum_maximum_fusion.l_ref, bf16[2,8,320,4096]{3,2,1,0:T(8,128)(2,1)} %k_hbm.11), custom_call_target="tpu_custom_call" | custom-call | flops 2684354560 | bytes 20971520 | tf_op jit(solution)/shard_map/adjoint/pallas_call | solution.py:91
  9.6 3.1 %collective-permute-start = (bf16[32,2048]{1,0:T(8,128)(2,1)S(1)}, bf16[32,2048]{1,0:T(8,128)(2,1)S(1)}, u32[]{:S(2)}, u32[]{:S(2)}) collective-permute-start(bf16[32,2048]{1,0:T(8,128)(2,1)S(1)} %get-tuple-element.73), channel_id=1, source_target_pairs={{0,4},{2,6},{4,0},{6,2},{8,12},{10,14},{12,8},{14,10},{1,5},{3,7},... | collective-permute-start | bytes 393224 | tf_op jit(solution)/shard_map/ppermute | solution.py:378
  12.7 2.6 %collective-permute-start.1 = (bf16[32,2048]{1,0:T(8,128)(2,1)S(1)}, bf16[32,2048]{1,0:T(8,128)(2,1)S(1)}, u32[]{:S(2)}, u32[]{:S(2)}) collective-permute-start(bf16[32,2048]{1,0:T(8,128)(2,1)S(1)} %get-tuple-element.74), channel_id=1, source_target_pairs={{0,8},{2,10},{4,12},{6,14},{8,0},{10,2},{12,4},{14,6},{1,9},{3,11}... | collective-permute-start | bytes 393224 | tf_op jit(solution)/shard_map/ppermute | solution.py:378
  15.6 7.8 %adjoint.5 = (bf16[32,2048]{1,0:T(8,128)(2,1)S(1)}, bf16[32,2048]{1,0:T(8,128)(2,1)S(1)}, bf16[32,2048]{1,0:T(8,128)(2,1)S(1)}, bf16[32,2048]{1,0:T(8,128)(2,1)S(1)}) custom-call(s32[1]{0:T(128)} %bitcast.1.turn_ref.turn, bf16[8,16,640]{2,1,0:T(8,128)(2,1)S(1)} %maximum_maximum_fusion.l_ref, bf16[2,8,320,4096]{3,2,1,0:T(8,128)(2,1)} %k_hbm.11), custom_call_target="tpu_custom_call" | custom-call | flops 2684354560 | bytes 20971520 | tf_op jit(solution)/shard_map/adjoint/pallas_call | solution.py:91
  33.3 7.3 %collective-permute-done.4 = bf16[32,2048]{1,0:T(8,128)(2,1)S(1)} collective-permute-done((bf16[32,2048]{1,0:T(8,128)(2,1)S(1)}, bf16[32,2048]{1,0:T(8,128)(2,1)S(1)}, u32[]{:S(2)}, u32[]{:S(2)}) %collective-permute-start.4) | collective-permute-done | bytes 131104 | tf_op jit(solution)/shard_map/ppermute | solution.py:378
  42.0 2.0 %collective-permute-start.8 = (bf16[32,2048]{1,0:T(8,128)(2,1)S(1)}, bf16[32,2048]{1,0:T(8,128)(2,1)S(1)}, u32[]{:S(2)}, u32[]{:S(2)}) collective-permute-start(bf16[32,2048]{1,0:T(8,128)(2,1)S(1)} %get-tuple-element.87), channel_id=1, source_target_pairs={{0,4},{2,6},{4,0},{6,2},{8,12},{10,14},{12,8},{14,10},{1,5},{3,7},... | collective-permute-start | bytes 393224 | tf_op jit(solution)/shard_map/ppermute | solution.py:378
  46.4 4.1 %collective-permute-done.6.refs_1_ = bf16[128,2048]{1,0:T(8,128)(2,1)S(1)} collective-permute-done((bf16[128,2048]{1,0:T(8,128)(2,1)S(1)}, bf16[128,2048]{1,0:T(8,128)(2,1)S(1)}, u32[]{:S(2)}, u32[]{:S(2)}) %collective-permute-start.6) | collective-permute-done | bytes 524320 | tf_op jit(solution)/shard_map/ppermute | solution.py:378
  51.0 4.8 %collective-permute-done.9.rest_2_.refs_3_ = bf16[32,2048]{1,0:T(8,128)(2,1)S(1)} collective-permute-done((bf16[32,2048]{1,0:T(8,128)(2,1)S(1)}, bf16[32,2048]{1,0:T(8,128)(2,1)S(1)}, u32[]{:S(2)}, u32[]{:S(2)}) %collective-permute-start.9) | collective-permute-done | bytes 131104 | tf_op jit(solution)/shard_map/ppermute | solution.py:378
  60.6 8.6 %forward.4.init_ref = f32[136,320]{1,0:T(8,128)S(1)} custom-call(s32[1]{0:T(128)} %bitcast.1.turn_ref.turn, bf16[2,8,320,4096]{3,2,1,0:T(8,128)(2,1)} %k_hbm.11, f32[8,128]{1,0:T(8,128)S(1)} %get-tuple-element.84.al, bf16[32,2048]{1,0:T(8,128)(2,1)S(1)} %get-tuple-element.91.rest_0_.refs_1_, bf16[32,2048]{1,0:T(8,128)(2,1)S(1)} %collective-permute-done.8.rest_1_.refs_2_, ...), custom_call_target="tpu_custom_call" | custom-call | flops 2684354560 | bytes 20971520 | tf_op jit(solution)/shard_map/forward/pallas_call | solution.py:177
  69.7 8.5 %forward.5.own_ref = f32[136,320]{1,0:T(8,128)S(1)} custom-call(s32[1]{0:T(128)} %bitcast.1.turn_ref.turn, bf16[2,8,320,4096]{3,2,1,0:T(8,128)(2,1)} %k_hbm.11, f32[8,128]{1,0:T(8,128)S(1)} %get-tuple-element.82.al_ref, f32[136,320]{1,0:T(8,128)S(1)} %forward.4.init_ref, bf16[32,2048]{1,0:T(8,128)(2,1)S(1)} %get-tuple-element.93.refs_0_.refs_9_, ...), custom_call_target="tpu_custom_call" | custom-call | flops 2684354560 | bytes 20971520 | tf_op jit(solution)/shard_map/forward/pallas_call | solution.py:177
  82.2 4.3 %all-to-all-start = ((f32[8,16,128]{2,1,0:T(8,128)}), f32[8,16,128]{2,1,0:T(8,128)S(1)}, u32[]{:S(2)}, u32[]{:S(2)}) async-start(f32[8,16,128]{2,1,0:T(8,128)} %bitcast.37), calls=%async_computation | async-start | bytes 131072 | tf_op jit(solution)/shard_map/all_to_all | solution.py:383
  87.2 6.2 %all-to-all-done = f32[8,16,128]{2,1,0:T(8,128)S(1)} async-done(((f32[8,16,128]{2,1,0:T(8,128)}), f32[8,16,128]{2,1,0:T(8,128)S(1)}, u32[]{:S(2)}, u32[]{:S(2)}) %all-to-all-start) | async-done | bytes 65568 | tf_op jit(solution)/shard_map/all_to_all | solution.py:383
  96.9 7.7 %adjoint.6 = (bf16[32,2048]{1,0:T(8,128)(2,1)S(1)}, bf16[32,2048]{1,0:T(8,128)(2,1)S(1)}, bf16[32,2048]{1,0:T(8,128)(2,1)S(1)}, bf16[32,2048]{1,0:T(8,128)(2,1)S(1)}) custom-call(s32[1]{0:T(128)} %bitcast.1.turn_ref.turn, bf16[8,16,640]{2,1,0:T(8,128)(2,1)S(1)} %copy-done.2, bf16[2,8,320,4096]{3,2,1,0:T(8,128)(2,1)} %k_hbm.11), custom_call_target="tpu_custom_call" | custom-call | flops 2684354560 | bytes 20971520 | tf_op jit(solution)/shard_map/adjoint/pallas_call | solution.py:91
  105.8 3.3 %collective-permute-start.16 = (bf16[32,2048]{1,0:T(8,128)(2,1)S(1)}, bf16[32,2048]{1,0:T(8,128)(2,1)S(1)}, u32[]{:S(2)}, u32[]{:S(2)}) collective-permute-start(bf16[32,2048]{1,0:T(8,128)(2,1)S(1)} %get-tuple-element.106), channel_id=1, source_target_pairs={{0,8},{2,10},{4,12},{6,14},{8,0},{10,2},{12,4},{14,6},{1,9},{3,11}... | collective-permute-start | bytes 393224 | tf_op jit(solution)/shard_map/ppermute | solution.py:378
  109.1 7.7 %adjoint.7 = (bf16[32,2048]{1,0:T(8,128)(2,1)S(1)}, bf16[32,2048]{1,0:T(8,128)(2,1)S(1)}, bf16[32,2048]{1,0:T(8,128)(2,1)S(1)}, bf16[32,2048]{1,0:T(8,128)(2,1)S(1)}) custom-call(s32[1]{0:T(128)} %bitcast.1.turn_ref.turn, bf16[8,16,640]{2,1,0:T(8,128)(2,1)S(1)} %copy-done.2, bf16[2,8,320,4096]{3,2,1,0:T(8,128)(2,1)} %k_hbm.11), custom_call_target="tpu_custom_call" | custom-call | flops 2684354560 | bytes 20971520 | tf_op jit(solution)/shard_map/adjoint/pallas_call | solution.py:91
  120.0 2.6 %collective-permute-start.20 = (bf16[32,2048]{1,0:T(8,128)(2,1)S(1)}, bf16[32,2048]{1,0:T(8,128)(2,1)S(1)}, u32[]{:S(2)}, u32[]{:S(2)}) collective-permute-start(bf16[32,2048]{1,0:T(8,128)(2,1)S(1)} %get-tuple-element.113), channel_id=1, source_target_pairs={{0,12},{2,14},{4,8},{6,10},{8,4},{10,6},{12,0},{14,2},{1,13},{3,15... | collective-permute-start | bytes 393224 | tf_op jit(solution)/shard_map/ppermute | solution.py:378
  124.3 4.9 %collective-permute-done.19 = bf16[32,2048]{1,0:T(8,128)(2,1)S(1)} collective-permute-done((bf16[32,2048]{1,0:T(8,128)(2,1)S(1)}, bf16[32,2048]{1,0:T(8,128)(2,1)S(1)}, u32[]{:S(2)}, u32[]{:S(2)}) %collective-permute-start.19) | collective-permute-done | bytes 131104 | tf_op jit(solution)/shard_map/ppermute | solution.py:378
  135.9 4.2 %collective-permute-done.21.refs_1_ = bf16[128,2048]{1,0:T(8,128)(2,1)S(1)} collective-permute-done((bf16[128,2048]{1,0:T(8,128)(2,1)S(1)}, bf16[128,2048]{1,0:T(8,128)(2,1)S(1)}, u32[]{:S(2)}, u32[]{:S(2)}) %collective-permute-start.21) | collective-permute-done | bytes 524320 | tf_op jit(solution)/shard_map/ppermute | solution.py:378
  140.6 3.7 %collective-permute-done.24.rest_2_.refs_7_ = bf16[32,2048]{1,0:T(8,128)(2,1)S(1)} collective-permute-done((bf16[32,2048]{1,0:T(8,128)(2,1)S(1)}, bf16[32,2048]{1,0:T(8,128)(2,1)S(1)}, u32[]{:S(2)}, u32[]{:S(2)}) %collective-permute-start.24) | collective-permute-done | bytes 131104 | tf_op jit(solution)/shard_map/ppermute | solution.py:378
  149.1 8.6 %forward.6.init_ref = f32[136,320]{1,0:T(8,128)S(1)} custom-call(s32[1]{0:T(128)} %bitcast.1.turn_ref.turn, bf16[2,8,320,4096]{3,2,1,0:T(8,128)(2,1)} %k_hbm.11, f32[8,128]{1,0:T(8,128)S(1)} %get-tuple-element.116.al, bf16[32,2048]{1,0:T(8,128)(2,1)S(1)} %get-tuple-element.123.rest_0_.refs_5_, bf16[32,2048]{1,0:T(8,128)(2,1)S(1)} %collective-permute-done.23.rest_1_.refs_6_, ...), custom_call_target="tpu_custom_call" | custom-call | flops 2684354560 | bytes 20971520 | tf_op jit(solution)/shard_map/forward/pallas_call | solution.py:177
  158.3 8.5 %forward.7.own_ref = f32[136,320]{1,0:T(8,128)S(1)} custom-call(s32[1]{0:T(128)} %bitcast.1.turn_ref.turn, bf16[2,8,320,4096]{3,2,1,0:T(8,128)(2,1)} %k_hbm.11, f32[8,128]{1,0:T(8,128)S(1)} %get-tuple-element.114.al_ref, f32[136,320]{1,0:T(8,128)S(1)} %forward.6.init_ref, bf16[32,2048]{1,0:T(8,128)(2,1)S(1)} %get-tuple-element.125.refs_0_.refs_13_, ...), custom_call_target="tpu_custom_call" | custom-call | flops 2684354560 | bytes 20971520 | tf_op jit(solution)/shard_map/forward/pallas_call | solution.py:177
  170.8 3.4 %all-to-all-start.1 = ((f32[8,16,128]{2,1,0:T(8,128)}), f32[8,16,128]{2,1,0:T(8,128)S(1)}, u32[]{:S(2)}, u32[]{:S(2)}) async-start(f32[8,16,128]{2,1,0:T(8,128)} %bitcast.36), calls=%async_computation.1 | async-start | bytes 131072 | tf_op jit(solution)/shard_map/all_to_all | solution.py:383
  174.2 6.8 %all-to-all-done.1 = f32[8,16,128]{2,1,0:T(8,128)S(1)} async-done(((f32[8,16,128]{2,1,0:T(8,128)}), f32[8,16,128]{2,1,0:T(8,128)S(1)}, u32[]{:S(2)}, u32[]{:S(2)}) %all-to-all-start.1) | async-done | bytes 65568 | tf_op jit(solution)/shard_map/all_to_all | solution.py:383
  182.0 3.8 %finish.1 = (f32[2,8,8,4096]{3,2,1,0:T(8,128)}, f32[2,8,8,160]{3,2,1,0:T(8,128)}) custom-call(s32[3]{0:T(128)S(1)} %pad_add_fusion.place_ref, f32[128,128]{1,0:T(8,128)S(1)} %bitcast.32, f32[128,320]{1,0:T(8,128)S(1)} %copy-done.4, f32[128,320]{1,0:T(8,128)S(1)} %copy-done.3, f32[8,128]{1,0:T(8,128)S(1)} %copy-done.5, ...), custom_call_target="tpu_custom_call" | custom-call | tf_op jit(solution)/shard_map/finish/pallas_call | solution.py:358
  (111 shorter events, 52.5 us)
Async XLA Ops:
  9.6 14.1 %collective-permute-start = (bf16[32,2048]{1,0:T(8,128)(2,1)S(1)}, bf16[32,2048]{1,0:T(8,128)(2,1)S(1)}, u32[]{:S(2)}, u32[]{:S(2)}) collective-permute-start(bf16[32,2048]{1,0:T(8,128)(2,1)S(1)} %get-tuple-element.73), channel_id=1, source_target_pairs={{0,4},{2,6},{4,0},{6,2},{8,12},{10,14},{12,8},{14,10},{1,5},{3,7},... | collective-permute-start | bytes 393224 | tf_op jit(solution)/shard_map/ppermute | solution.py:378
  12.7 12.9 %collective-permute-start.1 = (bf16[32,2048]{1,0:T(8,128)(2,1)S(1)}, bf16[32,2048]{1,0:T(8,128)(2,1)S(1)}, u32[]{:S(2)}, u32[]{:S(2)}) collective-permute-start(bf16[32,2048]{1,0:T(8,128)(2,1)S(1)} %get-tuple-element.74), channel_id=1, source_target_pairs={{0,8},{2,10},{4,12},{6,14},{8,0},{10,2},{12,4},{14,6},{1,9},{3,11}... | collective-permute-start | bytes 393224 | tf_op jit(solution)/shard_map/ppermute | solution.py:378
  15.2 10.4 %collective-permute-start.2 = (bf16[32,2048]{1,0:T(8,128)(2,1)S(1)}, bf16[32,2048]{1,0:T(8,128)(2,1)S(1)}, u32[]{:S(2)}, u32[]{:S(2)}) collective-permute-start(bf16[32,2048]{1,0:T(8,128)(2,1)S(1)} %get-tuple-element.69), channel_id=1, source_target_pairs={{0,12},{2,14},{4,8},{6,10},{8,4},{10,6},{12,0},{14,2},{1,13},{3,15... | collective-permute-start | bytes 393224 | tf_op jit(solution)/shard_map/ppermute | solution.py:378
  25.6 15.9 %collective-permute-start.7 = (bf16[128,2048]{1,0:T(8,128)(2,1)S(1)}, bf16[128,2048]{1,0:T(8,128)(2,1)S(1)}, u32[]{:S(2)}, u32[]{:S(2)}) collective-permute-start(bf16[128,2048]{1,0:T(8,128)(2,1)S(1)} %constant_dynamic-update-slice_fusion.refs_0_), channel_id=1, source_target_pairs={{0,2},{2,0},{4,6},{6,4},{8,10},{10,8},{12,14},{14,12},{1,3},{3,1},... | collective-permute-start | bytes 1572872 | tf_op jit(solution)/shard_map/ppermute | solution.py:378
  29.2 11.5 %collective-permute-start.4 = (bf16[32,2048]{1,0:T(8,128)(2,1)S(1)}, bf16[32,2048]{1,0:T(8,128)(2,1)S(1)}, u32[]{:S(2)}, u32[]{:S(2)}) collective-permute-start(bf16[32,2048]{1,0:T(8,128)(2,1)S(1)} %get-tuple-element.79), channel_id=1, source_target_pairs={{0,8},{2,10},{4,12},{6,14},{8,0},{10,2},{12,4},{14,6},{1,9},{3,11}... | collective-permute-start | bytes 393224 | tf_op jit(solution)/shard_map/ppermute | solution.py:378
  30.2 10.5 %collective-permute-start.5 = (bf16[32,2048]{1,0:T(8,128)(2,1)S(1)}, bf16[32,2048]{1,0:T(8,128)(2,1)S(1)}, u32[]{:S(2)}, u32[]{:S(2)}) collective-permute-start(bf16[32,2048]{1,0:T(8,128)(2,1)S(1)} %get-tuple-element.81), channel_id=1, source_target_pairs={{0,12},{2,14},{4,8},{6,10},{8,4},{10,6},{12,0},{14,2},{1,13},{3,15... | collective-permute-start | bytes 393224 | tf_op jit(solution)/shard_map/ppermute | solution.py:378
  40.7 9.8 %collective-permute-start.6 = (bf16[128,2048]{1,0:T(8,128)(2,1)S(1)}, bf16[128,2048]{1,0:T(8,128)(2,1)S(1)}, u32[]{:S(2)}, u32[]{:S(2)}) collective-permute-start(bf16[128,2048]{1,0:T(8,128)(2,1)S(1)} %constant_dynamic-update-slice_fusion.4.refs_0_), channel_id=1, source_target_pairs={{0,2},{2,0},{4,6},{6,4},{8,10},{10,8},{12,14},{14,12},{1,3},{3,1},... | collective-permute-start | bytes 1572872 | tf_op jit(solution)/shard_map/ppermute | solution.py:378
  44.0 11.8 %collective-permute-start.9 = (bf16[32,2048]{1,0:T(8,128)(2,1)S(1)}, bf16[32,2048]{1,0:T(8,128)(2,1)S(1)}, u32[]{:S(2)}, u32[]{:S(2)}) collective-permute-start(bf16[32,2048]{1,0:T(8,128)(2,1)S(1)} %get-tuple-element.88), channel_id=1, source_target_pairs={{0,8},{2,10},{4,12},{6,14},{8,0},{10,2},{12,4},{14,6},{1,9},{3,11}... | collective-permute-start | bytes 393224 | tf_op jit(solution)/shard_map/ppermute | solution.py:378
  45.0 10.8 %collective-permute-start.10 = (bf16[32,2048]{1,0:T(8,128)(2,1)S(1)}, bf16[32,2048]{1,0:T(8,128)(2,1)S(1)}, u32[]{:S(2)}, u32[]{:S(2)}) collective-permute-start(bf16[32,2048]{1,0:T(8,128)(2,1)S(1)} %get-tuple-element.89), channel_id=1, source_target_pairs={{0,12},{2,14},{4,8},{6,10},{8,4},{10,6},{12,0},{14,2},{1,13},{3,15... | collective-permute-start | bytes 393224 | tf_op jit(solution)/shard_map/ppermute | solution.py:378
  55.7 13.4 %collective-permute-start.13 = (bf16[32,2048]{1,0:T(8,128)(2,1)S(1)}, bf16[32,2048]{1,0:T(8,128)(2,1)S(1)}, u32[]{:S(2)}, u32[]{:S(2)}) collective-permute-start(bf16[32,2048]{1,0:T(8,128)(2,1)S(1)} %get-tuple-element.90), channel_id=1, source_target_pairs={{0,12},{2,14},{4,8},{6,10},{8,4},{10,6},{12,0},{14,2},{1,13},{3,15... | collective-permute-start | bytes 393224 | tf_op jit(solution)/shard_map/ppermute | solution.py:378
  57.6 11.6 %collective-permute-start.11 = (bf16[32,2048]{1,0:T(8,128)(2,1)S(1)}, bf16[32,2048]{1,0:T(8,128)(2,1)S(1)}, u32[]{:S(2)}, u32[]{:S(2)}) collective-permute-start(bf16[32,2048]{1,0:T(8,128)(2,1)S(1)} %get-tuple-element.95), channel_id=1, source_target_pairs={{0,4},{2,6},{4,0},{6,2},{8,12},{10,14},{12,8},{14,10},{1,5},{3,7},... | collective-permute-start | bytes 393224 | tf_op jit(solution)/shard_map/ppermute | solution.py:378
  59.3 10.5 %collective-permute-start.12 = (bf16[32,2048]{1,0:T(8,128)(2,1)S(1)}, bf16[32,2048]{1,0:T(8,128)(2,1)S(1)}, u32[]{:S(2)}, u32[]{:S(2)}) collective-permute-start(bf16[32,2048]{1,0:T(8,128)(2,1)S(1)} %get-tuple-element.97), channel_id=1, source_target_pairs={{0,8},{2,10},{4,12},{6,14},{8,0},{10,2},{12,4},{14,6},{1,9},{3,11}... | collective-permute-start | bytes 393224 | tf_op jit(solution)/shard_map/ppermute | solution.py:378
  82.2 11.2 %all-to-all-start = ((f32[8,16,128]{2,1,0:T(8,128)}), f32[8,16,128]{2,1,0:T(8,128)S(1)}, u32[]{:S(2)}, u32[]{:S(2)}) async-start(f32[8,16,128]{2,1,0:T(8,128)} %bitcast.37), calls=%async_computation | async-start | bytes 131072 | tf_op jit(solution)/shard_map/all_to_all | solution.py:383
  104.6 13.0 %collective-permute-start.17 = (bf16[32,2048]{1,0:T(8,128)(2,1)S(1)}, bf16[32,2048]{1,0:T(8,128)(2,1)S(1)}, u32[]{:S(2)}, u32[]{:S(2)}) collective-permute-start(bf16[32,2048]{1,0:T(8,128)(2,1)S(1)} %get-tuple-element.101), channel_id=1, source_target_pairs={{0,12},{2,14},{4,8},{6,10},{8,4},{10,6},{12,0},{14,2},{1,13},{3,15... | collective-permute-start | bytes 393224 | tf_op jit(solution)/shard_map/ppermute | solution.py:378
  105.3 11.6 %collective-permute-start.15 = (bf16[32,2048]{1,0:T(8,128)(2,1)S(1)}, bf16[32,2048]{1,0:T(8,128)(2,1)S(1)}, u32[]{:S(2)}, u32[]{:S(2)}) collective-permute-start(bf16[32,2048]{1,0:T(8,128)(2,1)S(1)} %get-tuple-element.105), channel_id=1, source_target_pairs={{0,4},{2,6},{4,0},{6,2},{8,12},{10,14},{12,8},{14,10},{1,5},{3,7},... | collective-permute-start | bytes 393224 | tf_op jit(solution)/shard_map/ppermute | solution.py:378
  105.8 11.9 %collective-permute-start.16 = (bf16[32,2048]{1,0:T(8,128)(2,1)S(1)}, bf16[32,2048]{1,0:T(8,128)(2,1)S(1)}, u32[]{:S(2)}, u32[]{:S(2)}) collective-permute-start(bf16[32,2048]{1,0:T(8,128)(2,1)S(1)} %get-tuple-element.106), channel_id=1, source_target_pairs={{0,8},{2,10},{4,12},{6,14},{8,0},{10,2},{12,4},{14,6},{1,9},{3,11}... | collective-permute-start | bytes 393224 | tf_op jit(solution)/shard_map/ppermute | solution.py:378
  117.7 13.3 %collective-permute-start.22 = (bf16[128,2048]{1,0:T(8,128)(2,1)S(1)}, bf16[128,2048]{1,0:T(8,128)(2,1)S(1)}, u32[]{:S(2)}, u32[]{:S(2)}) collective-permute-start(bf16[128,2048]{1,0:T(8,128)(2,1)S(1)} %constant_dynamic-update-slice_fusion.8.refs_0_), channel_id=1, source_target_pairs={{0,2},{2,0},{4,6},{6,4},{8,10},{10,8},{12,14},{14,12},{1,3},{3,1},... | collective-permute-start | bytes 1572872 | tf_op jit(solution)/shard_map/ppermute | solution.py:378
  118.2 11.1 %collective-permute-start.19 = (bf16[32,2048]{1,0:T(8,128)(2,1)S(1)}, bf16[32,2048]{1,0:T(8,128)(2,1)S(1)}, u32[]{:S(2)}, u32[]{:S(2)}) collective-permute-start(bf16[32,2048]{1,0:T(8,128)(2,1)S(1)} %get-tuple-element.111), channel_id=1, source_target_pairs={{0,8},{2,10},{4,12},{6,14},{8,0},{10,2},{12,4},{14,6},{1,9},{3,11}... | collective-permute-start | bytes 393224 | tf_op jit(solution)/shard_map/ppermute | solution.py:378
  129.3 10.9 %collective-permute-start.21 = (bf16[128,2048]{1,0:T(8,128)(2,1)S(1)}, bf16[128,2048]{1,0:T(8,128)(2,1)S(1)}, u32[]{:S(2)}, u32[]{:S(2)}) collective-permute-start(bf16[128,2048]{1,0:T(8,128)(2,1)S(1)} %constant_dynamic-update-slice_fusion.12.refs_0_), channel_id=1, source_target_pairs={{0,2},{2,0},{4,6},{6,4},{8,10},{10,8},{12,14},{14,12},{1,3},{3,1},... | collective-permute-start | bytes 1572872 | tf_op jit(solution)/shard_map/ppermute | solution.py:378
  133.4 10.8 %collective-permute-start.24 = (bf16[32,2048]{1,0:T(8,128)(2,1)S(1)}, bf16[32,2048]{1,0:T(8,128)(2,1)S(1)}, u32[]{:S(2)}, u32[]{:S(2)}) collective-permute-start(bf16[32,2048]{1,0:T(8,128)(2,1)S(1)} %get-tuple-element.120), channel_id=1, source_target_pairs={{0,8},{2,10},{4,12},{6,14},{8,0},{10,2},{12,4},{14,6},{1,9},{3,11}... | collective-permute-start | bytes 393224 | tf_op jit(solution)/shard_map/ppermute | solution.py:378
  144.3 13.4 %collective-permute-start.28 = (bf16[32,2048]{1,0:T(8,128)(2,1)S(1)}, bf16[32,2048]{1,0:T(8,128)(2,1)S(1)}, u32[]{:S(2)}, u32[]{:S(2)}) collective-permute-start(bf16[32,2048]{1,0:T(8,128)(2,1)S(1)} %get-tuple-element.122), channel_id=1, source_target_pairs={{0,12},{2,14},{4,8},{6,10},{8,4},{10,6},{12,0},{14,2},{1,13},{3,15... | collective-permute-start | bytes 393224 | tf_op jit(solution)/shard_map/ppermute | solution.py:378
  146.1 11.6 %collective-permute-start.26 = (bf16[32,2048]{1,0:T(8,128)(2,1)S(1)}, bf16[32,2048]{1,0:T(8,128)(2,1)S(1)}, u32[]{:S(2)}, u32[]{:S(2)}) collective-permute-start(bf16[32,2048]{1,0:T(8,128)(2,1)S(1)} %get-tuple-element.127), channel_id=1, source_target_pairs={{0,4},{2,6},{4,0},{6,2},{8,12},{10,14},{12,8},{14,10},{1,5},{3,7},... | collective-permute-start | bytes 393224 | tf_op jit(solution)/shard_map/ppermute | solution.py:378
  147.8 10.5 %collective-permute-start.27 = (bf16[32,2048]{1,0:T(8,128)(2,1)S(1)}, bf16[32,2048]{1,0:T(8,128)(2,1)S(1)}, u32[]{:S(2)}, u32[]{:S(2)}) collective-permute-start(bf16[32,2048]{1,0:T(8,128)(2,1)S(1)} %get-tuple-element.129), channel_id=1, source_target_pairs={{0,8},{2,10},{4,12},{6,14},{8,0},{10,2},{12,4},{14,6},{1,9},{3,11}... | collective-permute-start | bytes 393224 | tf_op jit(solution)/shard_map/ppermute | solution.py:378
  170.8 10.3 %all-to-all-start.1 = ((f32[8,16,128]{2,1,0:T(8,128)}), f32[8,16,128]{2,1,0:T(8,128)S(1)}, u32[]{:S(2)}, u32[]{:S(2)}) async-start(f32[8,16,128]{2,1,0:T(8,128)} %bitcast.36), calls=%async_computation.1 | async-start | bytes 131072 | tf_op jit(solution)/shard_map/all_to_all | solution.py:383
  (21 other events, 193.2 us)

commit v4 on v3

--- a/solution.py
+++ b/solution.py
@@ -31,7 +31,7 @@
     return max(t for t in range(LANES, min(limit, width) + 1, LANES) if width % t == 0)
 
 
-def stream(k_hbm, kbuf, sem, base, steps, step):
+def stream(k_hbm, kbuf, sem, base, steps, step, first=lambda: None):
     depth, _, group, _, ts = kbuf.shape
     groups = k_hbm.shape[1] // group
     total = steps * groups
@@ -44,6 +44,7 @@
 
     for i in range(min(depth - 1, total)):
         copy(i).start()
+    first()
 
     def body(i, carry):
         @pl.when(i + depth - 1 < total)
@@ -57,12 +58,32 @@
     lax.fori_loop(0, total, body, 0)
 
 
-def adjoint_body(turn_ref, l_ref, k_hbm, *refs, points, base, steps):
-    *o_refs, kbuf, sem, scr = refs
+def adjoint_body(turn_ref, k_hbm, *refs, pieces, points, base, steps, stage):
+    ins, refs = refs[: STAGES[stage]], refs[STAGES[stage] :]
+    o_refs, refs = refs[:pieces], refs[pieces:]
+    made, (kbuf, sem, scr) = refs[:-3], refs[-3:]
     _, _, _, receivers, ts = kbuf.shape
     fl = k_hbm.shape[1]
-    size = 2 * points * fl // len(o_refs)
+    size = 2 * points * fl // pieces
     turn = turn_ref[0]
+    l_ref = made[0] if made else ins[0]
+
+    def first():
+        if stage == "rest":
+            return
+        if stage == "step":
+            length = step_length(ins[1])
+            made[2][...] = jnp.broadcast_to(length, made[2].shape)
+        for f in range(fl):
+            real, imag = ins[0][0, f], ins[0][1, f]
+            if stage == "step":
+                top = 2 * points * f
+                real = real - length * ins[2][top : top + points]
+                imag = imag - length * ins[2][top + points : top + 2 * points]
+                made[1][0, f] = real
+                made[1][1, f] = imag
+            l_ref[f, :, :receivers] = jnp.concatenate([real, imag], 0).astype(BF16)
+            l_ref[f, :, receivers:] = jnp.concatenate([imag, -real], 0).astype(BF16)
 
     def step(s, f, block):
         out = jnp.dot(l_ref[f], block[...].reshape(2 * receivers, ts), preferred_element_type=F32)
@@ -80,19 +101,29 @@
                     at = pl.ds(pl.multiple_of(s * ts + j * LANES, LANES), LANES)
                     o_ref[:, at] = scr[j, rows, :].astype(BF16)
 
-    stream(k_hbm, kbuf, sem, base, steps, step)
-
-
-def adjoint(turn, kernel, rows, base, width, pieces):
+    stream(k_hbm, kbuf, sem, base, steps, step, first)
+
+
+STAGES = {"data": 1, "step": 3, "rest": 1}
+
+
+def adjoint(turn, kernel, ins, stage, points, base, width, pieces):
     _, fl, receivers, sources = kernel.shape
-    points = rows.shape[1] // 2
     ts = tile_of(width, ADJOINT_TILE)
     depth = min(ADJOINT_DEPTH, width // ts * fl)
-    return pl.pallas_call(
-        functools.partial(adjoint_body, points=points, base=base, steps=width // ts),
-        in_specs=[pl.BlockSpec(memory_space=pltpu.SMEM), in_vmem(), pl.BlockSpec(memory_space=pl.ANY)],
-        out_specs=[in_vmem()] * pieces,
-        out_shape=[jax.ShapeDtypeStruct((2 * points * fl // pieces, width), BF16)] * pieces,
+    shapes = [jax.ShapeDtypeStruct((2 * points * fl // pieces, width), BF16)] * pieces
+    if stage != "rest":
+        shapes.append(jax.ShapeDtypeStruct((fl, 2 * points, 2 * receivers), BF16))
+    if stage == "step":
+        shapes.append(jax.ShapeDtypeStruct((2, fl, points, receivers), F32))
+        shapes.append(jax.ShapeDtypeStruct((8, LANES), F32))
+    out = pl.pallas_call(
+        functools.partial(
+            adjoint_body, pieces=pieces, points=points, base=base, steps=width // ts, stage=stage
+        ),
+        in_specs=[pl.BlockSpec(memory_space=pltpu.SMEM), pl.BlockSpec(memory_space=pl.ANY)] + [in_vmem()] * len(ins),
+        out_specs=[in_vmem()] * len(shapes),
+        out_shape=shapes,
         scratch_shapes=[
             pltpu.VMEM((depth, 2, 1, receivers, ts), BF16),
             pltpu.SemaphoreType.DMA((depth,)),
@@ -103,7 +134,8 @@
             flops=64 * points * receivers * width * fl, bytes_accessed=4 * fl * receivers * width, transcendentals=0
         ),
         name="adjoint",
-    )(turn, rows, kernel)
+    )(turn, kernel, *ins)
+    return out[:pieces], out[pieces:]
 
 
 def forward_body(turn_ref, k_hbm, al_ref, init_ref, *refs, pieces, points, base, steps):
@@ -265,34 +297,6 @@
     )(own, got)
 
 
-def step_body(p_ref, r_ref, s_ref, a_ref, new_ref, l_ref, *, fl, points):
-    receivers = p_ref.shape[1]
-    length = step_length(s_ref)
-    a_ref[...] = jnp.broadcast_to(length, a_ref.shape)
-    new = r_ref[...] - length * p_ref[...]
-    new_ref[...] = new
-    for f in range(fl):
-        block = new[2 * points * f : 2 * points * (f + 1)]
-        real, imag = block[:points], block[points:]
-        l_ref[f, :, :receivers] = block.astype(BF16)
-        l_ref[f, :, receivers:] = jnp.concatenate([imag, -real], 0).astype(BF16)
-
-
-def advance(projected, residual, sums, fl, points):
-    receivers = projected.shape[1]
-    return pl.pallas_call(
-        functools.partial(step_body, fl=fl, points=points),
-        in_specs=[in_vmem()] * 3,
-        out_specs=[in_vmem()] * 3,
-        out_shape=[
-            jax.ShapeDtypeStruct((8, LANES), F32),
-            jax.ShapeDtypeStruct(projected.shape, F32),
-            jax.ShapeDtypeStruct((fl, 2 * points, 2 * receivers), BF16),
-        ],
-        name="step",
-    )(projected, residual, sums)
-
-
 def wave_table(freqs, fl):
     samples = np.arange(NT)[:, None]
     phase = (samples * np.arange(freqs)[None, :] % NT) * (2.0 * math.pi / NT)
@@ -339,14 +343,14 @@
         )
         copies[-1].start()
         at += ITERS * count
-    residual = r_ref[...] - lengths[-1] * p_ref[...]
-    mine = residual[:, :share]
-    for n in range(1, residual.shape[1] // share):
-        mine = jnp.where(place_ref[0] == n, residual[:, n * share : (n + 1) * share], mine)
     for c in range(2):
         for f in range(fl):
             top = (2 * f + c) * points
-            out_ref[c, f] = mine[top : top + points]
+            residual = r_ref[c, f] - lengths[-1] * p_ref[top : top + points]
+            mine = residual[:, :share]
+            for n in range(1, residual.shape[1] // share):
+                mine = jnp.where(place_ref[0] == n, residual[:, n * share : (n + 1) * share], mine)
+            out_ref[c, f] = mine
     for copy in copies:
         copy.wait()
 
@@ -451,18 +455,24 @@
         field = jnp.stack([d.reshape(count, rows, width) for d, _ in done], 1).reshape(-1, width)
         return [field], sum(a for _, a in done)
 
-    residual = data.transpose(1, 0, 3, 2).reshape(2 * fl * points, receivers)
-    real, imag = jnp.split(residual.reshape(fl, 2 * points, receivers).astype(BF16), 2, 1)
-    lhs = jnp.concatenate([jnp.concatenate([real, imag], 1), jnp.concatenate([imag, -real], 1)], 2)
+    residual = data.transpose(0, 1, 3, 2)
     lengths, fields = [], []
     for iteration in range(ITERS):
         image = None
         fields.append([])
         gradients, gathered, sent = [], [], []
-        after = lhs
+        if iteration == 0:
+            stage, ins = "data", [residual]
+        else:
+            stage, ins = "step", [residual, sums, projected]
         for base, width, mode in parts:
-            gradient = adjoint(turn_of(mode), kernel, after, base, width, pieces_of(mode))
-            after = then(lhs, gradient[-1])
+            gradient, made = adjoint(turn_of(mode), kernel, ins, stage, points, base, width, pieces_of(mode))
+            if stage == "step":
+                residual = made[1]
+                lengths.append(made[2])
+            if made:
+                lhs = made[0]
+            stage, ins = "rest", [then(lhs, gradient[-1])]
             gradients.append(gradient)
             if gathered and mode == "relay":
                 gradient = [then(x, gathered[-1][0]) for x in gradient]
@@ -473,7 +483,7 @@
                 got = [then(got[0], gradients[n + 1][-1])] + got[1:]
             field, alignment = tapered(got, mode)
             if sent and mode == "relay":
-                field = [then(x, *sent[-1][1][1:]) for x in field]
+                field = [then(x, sent[-1][1][len(field) // 2]) for x in field]
             sent.append((field, scatter(field, mode), alignment))
         for n, (base, _, mode) in enumerate(parts):
             _, field, alignment = sent[n]
@@ -484,9 +494,6 @@
         got = swap(image) if src_count == 2 else lax.psum(image, "src") - image
         projected, sums = merge(image, got, count)
         sums = exchange(sums, 16)
-        if iteration + 1 < ITERS:
-            length, residual, lhs = advance(projected, residual, sums, fl, points)
-            lengths.append(length)
     spans = [(base, width) for base, width, _ in parts]
     turns = [turn_of(mode) for _, _, mode in parts]
     core = lax.axis_index("src").reshape(1).astype(jnp.int32)

time: 186 us -> 180 us (0.968)
  blocking collectives: 0 us -> 11.2 us
  waiting for transfers between devices: 52.2 us -> 43.5 us
  starting transfers between devices: 49.6 us -> 44.7 us
    all_to_all x0 -> x1, blocking collectives: none -> 11.2 us  [exchange(): lax.all_to_all(x.reshape(-1, rows, width), 'freq', 0, 0, tiled=True)]
    all_to_all x2 -> x1, waiting for transfers between devices: 13 us -> 6.83 us  [exchange(): lax.all_to_all(x.reshape(-1, rows, width), 'freq', 0, 0, tiled=True)]
    all_to_all x2 -> x1, starting transfers between devices: 7.63 us -> 3.58 us  [exchange(): lax.all_to_all(x.reshape(-1, rows, width), 'freq', 0, 0, tiled=True)]
    ppermute x28, waiting for transfers between devices: 36.2 us -> 33.8 us  [send(): lax.ppermute(x, 'freq', [(i, i ^ hop) for i in range(lax.axis_size('freq'...]
    pallas_call x5 -> x4, Pallas kernels: 33 us -> 31.1 us  [adjoint(): pl.pallas_call(functools.partial(adjoint_body, pieces=pieces, points=poin...]
    unnamed x38 -> x34, local copies, waits for them, and re-layouts: 3.98 us -> 4.28 us
  transfers between devices with their start and end apart: 32 -> 31, of which waited for: 16 -> 14; matrix products, arithmetic and copies ran while one was open for 1% -> 1% of each run, Pallas kernels for 19% -> 19%
where the time goes in v4:
time: 180 us
  Pallas kernels  74.4 us (41%)
  starting transfers between devices  44.7 us (25%)
  waiting for transfers between devices  43.5 us (24%)
  blocking collectives  11.2 us (6%)
  local copies, waits for them, and re-layouts  4.76 us (3%)
    ppermute x28, starting transfers between devices, send(): lax.ppermute(x, 'freq', [(i, i ^ hop) for i in range(lax.axis_size('freq'...  41 us
    pallas_call x4, Pallas kernels, forward(): pl.pallas_call(body, in_specs=specs + [in_vmem()] * (len(start) + pieces)...  34.1 us
    ppermute x28, waiting for transfers between devices, send(): lax.ppermute(x, 'freq', [(i, i ^ hop) for i in range(lax.axis_size('freq'...  33.8 us
    pallas_call x4, Pallas kernels, adjoint(): pl.pallas_call(functools.partial(adjoint_body, pieces=pieces, points=poin...  31.1 us
    all_to_all x1, blocking collectives, exchange(): lax.all_to_all(x.reshape(-1, rows, width), 'freq', 0, 0, tiled=True)  11.2 us
    all_to_all x1, waiting for transfers between devices, exchange(): lax.all_to_all(x.reshape(-1, rows, width), 'freq', 0, 0, tiled=True)  6.83 us
    unnamed x34, local copies, waits for them, and re-layouts  4.28 us
    pallas_call x1, Pallas kernels, finish(): pl.pallas_call(functools.partial(finish_body, spans=spans, pieces=[len(fi...  3.83 us
  transfers between devices with their start and end apart: 31, of which 14 were waited for; matrix products, arithmetic and copies ran while one was open for 1% of the time, Pallas kernels for 19%

profile of v4, /device:TPU:0, one launch (start us, length us, event | category | flops | bytes accessed | tf_op | source)
XLA Modules:
  0.0 180.1 jit_solution(2732202667288816800)
XLA Ops:
  1.6 7.8 %adjoint.4 = (bf16[32,2048]{1,0:T(8,128)(2,1)S(1)}, bf16[32,2048]{1,0:T(8,128)(2,1)S(1)}, bf16[32,2048]{1,0:T(8,128)(2,1)S(1)}, bf16[32,2048]{1,0:T(8,128)(2,1)S(1)}, bf16[8,16,640]{2,1,0:T(8,128)(2,1)S(1)}) custom-call(s32[1]{0:T(128)} %bitcast.1.turn_ref.turn, bf16[2,8,320,4096]{3,2,1,0:T(8,128)(2,1)} %k_hbm.11, f32[2,8,8,320]{3,2,1,0:T(8,128)S(1)} %bitcast.27), custom_call_target="tpu_custom_call" | custom-call | flops 2684354560 | bytes 20971520 | tf_op jit(solution)/shard_map/adjoint/pallas_call | solution.py:120
  9.4 3.1 %collective-permute-start = (bf16[32,2048]{1,0:T(8,128)(2,1)S(1)}, bf16[32,2048]{1,0:T(8,128)(2,1)S(1)}, u32[]{:S(2)}, u32[]{:S(2)}) collective-permute-start(bf16[32,2048]{1,0:T(8,128)(2,1)S(1)} %get-tuple-element.75), channel_id=1, source_target_pairs={{0,4},{2,6},{4,0},{6,2},{8,12},{10,14},{12,8},{14,10},{1,5},{3,7},... | collective-permute-start | bytes 393224 | tf_op jit(solution)/shard_map/ppermute | solution.py:382
  12.5 2.6 %collective-permute-start.1 = (bf16[32,2048]{1,0:T(8,128)(2,1)S(1)}, bf16[32,2048]{1,0:T(8,128)(2,1)S(1)}, u32[]{:S(2)}, u32[]{:S(2)}) collective-permute-start(bf16[32,2048]{1,0:T(8,128)(2,1)S(1)} %get-tuple-element.76), channel_id=1, source_target_pairs={{0,8},{2,10},{4,12},{6,14},{8,0},{10,2},{12,4},{14,6},{1,9},{3,11}... | collective-permute-start | bytes 393224 | tf_op jit(solution)/shard_map/ppermute | solution.py:382
  15.5 7.8 %adjoint.5 = (bf16[32,2048]{1,0:T(8,128)(2,1)S(1)}, bf16[32,2048]{1,0:T(8,128)(2,1)S(1)}, bf16[32,2048]{1,0:T(8,128)(2,1)S(1)}, bf16[32,2048]{1,0:T(8,128)(2,1)S(1)}) custom-call(s32[1]{0:T(128)} %bitcast.1.turn_ref.turn, bf16[2,8,320,4096]{3,2,1,0:T(8,128)(2,1)} %k_hbm.11, bf16[8,16,640]{2,1,0:T(8,128)(2,1)S(1)} %get-tuple-element.72.refs_0_), custom_call_target="tpu_custom_call" | custom-call | flops 2684354560 | bytes 20971520 | tf_op jit(solution)/shard_map/adjoint/pallas_call | solution.py:120
  33.2 7.3 %collective-permute-done.4 = bf16[32,2048]{1,0:T(8,128)(2,1)S(1)} collective-permute-done((bf16[32,2048]{1,0:T(8,128)(2,1)S(1)}, bf16[32,2048]{1,0:T(8,128)(2,1)S(1)}, u32[]{:S(2)}, u32[]{:S(2)}) %collective-permute-start.4) | collective-permute-done | bytes 131104 | tf_op jit(solution)/shard_map/ppermute | solution.py:382
  41.8 2.9 %collective-permute-start.8 = (bf16[32,2048]{1,0:T(8,128)(2,1)S(1)}, bf16[32,2048]{1,0:T(8,128)(2,1)S(1)}, u32[]{:S(2)}, u32[]{:S(2)}) collective-permute-start(bf16[32,2048]{1,0:T(8,128)(2,1)S(1)} %get-tuple-element.89), channel_id=1, source_target_pairs={{0,8},{2,10},{4,12},{6,14},{8,0},{10,2},{12,4},{14,6},{1,9},{3,11}... | collective-permute-start | bytes 393224 | tf_op jit(solution)/shard_map/ppermute | solution.py:382
  46.3 4.1 %collective-permute-done.6.refs_1_ = bf16[128,2048]{1,0:T(8,128)(2,1)S(1)} collective-permute-done((bf16[128,2048]{1,0:T(8,128)(2,1)S(1)}, bf16[128,2048]{1,0:T(8,128)(2,1)S(1)}, u32[]{:S(2)}, u32[]{:S(2)}) %collective-permute-start.6) | collective-permute-done | bytes 524320 | tf_op jit(solution)/shard_map/ppermute | solution.py:382
  50.8 2.8 %collective-permute-done.8.rest_2_.refs_3_ = bf16[32,2048]{1,0:T(8,128)(2,1)S(1)} collective-permute-done((bf16[32,2048]{1,0:T(8,128)(2,1)S(1)}, bf16[32,2048]{1,0:T(8,128)(2,1)S(1)}, u32[]{:S(2)}, u32[]{:S(2)}) %collective-permute-start.8) | collective-permute-done | bytes 131104 | tf_op jit(solution)/shard_map/ppermute | solution.py:382
  58.0 8.6 %forward.4.init_ref = f32[136,320]{1,0:T(8,128)S(1)} custom-call(s32[1]{0:T(128)} %bitcast.1.turn_ref.turn, bf16[2,8,320,4096]{3,2,1,0:T(8,128)(2,1)} %k_hbm.11, f32[8,128]{1,0:T(8,128)S(1)} %get-tuple-element.86.al, bf16[32,2048]{1,0:T(8,128)(2,1)S(1)} %get-tuple-element.91.rest_0_.refs_1_, bf16[32,2048]{1,0:T(8,128)(2,1)S(1)} %collective-permute-done.9.rest_1_.refs_2_, ...), custom_call_target="tpu_custom_call" | custom-call | flops 2684354560 | bytes 20971520 | tf_op jit(solution)/shard_map/forward/pallas_call | solution.py:209
  67.1 8.5 %forward.5.own_ref = f32[136,320]{1,0:T(8,128)S(1)} custom-call(s32[1]{0:T(128)} %bitcast.1.turn_ref.turn, bf16[2,8,320,4096]{3,2,1,0:T(8,128)(2,1)} %k_hbm.11, f32[8,128]{1,0:T(8,128)S(1)} %get-tuple-element.84.al_ref, f32[136,320]{1,0:T(8,128)S(1)} %forward.4.init_ref, bf16[32,2048]{1,0:T(8,128)(2,1)S(1)} %get-tuple-element.95.refs_0_.refs_9_, ...), custom_call_target="tpu_custom_call" | custom-call | flops 2684354560 | bytes 20971520 | tf_op jit(solution)/shard_map/forward/pallas_call | solution.py:209
  79.6 11.2 %all_to_all.10 = f32[8,16,128]{2,1,0:T(8,128)S(1)} all-to-all(f32[8,16,128]{2,1,0:T(8,128)} %bitcast.32), channel_id=1, replica_groups=mesh['grp'=2,'freq'=8,'src'=2] {'freq'}, dimensions={0} | all-to-all | bytes 131072 | tf_op jit(solution)/shard_map/all_to_all | solution.py:387
  91.8 7.8 %adjoint.6 = (bf16[32,2048]{1,0:T(8,128)(2,1)S(1)}, bf16[32,2048]{1,0:T(8,128)(2,1)S(1)}, bf16[32,2048]{1,0:T(8,128)(2,1)S(1)}, bf16[32,2048]{1,0:T(8,128)(2,1)S...) custom-call(s32[1]{0:T(128)} %bitcast.1.turn_ref.turn, ...), custom_call_target="tpu_custom_call" | custom-call | flops 2684354560 | bytes 20971520 | tf_op jit(solution)/shard_map/adjoint/pallas_call | solution.py:120
  100.7 3.3 %collective-permute-start.16 = (bf16[32,2048]{1,0:T(8,128)(2,1)S(1)}, bf16[32,2048]{1,0:T(8,128)(2,1)S(1)}, u32[]{:S(2)}, u32[]{:S(2)}) collective-permute-start(bf16[32,2048]{1,0:T(8,128)(2,1)S(1)} %get-tuple-element.108), channel_id=1, source_target_pairs={{0,8},{2,10},{4,12},{6,14},{8,0},{10,2},{12,4},{14,6},{1,9},{3,11}... | collective-permute-start | bytes 393224 | tf_op jit(solution)/shard_map/ppermute | solution.py:382
  104.0 7.7 %adjoint.7 = (bf16[32,2048]{1,0:T(8,128)(2,1)S(1)}, bf16[32,2048]{1,0:T(8,128)(2,1)S(1)}, bf16[32,2048]{1,0:T(8,128)(2,1)S(1)}, bf16[32,2048]{1,0:T(8,128)(2,1)S(1)}) custom-call(s32[1]{0:T(128)} %bitcast.1.turn_ref.turn, bf16[2,8,320,4096]{3,2,1,0:T(8,128)(2,1)} %k_hbm.11, bf16[8,16,640]{2,1,0:T(8,128)(2,1)S(1)} %get-tuple-element.104.refs_0_), custom_call_target="tpu_custom_call" | custom-call | flops 2684354560 | bytes 20971520 | tf_op jit(solution)/shard_map/adjoint/pallas_call | solution.py:120
  119.2 4.9 %collective-permute-done.19 = bf16[32,2048]{1,0:T(8,128)(2,1)S(1)} collective-permute-done((bf16[32,2048]{1,0:T(8,128)(2,1)S(1)}, bf16[32,2048]{1,0:T(8,128)(2,1)S(1)}, u32[]{:S(2)}, u32[]{:S(2)}) %collective-permute-start.19) | collective-permute-done | bytes 131104 | tf_op jit(solution)/shard_map/ppermute | solution.py:382
  126.4 3.0 %collective-permute-start.23 = (bf16[32,2048]{1,0:T(8,128)(2,1)S(1)}, bf16[32,2048]{1,0:T(8,128)(2,1)S(1)}, u32[]{:S(2)}, u32[]{:S(2)}) collective-permute-start(bf16[32,2048]{1,0:T(8,128)(2,1)S(1)} %get-tuple-element.121), channel_id=1, source_target_pairs={{0,8},{2,10},{4,12},{6,14},{8,0},{10,2},{12,4},{14,6},{1,9},{3,11}... | collective-permute-start | bytes 393224 | tf_op jit(solution)/shard_map/ppermute | solution.py:382
  130.9 4.2 %collective-permute-done.21.refs_1_ = bf16[128,2048]{1,0:T(8,128)(2,1)S(1)} collective-permute-done((bf16[128,2048]{1,0:T(8,128)(2,1)S(1)}, bf16[128,2048]{1,0:T(8,128)(2,1)S(1)}, u32[]{:S(2)}, u32[]{:S(2)}) %collective-permute-start.21) | collective-permute-done | bytes 524320 | tf_op jit(solution)/shard_map/ppermute | solution.py:382
  135.5 3.9 %collective-permute-done.23.rest_2_.refs_7_ = bf16[32,2048]{1,0:T(8,128)(2,1)S(1)} collective-permute-done((bf16[32,2048]{1,0:T(8,128)(2,1)S(1)}, bf16[32,2048]{1,0:T(8,128)(2,1)S(1)}, u32[]{:S(2)}, u32[]{:S(2)}) %collective-permute-start.23) | collective-permute-done | bytes 131104 | tf_op jit(solution)/shard_map/ppermute | solution.py:382
  140.5 3.3 %collective-permute-start.27 = (bf16[32,2048]{1,0:T(8,128)(2,1)S(1)}, bf16[32,2048]{1,0:T(8,128)(2,1)S(1)}, u32[]{:S(2)}, u32[]{:S(2)}) collective-permute-start(bf16[32,2048]{1,0:T(8,128)(2,1)S(1)} %get-tuple-element.131), channel_id=1, source_target_pairs={{0,8},{2,10},{4,12},{6,14},{8,0},{10,2},{12,4},{14,6},{1,9},{3,11}... | collective-permute-start | bytes 393224 | tf_op jit(solution)/shard_map/ppermute | solution.py:382
  143.8 8.5 %forward.6.init_ref = f32[136,320]{1,0:T(8,128)S(1)} custom-call(s32[1]{0:T(128)} %bitcast.1.turn_ref.turn, bf16[2,8,320,4096]{3,2,1,0:T(8,128)(2,1)} %k_hbm.11, f32[8,128]{1,0:T(8,128)S(1)} %get-tuple-element.118.al, bf16[32,2048]{1,0:T(8,128)(2,1)S(1)} %get-tuple-element.123.rest_0_.refs_5_, bf16[32,2048]{1,0:T(8,128)(2,1)S(1)} %collective-permute-done.24.rest_1_.refs_6_, ...), custom_call_target="tpu_custom_call" | custom-call | flops 2684354560 | bytes 20971520 | tf_op jit(solution)/shard_map/forward/pallas_call | solution.py:209
  152.3 8.5 %forward.7.own_ref = f32[136,320]{1,0:T(8,128)S(1)} custom-call(s32[1]{0:T(128)} %bitcast.1.turn_ref.turn, bf16[2,8,320,4096]{3,2,1,0:T(8,128)(2,1)} %k_hbm.11, f32[8,128]{1,0:T(8,128)S(1)} %get-tuple-element.116.al_ref, f32[136,320]{1,0:T(8,128)S(1)} %forward.6.init_ref, bf16[32,2048]{1,0:T(8,128)(2,1)S(1)} %get-tuple-element.127.refs_0_.refs_13_, ...), custom_call_target="tpu_custom_call" | custom-call | flops 2684354560 | bytes 20971520 | tf_op jit(solution)/shard_map/forward/pallas_call | solution.py:209
  164.9 3.6 %all-to-all-start.1 = ((f32[8,16,128]{2,1,0:T(8,128)}), f32[8,16,128]{2,1,0:T(8,128)S(1)}, u32[]{:S(2)}, u32[]{:S(2)}) async-start(f32[8,16,128]{2,1,0:T(8,128)} %bitcast.31), calls=%async_computation.1 | async-start | bytes 131072 | tf_op jit(solution)/shard_map/all_to_all | solution.py:387
  168.5 6.8 %all-to-all-done.1 = f32[8,16,128]{2,1,0:T(8,128)S(1)} async-done(((f32[8,16,128]{2,1,0:T(8,128)}), f32[8,16,128]{2,1,0:T(8,128)S(1)}, u32[]{:S(2)}, u32[]{:S(2)}) %all-to-all-start.1) | async-done | bytes 65568 | tf_op jit(solution)/shard_map/all_to_all | solution.py:387
  176.3 3.8 %finish.1 = (f32[2,8,8,4096]{3,2,1,0:T(8,128)}, f32[2,8,8,160]{3,2,1,0:T(8,128)}) custom-call(s32[3]{0:T(128)S(1)} %pad_add_fusion.place_ref, f32[128,128]{1,0:T(8,128)S(1)} %bitcast.30, f32[128,320]{1,0:T(8,128)S(1)} %copy-done.5, f32[2,8,8,320]{3,2,1,0:T(8,128)S(1)} %get-tuple-element.134.r_ref, f32[8,128]{1,0:T(8,128)S(1)} %get-tuple-element.135.refs_0_, ...), custom_call_target="tpu_custom_call" | custom-call | tf_op jit(solution)/shard_map/finish/pallas_call | solution.py:362
  (101 shorter events, 43.0 us)
Async XLA Ops:
  9.4 14.1 %collective-permute-start = (bf16[32,2048]{1,0:T(8,128)(2,1)S(1)}, bf16[32,2048]{1,0:T(8,128)(2,1)S(1)}, u32[]{:S(2)}, u32[]{:S(2)}) collective-permute-start(bf16[32,2048]{1,0:T(8,128)(2,1)S(1)} %get-tuple-element.75), channel_id=1, source_target_pairs={{0,4},{2,6},{4,0},{6,2},{8,12},{10,14},{12,8},{14,10},{1,5},{3,7},... | collective-permute-start | bytes 393224 | tf_op jit(solution)/shard_map/ppermute | solution.py:382
  12.5 12.9 %collective-permute-start.1 = (bf16[32,2048]{1,0:T(8,128)(2,1)S(1)}, bf16[32,2048]{1,0:T(8,128)(2,1)S(1)}, u32[]{:S(2)}, u32[]{:S(2)}) collective-permute-start(bf16[32,2048]{1,0:T(8,128)(2,1)S(1)} %get-tuple-element.76), channel_id=1, source_target_pairs={{0,8},{2,10},{4,12},{6,14},{8,0},{10,2},{12,4},{14,6},{1,9},{3,11}... | collective-permute-start | bytes 393224 | tf_op jit(solution)/shard_map/ppermute | solution.py:382
  15.1 10.4 %collective-permute-start.2 = (bf16[32,2048]{1,0:T(8,128)(2,1)S(1)}, bf16[32,2048]{1,0:T(8,128)(2,1)S(1)}, u32[]{:S(2)}, u32[]{:S(2)}) collective-permute-start(bf16[32,2048]{1,0:T(8,128)(2,1)S(1)} %get-tuple-element.71), channel_id=1, source_target_pairs={{0,12},{2,14},{4,8},{6,10},{8,4},{10,6},{12,0},{14,2},{1,13},{3,15... | collective-permute-start | bytes 393224 | tf_op jit(solution)/shard_map/ppermute | solution.py:382
  25.5 15.9 %collective-permute-start.7 = (bf16[128,2048]{1,0:T(8,128)(2,1)S(1)}, bf16[128,2048]{1,0:T(8,128)(2,1)S(1)}, u32[]{:S(2)}, u32[]{:S(2)}) collective-permute-start(bf16[128,2048]{1,0:T(8,128)(2,1)S(1)} %constant_dynamic-update-slice_fusion.refs_0_), channel_id=1, source_target_pairs={{0,2},{2,0},{4,6},{6,4},{8,10},{10,8},{12,14},{14,12},{1,3},{3,1},... | collective-permute-start | bytes 1572872 | tf_op jit(solution)/shard_map/ppermute | solution.py:382
  29.0 11.5 %collective-permute-start.4 = (bf16[32,2048]{1,0:T(8,128)(2,1)S(1)}, bf16[32,2048]{1,0:T(8,128)(2,1)S(1)}, u32[]{:S(2)}, u32[]{:S(2)}) collective-permute-start(bf16[32,2048]{1,0:T(8,128)(2,1)S(1)} %get-tuple-element.81), channel_id=1, source_target_pairs={{0,8},{2,10},{4,12},{6,14},{8,0},{10,2},{12,4},{14,6},{1,9},{3,11}... | collective-permute-start | bytes 393224 | tf_op jit(solution)/shard_map/ppermute | solution.py:382
  30.0 10.5 %collective-permute-start.5 = (bf16[32,2048]{1,0:T(8,128)(2,1)S(1)}, bf16[32,2048]{1,0:T(8,128)(2,1)S(1)}, u32[]{:S(2)}, u32[]{:S(2)}) collective-permute-start(bf16[32,2048]{1,0:T(8,128)(2,1)S(1)} %get-tuple-element.83), channel_id=1, source_target_pairs={{0,12},{2,14},{4,8},{6,10},{8,4},{10,6},{12,0},{14,2},{1,13},{3,15... | collective-permute-start | bytes 393224 | tf_op jit(solution)/shard_map/ppermute | solution.py:382
  41.8 11.7 %collective-permute-start.8 = (bf16[32,2048]{1,0:T(8,128)(2,1)S(1)}, bf16[32,2048]{1,0:T(8,128)(2,1)S(1)}, u32[]{:S(2)}, u32[]{:S(2)}) collective-permute-start(bf16[32,2048]{1,0:T(8,128)(2,1)S(1)} %get-tuple-element.89), channel_id=1, source_target_pairs={{0,8},{2,10},{4,12},{6,14},{8,0},{10,2},{12,4},{14,6},{1,9},{3,11}... | collective-permute-start | bytes 393224 | tf_op jit(solution)/shard_map/ppermute | solution.py:382
  44.7 13.2 %collective-permute-start.9 = (bf16[32,2048]{1,0:T(8,128)(2,1)S(1)}, bf16[32,2048]{1,0:T(8,128)(2,1)S(1)}, u32[]{:S(2)}, u32[]{:S(2)}) collective-permute-start(bf16[32,2048]{1,0:T(8,128)(2,1)S(1)} %get-tuple-element.92), channel_id=1, source_target_pairs={{0,4},{2,6},{4,0},{6,2},{8,12},{10,14},{12,8},{14,10},{1,5},{3,7},... | collective-permute-start | bytes 393224 | tf_op jit(solution)/shard_map/ppermute | solution.py:382
  44.7 13.2 %collective-permute-start.10 = (bf16[32,2048]{1,0:T(8,128)(2,1)S(1)}, bf16[32,2048]{1,0:T(8,128)(2,1)S(1)}, u32[]{:S(2)}, u32[]{:S(2)}) collective-permute-start(bf16[32,2048]{1,0:T(8,128)(2,1)S(1)} %get-tuple-element.93), channel_id=1, source_target_pairs={{0,12},{2,14},{4,8},{6,10},{8,4},{10,6},{12,0},{14,2},{1,13},{3,15... | collective-permute-start | bytes 393224 | tf_op jit(solution)/shard_map/ppermute | solution.py:382
  53.6 13.0 %collective-permute-start.13 = (bf16[32,2048]{1,0:T(8,128)(2,1)S(1)}, bf16[32,2048]{1,0:T(8,128)(2,1)S(1)}, u32[]{:S(2)}, u32[]{:S(2)}) collective-permute-start(bf16[32,2048]{1,0:T(8,128)(2,1)S(1)} %get-tuple-element.90), channel_id=1, source_target_pairs={{0,12},{2,14},{4,8},{6,10},{8,4},{10,6},{12,0},{14,2},{1,13},{3,15... | collective-permute-start | bytes 393224 | tf_op jit(solution)/shard_map/ppermute | solution.py:382
  55.2 11.4 %collective-permute-start.11 = (bf16[32,2048]{1,0:T(8,128)(2,1)S(1)}, bf16[32,2048]{1,0:T(8,128)(2,1)S(1)}, u32[]{:S(2)}, u32[]{:S(2)}) collective-permute-start(bf16[32,2048]{1,0:T(8,128)(2,1)S(1)} %get-tuple-element.97), channel_id=1, source_target_pairs={{0,4},{2,6},{4,0},{6,2},{8,12},{10,14},{12,8},{14,10},{1,5},{3,7},... | collective-permute-start | bytes 393224 | tf_op jit(solution)/shard_map/ppermute | solution.py:382
  99.6 13.0 %collective-permute-start.17 = (bf16[32,2048]{1,0:T(8,128)(2,1)S(1)}, bf16[32,2048]{1,0:T(8,128)(2,1)S(1)}, u32[]{:S(2)}, u32[]{:S(2)}) collective-permute-start(bf16[32,2048]{1,0:T(8,128)(2,1)S(1)} %get-tuple-element.103), channel_id=1, source_target_pairs={{0,12},{2,14},{4,8},{6,10},{8,4},{10,6},{12,0},{14,2},{1,13},{3,15... | collective-permute-start | bytes 393224 | tf_op jit(solution)/shard_map/ppermute | solution.py:382
  100.2 11.6 %collective-permute-start.15 = (bf16[32,2048]{1,0:T(8,128)(2,1)S(1)}, bf16[32,2048]{1,0:T(8,128)(2,1)S(1)}, u32[]{:S(2)}, u32[]{:S(2)}) collective-permute-start(bf16[32,2048]{1,0:T(8,128)(2,1)S(1)} %get-tuple-element.107), channel_id=1, source_target_pairs={{0,4},{2,6},{4,0},{6,2},{8,12},{10,14},{12,8},{14,10},{1,5},{3,7},... | collective-permute-start | bytes 393224 | tf_op jit(solution)/shard_map/ppermute | solution.py:382
  100.7 11.9 %collective-permute-start.16 = (bf16[32,2048]{1,0:T(8,128)(2,1)S(1)}, bf16[32,2048]{1,0:T(8,128)(2,1)S(1)}, u32[]{:S(2)}, u32[]{:S(2)}) collective-permute-start(bf16[32,2048]{1,0:T(8,128)(2,1)S(1)} %get-tuple-element.108), channel_id=1, source_target_pairs={{0,8},{2,10},{4,12},{6,14},{8,0},{10,2},{12,4},{14,6},{1,9},{3,11}... | collective-permute-start | bytes 393224 | tf_op jit(solution)/shard_map/ppermute | solution.py:382
  112.6 13.3 %collective-permute-start.22 = (bf16[128,2048]{1,0:T(8,128)(2,1)S(1)}, bf16[128,2048]{1,0:T(8,128)(2,1)S(1)}, u32[]{:S(2)}, u32[]{:S(2)}) collective-permute-start(bf16[128,2048]{1,0:T(8,128)(2,1)S(1)} %constant_dynamic-update-slice_fusion.8.refs_0_), channel_id=1, source_target_pairs={{0,2},{2,0},{4,6},{6,4},{8,10},{10,8},{12,14},{14,12},{1,3},{3,1},... | collective-permute-start | bytes 1572872 | tf_op jit(solution)/shard_map/ppermute | solution.py:382
  113.1 11.1 %collective-permute-start.19 = (bf16[32,2048]{1,0:T(8,128)(2,1)S(1)}, bf16[32,2048]{1,0:T(8,128)(2,1)S(1)}, u32[]{:S(2)}, u32[]{:S(2)}) collective-permute-start(bf16[32,2048]{1,0:T(8,128)(2,1)S(1)} %get-tuple-element.113), channel_id=1, source_target_pairs={{0,8},{2,10},{4,12},{6,14},{8,0},{10,2},{12,4},{14,6},{1,9},{3,11}... | collective-permute-start | bytes 393224 | tf_op jit(solution)/shard_map/ppermute | solution.py:382
  124.2 10.9 %collective-permute-start.21 = (bf16[128,2048]{1,0:T(8,128)(2,1)S(1)}, bf16[128,2048]{1,0:T(8,128)(2,1)S(1)}, u32[]{:S(2)}, u32[]{:S(2)}) collective-permute-start(bf16[128,2048]{1,0:T(8,128)(2,1)S(1)} %constant_dynamic-update-slice_fusion.12.refs_0_), channel_id=1, source_target_pairs={{0,2},{2,0},{4,6},{6,4},{8,10},{10,8},{12,14},{14,12},{1,3},{3,1},... | collective-permute-start | bytes 1572872 | tf_op jit(solution)/shard_map/ppermute | solution.py:382
  126.4 13.0 %collective-permute-start.23 = (bf16[32,2048]{1,0:T(8,128)(2,1)S(1)}, bf16[32,2048]{1,0:T(8,128)(2,1)S(1)}, u32[]{:S(2)}, u32[]{:S(2)}) collective-permute-start(bf16[32,2048]{1,0:T(8,128)(2,1)S(1)} %get-tuple-element.121), channel_id=1, source_target_pairs={{0,8},{2,10},{4,12},{6,14},{8,0},{10,2},{12,4},{14,6},{1,9},{3,11}... | collective-permute-start | bytes 393224 | tf_op jit(solution)/shard_map/ppermute | solution.py:382
  129.3 14.5 %collective-permute-start.24 = (bf16[32,2048]{1,0:T(8,128)(2,1)S(1)}, bf16[32,2048]{1,0:T(8,128)(2,1)S(1)}, u32[]{:S(2)}, u32[]{:S(2)}) collective-permute-start(bf16[32,2048]{1,0:T(8,128)(2,1)S(1)} %get-tuple-element.124), channel_id=1, source_target_pairs={{0,4},{2,6},{4,0},{6,2},{8,12},{10,14},{12,8},{14,10},{1,5},{3,7},... | collective-permute-start | bytes 393224 | tf_op jit(solution)/shard_map/ppermute | solution.py:382
  129.4 14.3 %collective-permute-start.25 = (bf16[32,2048]{1,0:T(8,128)(2,1)S(1)}, bf16[32,2048]{1,0:T(8,128)(2,1)S(1)}, u32[]{:S(2)}, u32[]{:S(2)}) collective-permute-start(bf16[32,2048]{1,0:T(8,128)(2,1)S(1)} %get-tuple-element.125), channel_id=1, source_target_pairs={{0,12},{2,14},{4,8},{6,10},{8,4},{10,6},{12,0},{14,2},{1,13},{3,15... | collective-permute-start | bytes 393224 | tf_op jit(solution)/shard_map/ppermute | solution.py:382
  139.4 12.9 %collective-permute-start.28 = (bf16[32,2048]{1,0:T(8,128)(2,1)S(1)}, bf16[32,2048]{1,0:T(8,128)(2,1)S(1)}, u32[]{:S(2)}, u32[]{:S(2)}) collective-permute-start(bf16[32,2048]{1,0:T(8,128)(2,1)S(1)} %get-tuple-element.122), channel_id=1, source_target_pairs={{0,12},{2,14},{4,8},{6,10},{8,4},{10,6},{12,0},{14,2},{1,13},{3,15... | collective-permute-start | bytes 393224 | tf_op jit(solution)/shard_map/ppermute | solution.py:382
  139.4 12.9 %collective-permute-start.26 = (bf16[32,2048]{1,0:T(8,128)(2,1)S(1)}, bf16[32,2048]{1,0:T(8,128)(2,1)S(1)}, u32[]{:S(2)}, u32[]{:S(2)}) collective-permute-start(bf16[32,2048]{1,0:T(8,128)(2,1)S(1)} %get-tuple-element.129), channel_id=1, source_target_pairs={{0,4},{2,6},{4,0},{6,2},{8,12},{10,14},{12,8},{14,10},{1,5},{3,7},... | collective-permute-start | bytes 393224 | tf_op jit(solution)/shard_map/ppermute | solution.py:382
  140.5 11.8 %collective-permute-start.27 = (bf16[32,2048]{1,0:T(8,128)(2,1)S(1)}, bf16[32,2048]{1,0:T(8,128)(2,1)S(1)}, u32[]{:S(2)}, u32[]{:S(2)}) collective-permute-start(bf16[32,2048]{1,0:T(8,128)(2,1)S(1)} %get-tuple-element.131), channel_id=1, source_target_pairs={{0,8},{2,10},{4,12},{6,14},{8,0},{10,2},{12,4},{14,6},{1,9},{3,11}... | collective-permute-start | bytes 393224 | tf_op jit(solution)/shard_map/ppermute | solution.py:382
  164.9 10.5 %all-to-all-start.1 = ((f32[8,16,128]{2,1,0:T(8,128)}), f32[8,16,128]{2,1,0:T(8,128)S(1)}, u32[]{:S(2)}, u32[]{:S(2)}) async-start(f32[8,16,128]{2,1,0:T(8,128)} %bitcast.31), calls=%async_computation.1 | async-start | bytes 131072 | tf_op jit(solution)/shard_map/all_to_all | solution.py:387
  (18 other events, 126.6 us)

commit v5 on v4

--- a/solution.py
+++ b/solution.py
@@ -233,7 +233,7 @@
 def taper_body(t_ref, *refs, inputs, points, rows):
     g_refs, d_refs, al_ref = refs[:inputs], refs[inputs:-1], refs[-1]
     width = g_refs[0].shape[1]
-    step = min(512, width)
+    step = tile_of(width, 512)
     own = len(d_refs) * rows
     total = jnp.zeros((8, LANES), F32)
     for p in range(points):
@@ -475,7 +475,7 @@
             stage, ins = "rest", [then(lhs, gradient[-1])]
             gradients.append(gradient)
             if gathered and mode == "relay":
-                gradient = [then(x, gathered[-1][0]) for x in gradient]
+                gradient = list(gradient[:2]) + [then(x, gathered[-1][0]) for x in gradient[2:]]
             gathered.append(pair_up(scatter(gradient, mode), mode))
         for n, (_, _, mode) in enumerate(parts):
             got = gathered[n]
@@ -483,7 +483,7 @@
                 got = [then(got[0], gradients[n + 1][-1])] + got[1:]
             field, alignment = tapered(got, mode)
             if sent and mode == "relay":
-                field = [then(x, sent[-1][1][len(field) // 2]) for x in field]
+                field = list(field[:2]) + [then(x, sent[-1][1][len(field) // 2]) for x in field[2:]]
             sent.append((field, scatter(field, mode), alignment))
         for n, (base, _, mode) in enumerate(parts):
             _, field, alignment = sent[n]

time: 180 us -> 178 us (0.989)
  waiting for transfers between devices: 43.5 us -> 39.7 us
  starting transfers between devices: 44.7 us -> 46.9 us
    ppermute x28, waiting for transfers between devices: 33.8 us -> 30 us  [send(): lax.ppermute(x, 'freq', [(i, i ^ hop) for i in range(lax.axis_size('freq'...]
  transfers between devices with their start and end apart: 31 -> 31, of which waited for: 14 -> 13; matrix products, arithmetic and copies ran while one was open for 1% -> 1% of each run, Pallas kernels for 19% -> 19%
where the time goes in v5:
time: 178 us
  Pallas kernels  74.5 us (42%)
  starting transfers between devices  46.9 us (26%)
  waiting for transfers between devices  39.7 us (22%)
  blocking collectives  10.3 us (6%)
  local copies, waits for them, and re-layouts  4.78 us (3%)
    ppermute x28, starting transfers between devices, send(): lax.ppermute(x, 'freq', [(i, i ^ hop) for i in range(lax.axis_size('freq'...  42.5 us
    pallas_call x4, Pallas kernels, forward(): pl.pallas_call(body, in_specs=specs + [in_vmem()] * (len(start) + pieces)...  34.1 us
    pallas_call x4, Pallas kernels, adjoint(): pl.pallas_call(functools.partial(adjoint_body, pieces=pieces, points=poin...  31.2 us
    ppermute x28, waiting for transfers between devices, send(): lax.ppermute(x, 'freq', [(i, i ^ hop) for i in range(lax.axis_size('freq'...  30 us
    all_to_all x1, blocking collectives, exchange(): lax.all_to_all(x.reshape(-1, rows, width), 'freq', 0, 0, tiled=True)  10.3 us
    all_to_all x1, waiting for transfers between devices, exchange(): lax.all_to_all(x.reshape(-1, rows, width), 'freq', 0, 0, tiled=True)  6.83 us
    unnamed x34, local copies, waits for them, and re-layouts  4.3 us
    all_to_all x1, starting transfers between devices, exchange(): lax.all_to_all(x.reshape(-1, rows, width), 'freq', 0, 0, tiled=True)  4.25 us
  transfers between devices with their start and end apart: 31, of which 13 were waited for; matrix products, arithmetic and copies ran while one was open for 1% of the time, Pallas kernels for 19%

profile of v5, /device:TPU:0, one launch (start us, length us, event | category | flops | bytes accessed | tf_op | source)
XLA Modules:
  0.0 177.7 jit_solution(7791652867980980625)
XLA Ops:
  1.6 7.9 %adjoint.4 = (bf16[32,2048]{1,0:T(8,128)(2,1)S(1)}, bf16[32,2048]{1,0:T(8,128)(2,1)S(1)}, bf16[32,2048]{1,0:T(8,128)(2,1)S(1)}, bf16[32,2048]{1,0:T(8,128)(2,1)S(1)}, bf16[8,16,640]{2,1,0:T(8,128)(2,1)S(1)}) custom-call(s32[1]{0:T(128)} %bitcast.1.turn_ref.turn, bf16[2,8,320,4096]{3,2,1,0:T(8,128)(2,1)} %k_hbm.11, f32[2,8,8,320]{3,2,1,0:T(8,128)S(1)} %bitcast.27), custom_call_target="tpu_custom_call" | custom-call | flops 2684354560 | bytes 20971520 | tf_op jit(solution)/shard_map/adjoint/pallas_call | solution.py:120
  9.5 3.1 %collective-permute-start.1 = (bf16[32,2048]{1,0:T(8,128)(2,1)S(1)}, bf16[32,2048]{1,0:T(8,128)(2,1)S(1)}, u32[]{:S(2)}, u32[]{:S(2)}) collective-permute-start(bf16[32,2048]{1,0:T(8,128)(2,1)S(1)} %get-tuple-element.69), channel_id=1, source_target_pairs={{0,4},{2,6},{4,0},{6,2},{8,12},{10,14},{12,8},{14,10},{1,5},{3,7},... | collective-permute-start | bytes 393224 | tf_op jit(solution)/shard_map/ppermute | solution.py:382
  12.6 2.6 %collective-permute-start.2 = (bf16[32,2048]{1,0:T(8,128)(2,1)S(1)}, bf16[32,2048]{1,0:T(8,128)(2,1)S(1)}, u32[]{:S(2)}, u32[]{:S(2)}) collective-permute-start(bf16[32,2048]{1,0:T(8,128)(2,1)S(1)} %get-tuple-element.70), channel_id=1, source_target_pairs={{0,8},{2,10},{4,12},{6,14},{8,0},{10,2},{12,4},{14,6},{1,9},{3,11}... | collective-permute-start | bytes 393224 | tf_op jit(solution)/shard_map/ppermute | solution.py:382
  15.2 7.7 %adjoint.5 = (bf16[32,2048]{1,0:T(8,128)(2,1)S(1)}, bf16[32,2048]{1,0:T(8,128)(2,1)S(1)}, bf16[32,2048]{1,0:T(8,128)(2,1)S(1)}, bf16[32,2048]{1,0:T(8,128)(2,1)S(1)}) custom-call(s32[1]{0:T(128)} %bitcast.1.turn_ref.turn, bf16[2,8,320,4096]{3,2,1,0:T(8,128)(2,1)} %k_hbm.11, bf16[8,16,640]{2,1,0:T(8,128)(2,1)S(1)} %get-tuple-element.64.refs_0_), custom_call_target="tpu_custom_call" | custom-call | flops 2684354560 | bytes 20971520 | tf_op jit(solution)/shard_map/adjoint/pallas_call | solution.py:120
  27.3 2.8 %collective-permute-start.4 = (bf16[32,2048]{1,0:T(8,128)(2,1)S(1)}, bf16[32,2048]{1,0:T(8,128)(2,1)S(1)}, u32[]{:S(2)}, u32[]{:S(2)}) collective-permute-start(bf16[32,2048]{1,0:T(8,128)(2,1)S(1)} %get-tuple-element.71), channel_id=1, source_target_pairs={{0,8},{2,10},{4,12},{6,14},{8,0},{10,2},{12,4},{14,6},{1,9},{3,11}... | collective-permute-start | bytes 393224 | tf_op jit(solution)/shard_map/ppermute | solution.py:382
  31.5 7.3 %collective-permute-done.4 = bf16[32,2048]{1,0:T(8,128)(2,1)S(1)} collective-permute-done((bf16[32,2048]{1,0:T(8,128)(2,1)S(1)}, bf16[32,2048]{1,0:T(8,128)(2,1)S(1)}, u32[]{:S(2)}, u32[]{:S(2)}) %collective-permute-start.4) | collective-permute-done | bytes 131104 | tf_op jit(solution)/shard_map/ppermute | solution.py:382
  40.7 2.5 %collective-permute-start.8 = (bf16[32,2048]{1,0:T(8,128)(2,1)S(1)}, bf16[32,2048]{1,0:T(8,128)(2,1)S(1)}, u32[]{:S(2)}, u32[]{:S(2)}) collective-permute-start(bf16[32,2048]{1,0:T(8,128)(2,1)S(1)} %get-tuple-element.79), channel_id=1, source_target_pairs={{0,8},{2,10},{4,12},{6,14},{8,0},{10,2},{12,4},{14,6},{1,9},{3,11}... | collective-permute-start | bytes 393224 | tf_op jit(solution)/shard_map/ppermute | solution.py:382
  45.1 6.1 %collective-permute-done.6.refs_1_ = bf16[128,2048]{1,0:T(8,128)(2,1)S(1)} collective-permute-done((bf16[128,2048]{1,0:T(8,128)(2,1)S(1)}, bf16[128,2048]{1,0:T(8,128)(2,1)S(1)}, u32[]{:S(2)}, u32[]{:S(2)}) %collective-permute-start.6) | collective-permute-done | bytes 524320 | tf_op jit(solution)/shard_map/ppermute | solution.py:382
  51.7 3.4 %collective-permute-start.11 = (bf16[32,2048]{1,0:T(8,128)(2,1)S(1)}, bf16[32,2048]{1,0:T(8,128)(2,1)S(1)}, u32[]{:S(2)}, u32[]{:S(2)}) collective-permute-start(bf16[32,2048]{1,0:T(8,128)(2,1)S(1)} %get-tuple-element.85), channel_id=1, source_target_pairs={{0,4},{2,6},{4,0},{6,2},{8,12},{10,14},{12,8},{14,10},{1,5},{3,7},... | collective-permute-start | bytes 393224 | tf_op jit(solution)/shard_map/ppermute | solution.py:382
  56.6 8.6 %forward.4.init_ref = f32[136,320]{1,0:T(8,128)S(1)} custom-call(s32[1]{0:T(128)} %bitcast.1.turn_ref.turn, bf16[2,8,320,4096]{3,2,1,0:T(8,128)(2,1)} %k_hbm.11, f32[8,128]{1,0:T(8,128)S(1)} %get-tuple-element.76.al, bf16[32,2048]{1,0:T(8,128)(2,1)S(1)} %get-tuple-element.81.rest_0_.refs_1_, bf16[32,2048]{1,0:T(8,128)(2,1)S(1)} %collective-permute-done.9.rest_1_.refs_2_, ...), custom_call_target="tpu_custom_call" | custom-call | flops 2684354560 | bytes 20971520 | tf_op jit(solution)/shard_map/forward/pallas_call | solution.py:209
  66.8 8.5 %forward.5.own_ref = f32[136,320]{1,0:T(8,128)S(1)} custom-call(s32[1]{0:T(128)} %bitcast.1.turn_ref.turn, bf16[2,8,320,4096]{3,2,1,0:T(8,128)(2,1)} %k_hbm.11, f32[8,128]{1,0:T(8,128)S(1)} %get-tuple-element.74.al_ref, f32[136,320]{1,0:T(8,128)S(1)} %forward.4.init_ref, bf16[32,2048]{1,0:T(8,128)(2,1)S(1)} %get-tuple-element.84.refs_0_.refs_9_, ...), custom_call_target="tpu_custom_call" | custom-call | flops 2684354560 | bytes 20971520 | tf_op jit(solution)/shard_map/forward/pallas_call | solution.py:209
  79.3 10.3 %all_to_all.10 = f32[8,16,128]{2,1,0:T(8,128)S(1)} all-to-all(f32[8,16,128]{2,1,0:T(8,128)} %bitcast.32), channel_id=1, replica_groups=mesh['grp'=2,'freq'=8,'src'=2] {'freq'}, dimensions={0} | all-to-all | bytes 131072 | tf_op jit(solution)/shard_map/all_to_all | solution.py:387
  90.6 7.8 %adjoint.6 = (bf16[32,2048]{1,0:T(8,128)(2,1)S(1)}, bf16[32,2048]{1,0:T(8,128)(2,1)S(1)}, bf16[32,2048]{1,0:T(8,128)(2,1)S(1)}, bf16[32,2048]{1,0:T(8,128)(2,1)S...) custom-call(s32[1]{0:T(128)} %bitcast.1.turn_ref.turn, ...), custom_call_target="tpu_custom_call" | custom-call | flops 2684354560 | bytes 20971520 | tf_op jit(solution)/shard_map/adjoint/pallas_call | solution.py:120
  99.5 3.3 %collective-permute-start.17 = (bf16[32,2048]{1,0:T(8,128)(2,1)S(1)}, bf16[32,2048]{1,0:T(8,128)(2,1)S(1)}, u32[]{:S(2)}, u32[]{:S(2)}) collective-permute-start(bf16[32,2048]{1,0:T(8,128)(2,1)S(1)} %get-tuple-element.98), channel_id=1, source_target_pairs={{0,8},{2,10},{4,12},{6,14},{8,0},{10,2},{12,4},{14,6},{1,9},{3,11}... | collective-permute-start | bytes 393224 | tf_op jit(solution)/shard_map/ppermute | solution.py:382
  102.8 7.7 %adjoint.7 = (bf16[32,2048]{1,0:T(8,128)(2,1)S(1)}, bf16[32,2048]{1,0:T(8,128)(2,1)S(1)}, bf16[32,2048]{1,0:T(8,128)(2,1)S(1)}, bf16[32,2048]{1,0:T(8,128)(2,1)S(1)}) custom-call(s32[1]{0:T(128)} %bitcast.1.turn_ref.turn, bf16[2,8,320,4096]{3,2,1,0:T(8,128)(2,1)} %k_hbm.11, bf16[8,16,640]{2,1,0:T(8,128)(2,1)S(1)} %get-tuple-element.92.refs_0_), custom_call_target="tpu_custom_call" | custom-call | flops 2684354560 | bytes 20971520 | tf_op jit(solution)/shard_map/adjoint/pallas_call | solution.py:120
  112.8 2.8 %collective-permute-start.20 = (bf16[32,2048]{1,0:T(8,128)(2,1)S(1)}, bf16[32,2048]{1,0:T(8,128)(2,1)S(1)}, u32[]{:S(2)}, u32[]{:S(2)}) collective-permute-start(bf16[32,2048]{1,0:T(8,128)(2,1)S(1)} %get-tuple-element.101), channel_id=1, source_target_pairs={{0,12},{2,14},{4,8},{6,10},{8,4},{10,6},{12,0},{14,2},{1,13},{3,15... | collective-permute-start | bytes 393224 | tf_op jit(solution)/shard_map/ppermute | solution.py:382
  115.7 6.7 %collective-permute-done.19 = bf16[32,2048]{1,0:T(8,128)(2,1)S(1)} collective-permute-done((bf16[32,2048]{1,0:T(8,128)(2,1)S(1)}, bf16[32,2048]{1,0:T(8,128)(2,1)S(1)}, u32[]{:S(2)}, u32[]{:S(2)}) %collective-permute-start.19) | collective-permute-done | bytes 131104 | tf_op jit(solution)/shard_map/ppermute | solution.py:382
  129.4 4.6 %collective-permute-done.21.refs_1_ = bf16[128,2048]{1,0:T(8,128)(2,1)S(1)} collective-permute-done((bf16[128,2048]{1,0:T(8,128)(2,1)S(1)}, bf16[128,2048]{1,0:T(8,128)(2,1)S(1)}, u32[]{:S(2)}, u32[]{:S(2)}) %collective-permute-start.21) | collective-permute-done | bytes 524320 | tf_op jit(solution)/shard_map/ppermute | solution.py:382
  134.5 3.0 %collective-permute-start.26 = (bf16[32,2048]{1,0:T(8,128)(2,1)S(1)}, bf16[32,2048]{1,0:T(8,128)(2,1)S(1)}, u32[]{:S(2)}, u32[]{:S(2)}) collective-permute-start(bf16[32,2048]{1,0:T(8,128)(2,1)S(1)} %get-tuple-element.113), channel_id=1, source_target_pairs={{0,4},{2,6},{4,0},{6,2},{8,12},{10,14},{12,8},{14,10},{1,5},{3,7},... | collective-permute-start | bytes 393224 | tf_op jit(solution)/shard_map/ppermute | solution.py:382
  139.5 8.5 %forward.6.init_ref = f32[136,320]{1,0:T(8,128)S(1)} custom-call(s32[1]{0:T(128)} %bitcast.1.turn_ref.turn, bf16[2,8,320,4096]{3,2,1,0:T(8,128)(2,1)} %k_hbm.11, f32[8,128]{1,0:T(8,128)S(1)} %get-tuple-element.104.al, bf16[32,2048]{1,0:T(8,128)(2,1)S(1)} %get-tuple-element.109.rest_0_.refs_5_, bf16[32,2048]{1,0:T(8,128)(2,1)S(1)} %collective-permute-done.24.rest_1_.refs_6_, ...), custom_call_target="tpu_custom_call" | custom-call | flops 2684354560 | bytes 20971520 | tf_op jit(solution)/shard_map/forward/pallas_call | solution.py:209
  149.3 8.5 %forward.7.own_ref = f32[136,320]{1,0:T(8,128)S(1)} custom-call(s32[1]{0:T(128)} %bitcast.1.turn_ref.turn, bf16[2,8,320,4096]{3,2,1,0:T(8,128)(2,1)} %k_hbm.11, f32[8,128]{1,0:T(8,128)S(1)} %get-tuple-element.102.al_ref, f32[136,320]{1,0:T(8,128)S(1)} %forward.6.init_ref, bf16[32,2048]{1,0:T(8,128)(2,1)S(1)} %get-tuple-element.112.refs_0_.refs_13_, ...), custom_call_target="tpu_custom_call" | custom-call | flops 2684354560 | bytes 20971520 | tf_op jit(solution)/shard_map/forward/pallas_call | solution.py:209
  161.8 4.3 %all-to-all-start.1 = ((f32[8,16,128]{2,1,0:T(8,128)}), f32[8,16,128]{2,1,0:T(8,128)S(1)}, u32[]{:S(2)}, u32[]{:S(2)}) async-start(f32[8,16,128]{2,1,0:T(8,128)} %bitcast.31), calls=%async_computation.1 | async-start | bytes 131072 | tf_op jit(solution)/shard_map/all_to_all | solution.py:387
  166.1 6.8 %all-to-all-done.1 = f32[8,16,128]{2,1,0:T(8,128)S(1)} async-done(((f32[8,16,128]{2,1,0:T(8,128)}), f32[8,16,128]{2,1,0:T(8,128)S(1)}, u32[]{:S(2)}, u32[]{:S(2)}) %all-to-all-start.1) | async-done | bytes 65568 | tf_op jit(solution)/shard_map/all_to_all | solution.py:387
  173.8 3.8 %finish.1 = (f32[2,8,8,4096]{3,2,1,0:T(8,128)}, f32[2,8,8,160]{3,2,1,0:T(8,128)}) custom-call(s32[3]{0:T(128)S(1)} %pad_add_fusion.place_ref, f32[128,128]{1,0:T(8,128)S(1)} %bitcast.30, f32[128,320]{1,0:T(8,128)S(1)} %copy-done.5, f32[2,8,8,320]{3,2,1,0:T(8,128)S(1)} %get-tuple-element.118.r_ref, f32[8,128]{1,0:T(8,128)S(1)} %get-tuple-element.119.refs_0_, ...), custom_call_target="tpu_custom_call" | custom-call | tf_op jit(solution)/shard_map/finish/pallas_call | solution.py:362
  (101 shorter events, 37.6 us)
Async XLA Ops:
  9.5 15.0 %collective-permute-start.1 = (bf16[32,2048]{1,0:T(8,128)(2,1)S(1)}, bf16[32,2048]{1,0:T(8,128)(2,1)S(1)}, u32[]{:S(2)}, u32[]{:S(2)}) collective-permute-start(bf16[32,2048]{1,0:T(8,128)(2,1)S(1)} %get-tuple-element.69), channel_id=1, source_target_pairs={{0,4},{2,6},{4,0},{6,2},{8,12},{10,14},{12,8},{14,10},{1,5},{3,7},... | collective-permute-start | bytes 393224 | tf_op jit(solution)/shard_map/ppermute | solution.py:382
  12.6 13.0 %collective-permute-start.2 = (bf16[32,2048]{1,0:T(8,128)(2,1)S(1)}, bf16[32,2048]{1,0:T(8,128)(2,1)S(1)}, u32[]{:S(2)}, u32[]{:S(2)}) collective-permute-start(bf16[32,2048]{1,0:T(8,128)(2,1)S(1)} %get-tuple-element.70), channel_id=1, source_target_pairs={{0,8},{2,10},{4,12},{6,14},{8,0},{10,2},{12,4},{14,6},{1,9},{3,11}... | collective-permute-start | bytes 393224 | tf_op jit(solution)/shard_map/ppermute | solution.py:382
  15.2 10.5 %collective-permute-start.3 = (bf16[32,2048]{1,0:T(8,128)(2,1)S(1)}, bf16[32,2048]{1,0:T(8,128)(2,1)S(1)}, u32[]{:S(2)}, u32[]{:S(2)}) collective-permute-start(bf16[32,2048]{1,0:T(8,128)(2,1)S(1)} %get-tuple-element.63), channel_id=1, source_target_pairs={{0,12},{2,14},{4,8},{6,10},{8,4},{10,6},{12,0},{14,2},{1,13},{3,15... | collective-permute-start | bytes 393224 | tf_op jit(solution)/shard_map/ppermute | solution.py:382
  25.7 14.5 %collective-permute-start.7 = (bf16[128,2048]{1,0:T(8,128)(2,1)S(1)}, bf16[128,2048]{1,0:T(8,128)(2,1)S(1)}, u32[]{:S(2)}, u32[]{:S(2)}) collective-permute-start(bf16[128,2048]{1,0:T(8,128)(2,1)S(1)} %constant_dynamic-update-slice_fusion.refs_0_), channel_id=1, source_target_pairs={{0,2},{2,0},{4,6},{6,4},{8,10},{10,8},{12,14},{14,12},{1,3},{3,1},... | collective-permute-start | bytes 1572872 | tf_op jit(solution)/shard_map/ppermute | solution.py:382
  27.3 11.5 %collective-permute-start.4 = (bf16[32,2048]{1,0:T(8,128)(2,1)S(1)}, bf16[32,2048]{1,0:T(8,128)(2,1)S(1)}, u32[]{:S(2)}, u32[]{:S(2)}) collective-permute-start(bf16[32,2048]{1,0:T(8,128)(2,1)S(1)} %get-tuple-element.71), channel_id=1, source_target_pairs={{0,8},{2,10},{4,12},{6,14},{8,0},{10,2},{12,4},{14,6},{1,9},{3,11}... | collective-permute-start | bytes 393224 | tf_op jit(solution)/shard_map/ppermute | solution.py:382
  38.9 12.3 %collective-permute-start.6 = (bf16[128,2048]{1,0:T(8,128)(2,1)S(1)}, bf16[128,2048]{1,0:T(8,128)(2,1)S(1)}, u32[]{:S(2)}, u32[]{:S(2)}) collective-permute-start(bf16[128,2048]{1,0:T(8,128)(2,1)S(1)} %constant_dynamic-update-slice_fusion.4.refs_0_), channel_id=1, source_target_pairs={{0,2},{2,0},{4,6},{6,4},{8,10},{10,8},{12,14},{14,12},{1,3},{3,1},... | collective-permute-start | bytes 1572872 | tf_op jit(solution)/shard_map/ppermute | solution.py:382
  40.7 14.4 %collective-permute-start.8 = (bf16[32,2048]{1,0:T(8,128)(2,1)S(1)}, bf16[32,2048]{1,0:T(8,128)(2,1)S(1)}, u32[]{:S(2)}, u32[]{:S(2)}) collective-permute-start(bf16[32,2048]{1,0:T(8,128)(2,1)S(1)} %get-tuple-element.79), channel_id=1, source_target_pairs={{0,8},{2,10},{4,12},{6,14},{8,0},{10,2},{12,4},{14,6},{1,9},{3,11}... | collective-permute-start | bytes 393224 | tf_op jit(solution)/shard_map/ppermute | solution.py:382
  43.2 13.4 %collective-permute-start.9 = (bf16[32,2048]{1,0:T(8,128)(2,1)S(1)}, bf16[32,2048]{1,0:T(8,128)(2,1)S(1)}, u32[]{:S(2)}, u32[]{:S(2)}) collective-permute-start(bf16[32,2048]{1,0:T(8,128)(2,1)S(1)} %get-tuple-element.82), channel_id=1, source_target_pairs={{0,4},{2,6},{4,0},{6,2},{8,12},{10,14},{12,8},{14,10},{1,5},{3,7},... | collective-permute-start | bytes 393224 | tf_op jit(solution)/shard_map/ppermute | solution.py:382
  43.3 13.3 %collective-permute-start.10 = (bf16[32,2048]{1,0:T(8,128)(2,1)S(1)}, bf16[32,2048]{1,0:T(8,128)(2,1)S(1)}, u32[]{:S(2)}, u32[]{:S(2)}) collective-permute-start(bf16[32,2048]{1,0:T(8,128)(2,1)S(1)} %get-tuple-element.83), channel_id=1, source_target_pairs={{0,12},{2,14},{4,8},{6,10},{8,4},{10,6},{12,0},{14,2},{1,13},{3,15... | collective-permute-start | bytes 393224 | tf_op jit(solution)/shard_map/ppermute | solution.py:382
  51.7 13.5 %collective-permute-start.11 = (bf16[32,2048]{1,0:T(8,128)(2,1)S(1)}, bf16[32,2048]{1,0:T(8,128)(2,1)S(1)}, u32[]{:S(2)}, u32[]{:S(2)}) collective-permute-start(bf16[32,2048]{1,0:T(8,128)(2,1)S(1)} %get-tuple-element.85), channel_id=1, source_target_pairs={{0,4},{2,6},{4,0},{6,2},{8,12},{10,14},{12,8},{14,10},{1,5},{3,7},... | collective-permute-start | bytes 393224 | tf_op jit(solution)/shard_map/ppermute | solution.py:382
  55.1 10.2 %collective-permute-start.13 = (bf16[32,2048]{1,0:T(8,128)(2,1)S(1)}, bf16[32,2048]{1,0:T(8,128)(2,1)S(1)}, u32[]{:S(2)}, u32[]{:S(2)}) collective-permute-start(bf16[32,2048]{1,0:T(8,128)(2,1)S(1)} %get-tuple-element.80), channel_id=1, source_target_pairs={{0,12},{2,14},{4,8},{6,10},{8,4},{10,6},{12,0},{14,2},{1,13},{3,15... | collective-permute-start | bytes 393224 | tf_op jit(solution)/shard_map/ppermute | solution.py:382
  56.0 10.8 %collective-permute-start.12 = (bf16[32,2048]{1,0:T(8,128)(2,1)S(1)}, bf16[32,2048]{1,0:T(8,128)(2,1)S(1)}, u32[]{:S(2)}, u32[]{:S(2)}) collective-permute-start(bf16[32,2048]{1,0:T(8,128)(2,1)S(1)} %get-tuple-element.87), channel_id=1, source_target_pairs={{0,8},{2,10},{4,12},{6,14},{8,0},{10,2},{12,4},{14,6},{1,9},{3,11}... | collective-permute-start | bytes 393224 | tf_op jit(solution)/shard_map/ppermute | solution.py:382
  98.4 13.1 %collective-permute-start.18 = (bf16[32,2048]{1,0:T(8,128)(2,1)S(1)}, bf16[32,2048]{1,0:T(8,128)(2,1)S(1)}, u32[]{:S(2)}, u32[]{:S(2)}) collective-permute-start(bf16[32,2048]{1,0:T(8,128)(2,1)S(1)} %get-tuple-element.91), channel_id=1, source_target_pairs={{0,12},{2,14},{4,8},{6,10},{8,4},{10,6},{12,0},{14,2},{1,13},{3,15... | collective-permute-start | bytes 393224 | tf_op jit(solution)/shard_map/ppermute | solution.py:382
  99.0 11.7 %collective-permute-start.16 = (bf16[32,2048]{1,0:T(8,128)(2,1)S(1)}, bf16[32,2048]{1,0:T(8,128)(2,1)S(1)}, u32[]{:S(2)}, u32[]{:S(2)}) collective-permute-start(bf16[32,2048]{1,0:T(8,128)(2,1)S(1)} %get-tuple-element.97), channel_id=1, source_target_pairs={{0,4},{2,6},{4,0},{6,2},{8,12},{10,14},{12,8},{14,10},{1,5},{3,7},... | collective-permute-start | bytes 393224 | tf_op jit(solution)/shard_map/ppermute | solution.py:382
  99.5 12.0 %collective-permute-start.17 = (bf16[32,2048]{1,0:T(8,128)(2,1)S(1)}, bf16[32,2048]{1,0:T(8,128)(2,1)S(1)}, u32[]{:S(2)}, u32[]{:S(2)}) collective-permute-start(bf16[32,2048]{1,0:T(8,128)(2,1)S(1)} %get-tuple-element.98), channel_id=1, source_target_pairs={{0,8},{2,10},{4,12},{6,14},{8,0},{10,2},{12,4},{14,6},{1,9},{3,11}... | collective-permute-start | bytes 393224 | tf_op jit(solution)/shard_map/ppermute | solution.py:382
  111.5 13.0 %collective-permute-start.22 = (bf16[128,2048]{1,0:T(8,128)(2,1)S(1)}, bf16[128,2048]{1,0:T(8,128)(2,1)S(1)}, u32[]{:S(2)}, u32[]{:S(2)}) collective-permute-start(bf16[128,2048]{1,0:T(8,128)(2,1)S(1)} %constant_dynamic-update-slice_fusion.8.refs_0_), channel_id=1, source_target_pairs={{0,2},{2,0},{4,6},{6,4},{8,10},{10,8},{12,14},{14,12},{1,3},{3,1},... | collective-permute-start | bytes 1572872 | tf_op jit(solution)/shard_map/ppermute | solution.py:382
  112.1 10.4 %collective-permute-start.19 = (bf16[32,2048]{1,0:T(8,128)(2,1)S(1)}, bf16[32,2048]{1,0:T(8,128)(2,1)S(1)}, u32[]{:S(2)}, u32[]{:S(2)}) collective-permute-start(bf16[32,2048]{1,0:T(8,128)(2,1)S(1)} %get-tuple-element.99), channel_id=1, source_target_pairs={{0,8},{2,10},{4,12},{6,14},{8,0},{10,2},{12,4},{14,6},{1,9},{3,11}... | collective-permute-start | bytes 393224 | tf_op jit(solution)/shard_map/ppermute | solution.py:382
  122.5 11.6 %collective-permute-start.21 = (bf16[128,2048]{1,0:T(8,128)(2,1)S(1)}, bf16[128,2048]{1,0:T(8,128)(2,1)S(1)}, u32[]{:S(2)}, u32[]{:S(2)}) collective-permute-start(bf16[128,2048]{1,0:T(8,128)(2,1)S(1)} %constant_dynamic-update-slice_fusion.12.refs_0_), channel_id=1, source_target_pairs={{0,2},{2,0},{4,6},{6,4},{8,10},{10,8},{12,14},{14,12},{1,3},{3,1},... | collective-permute-start | bytes 1572872 | tf_op jit(solution)/shard_map/ppermute | solution.py:382
  125.0 12.5 %collective-permute-start.23 = (bf16[32,2048]{1,0:T(8,128)(2,1)S(1)}, bf16[32,2048]{1,0:T(8,128)(2,1)S(1)}, u32[]{:S(2)}, u32[]{:S(2)}) collective-permute-start(bf16[32,2048]{1,0:T(8,128)(2,1)S(1)} %get-tuple-element.107), channel_id=1, source_target_pairs={{0,8},{2,10},{4,12},{6,14},{8,0},{10,2},{12,4},{14,6},{1,9},{3,11}... | collective-permute-start | bytes 393224 | tf_op jit(solution)/shard_map/ppermute | solution.py:382
  127.1 12.4 %collective-permute-start.24 = (bf16[32,2048]{1,0:T(8,128)(2,1)S(1)}, bf16[32,2048]{1,0:T(8,128)(2,1)S(1)}, u32[]{:S(2)}, u32[]{:S(2)}) collective-permute-start(bf16[32,2048]{1,0:T(8,128)(2,1)S(1)} %get-tuple-element.110), channel_id=1, source_target_pairs={{0,4},{2,6},{4,0},{6,2},{8,12},{10,14},{12,8},{14,10},{1,5},{3,7},... | collective-permute-start | bytes 393224 | tf_op jit(solution)/shard_map/ppermute | solution.py:382
  128.7 10.8 %collective-permute-start.25 = (bf16[32,2048]{1,0:T(8,128)(2,1)S(1)}, bf16[32,2048]{1,0:T(8,128)(2,1)S(1)}, u32[]{:S(2)}, u32[]{:S(2)}) collective-permute-start(bf16[32,2048]{1,0:T(8,128)(2,1)S(1)} %get-tuple-element.111), channel_id=1, source_target_pairs={{0,12},{2,14},{4,8},{6,10},{8,4},{10,6},{12,0},{14,2},{1,13},{3,15... | collective-permute-start | bytes 393224 | tf_op jit(solution)/shard_map/ppermute | solution.py:382
  134.5 13.5 %collective-permute-start.26 = (bf16[32,2048]{1,0:T(8,128)(2,1)S(1)}, bf16[32,2048]{1,0:T(8,128)(2,1)S(1)}, u32[]{:S(2)}, u32[]{:S(2)}) collective-permute-start(bf16[32,2048]{1,0:T(8,128)(2,1)S(1)} %get-tuple-element.113), channel_id=1, source_target_pairs={{0,4},{2,6},{4,0},{6,2},{8,12},{10,14},{12,8},{14,10},{1,5},{3,7},... | collective-permute-start | bytes 393224 | tf_op jit(solution)/shard_map/ppermute | solution.py:382
  137.5 10.5 %collective-permute-start.28 = (bf16[32,2048]{1,0:T(8,128)(2,1)S(1)}, bf16[32,2048]{1,0:T(8,128)(2,1)S(1)}, u32[]{:S(2)}, u32[]{:S(2)}) collective-permute-start(bf16[32,2048]{1,0:T(8,128)(2,1)S(1)} %get-tuple-element.108), channel_id=1, source_target_pairs={{0,12},{2,14},{4,8},{6,10},{8,4},{10,6},{12,0},{14,2},{1,13},{3,15... | collective-permute-start | bytes 393224 | tf_op jit(solution)/shard_map/ppermute | solution.py:382
  161.8 11.2 %all-to-all-start.1 = ((f32[8,16,128]{2,1,0:T(8,128)}), f32[8,16,128]{2,1,0:T(8,128)S(1)}, u32[]{:S(2)}, u32[]{:S(2)}) async-start(f32[8,16,128]{2,1,0:T(8,128)} %bitcast.31), calls=%async_computation.1 | async-start | bytes 131072 | tf_op jit(solution)/shard_map/all_to_all | solution.py:387
  (18 other events, 152.4 us)

commit v6 on v5

--- a/solution.py
+++ b/solution.py
@@ -127,7 +127,7 @@
         scratch_shapes=[
             pltpu.VMEM((depth, 2, 1, receivers, ts), BF16),
             pltpu.SemaphoreType.DMA((depth,)),
-            pltpu.VMEM((ts // LANES, 2 * points * fl, LANES), F32),
+            pltpu.VMEM((ts // LANES, 2 * points * fl + 2 * fl, LANES), F32),
         ],
         compiler_params=pltpu.CompilerParams(vmem_limit_bytes=VMEM_LIMIT),
         cost_estimate=pl.CostEstimate(
@@ -214,7 +214,7 @@
         scratch_shapes=[
             pltpu.VMEM((depth, 2, group, receivers, ts), BF16),
             pltpu.SemaphoreType.DMA((depth,)),
-            pltpu.VMEM((ts // LANES, 2 * points * fl, LANES), F32),
+            pltpu.VMEM((ts // LANES, 2 * points * fl + 2 * fl, LANES), F32),
             pltpu.VMEM((fl // group, 2 * points * group, 2 * receivers * group), F32),
         ],
         compiler_params=pltpu.CompilerParams(vmem_limit_bytes=VMEM_LIMIT),
@@ -336,7 +336,7 @@
                     stage[c, f, :, out] = scr[i % 2, pl.ds(c * fl + f, points, stride=2 * fl), :]
             return carry
 
-        lax.fori_loop(0, width // LANES, one, 0, unroll=2)
+        lax.fori_loop(0, width // LANES, one, 0, unroll=4)
         span = pl.ds(base, width)
         copies.append(
             pltpu.make_async_copy(stage.at[:, :, :, span], e_hbm.at[:, :, :, span], sem.at[part])
@@ -366,7 +366,7 @@
         out_shape=[jax.ShapeDtypeStruct(shape, F32), jax.ShapeDtypeStruct((2, fl, points, share), F32)],
         scratch_shapes=[
             pltpu.VMEM(shape, F32),
-            pltpu.VMEM((2, 2 * points * fl, LANES), F32),
+            pltpu.VMEM((2, 2 * points * fl + 2 * fl, LANES), F32),
             pltpu.SemaphoreType.DMA((len(spans),)),
         ],
         compiler_params=pltpu.CompilerParams(vmem_limit_bytes=VMEM_LIMIT),

time: 178 us -> 178 us (level)
  no operation moved by 1% of the time
where the time goes in v6:
time: 178 us
  Pallas kernels  74.3 us (42%)
  starting transfers between devices  46.9 us (26%)
  waiting for transfers between devices  39.8 us (22%)
  blocking collectives  10.3 us (6%)
  local copies, waits for them, and re-layouts  4.78 us (3%)
    ppermute x28, starting transfers between devices, send(): lax.ppermute(x, 'freq', [(i, i ^ hop) for i in range(lax.axis_size('freq'...  43 us
    pallas_call x4, Pallas kernels, forward(): pl.pallas_call(body, in_specs=specs + [in_vmem()] * (len(start) + pieces)...  34.1 us
    pallas_call x4, Pallas kernels, adjoint(): pl.pallas_call(functools.partial(adjoint_body, pieces=pieces, points=poin...  31.2 us
    ppermute x28, waiting for transfers between devices, send(): lax.ppermute(x, 'freq', [(i, i ^ hop) for i in range(lax.axis_size('freq'...  30.1 us
    all_to_all x1, blocking collectives, exchange(): lax.all_to_all(x.reshape(-1, rows, width), 'freq', 0, 0, tiled=True)  10.3 us
    all_to_all x1, waiting for transfers between devices, exchange(): lax.all_to_all(x.reshape(-1, rows, width), 'freq', 0, 0, tiled=True)  6.83 us
    unnamed x34, local copies, waits for them, and re-layouts  4.3 us
    all_to_all x1, starting transfers between devices, exchange(): lax.all_to_all(x.reshape(-1, rows, width), 'freq', 0, 0, tiled=True)  3.8 us
  transfers between devices with their start and end apart: 31, of which 13 were waited for; matrix products, arithmetic and copies ran while one was open for 1% of the time, Pallas kernels for 19%

profile of v6, /device:TPU:0, one launch (start us, length us, event | category | flops | bytes accessed | tf_op | source)
XLA Modules:
  0.0 177.5 jit_solution(10471496813566817551)
XLA Ops:
  1.6 7.9 %adjoint.4 = (bf16[32,2048]{1,0:T(8,128)(2,1)S(1)}, bf16[32,2048]{1,0:T(8,128)(2,1)S(1)}, bf16[32,2048]{1,0:T(8,128)(2,1)S(1)}, bf16[32,2048]{1,0:T(8,128)(2,1)S(1)}, bf16[8,16,640]{2,1,0:T(8,128)(2,1)S(1)}) custom-call(s32[1]{0:T(128)} %bitcast.1.turn_ref.turn, bf16[2,8,320,4096]{3,2,1,0:T(8,128)(2,1)} %k_hbm.11, f32[2,8,8,320]{3,2,1,0:T(8,128)S(1)} %bitcast.27), custom_call_target="tpu_custom_call" | custom-call | flops 2684354560 | bytes 20971520 | tf_op jit(solution)/shard_map/adjoint/pallas_call | solution.py:120
  9.5 3.1 %collective-permute-start.1 = (bf16[32,2048]{1,0:T(8,128)(2,1)S(1)}, bf16[32,2048]{1,0:T(8,128)(2,1)S(1)}, u32[]{:S(2)}, u32[]{:S(2)}) collective-permute-start(bf16[32,2048]{1,0:T(8,128)(2,1)S(1)} %get-tuple-element.69), channel_id=1, source_target_pairs={{0,4},{2,6},{4,0},{6,2},{8,12},{10,14},{12,8},{14,10},{1,5},{3,7},... | collective-permute-start | bytes 393224 | tf_op jit(solution)/shard_map/ppermute | solution.py:382
  12.6 2.6 %collective-permute-start.2 = (bf16[32,2048]{1,0:T(8,128)(2,1)S(1)}, bf16[32,2048]{1,0:T(8,128)(2,1)S(1)}, u32[]{:S(2)}, u32[]{:S(2)}) collective-permute-start(bf16[32,2048]{1,0:T(8,128)(2,1)S(1)} %get-tuple-element.70), channel_id=1, source_target_pairs={{0,8},{2,10},{4,12},{6,14},{8,0},{10,2},{12,4},{14,6},{1,9},{3,11}... | collective-permute-start | bytes 393224 | tf_op jit(solution)/shard_map/ppermute | solution.py:382
  15.2 7.7 %adjoint.5 = (bf16[32,2048]{1,0:T(8,128)(2,1)S(1)}, bf16[32,2048]{1,0:T(8,128)(2,1)S(1)}, bf16[32,2048]{1,0:T(8,128)(2,1)S(1)}, bf16[32,2048]{1,0:T(8,128)(2,1)S(1)}) custom-call(s32[1]{0:T(128)} %bitcast.1.turn_ref.turn, bf16[2,8,320,4096]{3,2,1,0:T(8,128)(2,1)} %k_hbm.11, bf16[8,16,640]{2,1,0:T(8,128)(2,1)S(1)} %get-tuple-element.64.refs_0_), custom_call_target="tpu_custom_call" | custom-call | flops 2684354560 | bytes 20971520 | tf_op jit(solution)/shard_map/adjoint/pallas_call | solution.py:120
  27.3 2.8 %collective-permute-start.4 = (bf16[32,2048]{1,0:T(8,128)(2,1)S(1)}, bf16[32,2048]{1,0:T(8,128)(2,1)S(1)}, u32[]{:S(2)}, u32[]{:S(2)}) collective-permute-start(bf16[32,2048]{1,0:T(8,128)(2,1)S(1)} %get-tuple-element.71), channel_id=1, source_target_pairs={{0,8},{2,10},{4,12},{6,14},{8,0},{10,2},{12,4},{14,6},{1,9},{3,11}... | collective-permute-start | bytes 393224 | tf_op jit(solution)/shard_map/ppermute | solution.py:382
  31.5 7.3 %collective-permute-done.4 = bf16[32,2048]{1,0:T(8,128)(2,1)S(1)} collective-permute-done((bf16[32,2048]{1,0:T(8,128)(2,1)S(1)}, bf16[32,2048]{1,0:T(8,128)(2,1)S(1)}, u32[]{:S(2)}, u32[]{:S(2)}) %collective-permute-start.4) | collective-permute-done | bytes 131104 | tf_op jit(solution)/shard_map/ppermute | solution.py:382
  40.7 2.6 %collective-permute-start.8 = (bf16[32,2048]{1,0:T(8,128)(2,1)S(1)}, bf16[32,2048]{1,0:T(8,128)(2,1)S(1)}, u32[]{:S(2)}, u32[]{:S(2)}) collective-permute-start(bf16[32,2048]{1,0:T(8,128)(2,1)S(1)} %get-tuple-element.79), channel_id=1, source_target_pairs={{0,8},{2,10},{4,12},{6,14},{8,0},{10,2},{12,4},{14,6},{1,9},{3,11}... | collective-permute-start | bytes 393224 | tf_op jit(solution)/shard_map/ppermute | solution.py:382
  45.1 6.1 %collective-permute-done.6.refs_1_ = bf16[128,2048]{1,0:T(8,128)(2,1)S(1)} collective-permute-done((bf16[128,2048]{1,0:T(8,128)(2,1)S(1)}, bf16[128,2048]{1,0:T(8,128)(2,1)S(1)}, u32[]{:S(2)}, u32[]{:S(2)}) %collective-permute-start.6) | collective-permute-done | bytes 524320 | tf_op jit(solution)/shard_map/ppermute | solution.py:382
  51.7 3.4 %collective-permute-start.11 = (bf16[32,2048]{1,0:T(8,128)(2,1)S(1)}, bf16[32,2048]{1,0:T(8,128)(2,1)S(1)}, u32[]{:S(2)}, u32[]{:S(2)}) collective-permute-start(bf16[32,2048]{1,0:T(8,128)(2,1)S(1)} %get-tuple-element.85), channel_id=1, source_target_pairs={{0,4},{2,6},{4,0},{6,2},{8,12},{10,14},{12,8},{14,10},{1,5},{3,7},... | collective-permute-start | bytes 393224 | tf_op jit(solution)/shard_map/ppermute | solution.py:382
  56.6 8.6 %forward.4.init_ref = f32[136,320]{1,0:T(8,128)S(1)} custom-call(s32[1]{0:T(128)} %bitcast.1.turn_ref.turn, bf16[2,8,320,4096]{3,2,1,0:T(8,128)(2,1)} %k_hbm.11, f32[8,128]{1,0:T(8,128)S(1)} %get-tuple-element.76.al, bf16[32,2048]{1,0:T(8,128)(2,1)S(1)} %get-tuple-element.81.rest_0_.refs_1_, bf16[32,2048]{1,0:T(8,128)(2,1)S(1)} %collective-permute-done.9.rest_1_.refs_2_, ...), custom_call_target="tpu_custom_call" | custom-call | flops 2684354560 | bytes 20971520 | tf_op jit(solution)/shard_map/forward/pallas_call | solution.py:209
  66.8 8.5 %forward.5.own_ref = f32[136,320]{1,0:T(8,128)S(1)} custom-call(s32[1]{0:T(128)} %bitcast.1.turn_ref.turn, bf16[2,8,320,4096]{3,2,1,0:T(8,128)(2,1)} %k_hbm.11, f32[8,128]{1,0:T(8,128)S(1)} %get-tuple-element.74.al_ref, f32[136,320]{1,0:T(8,128)S(1)} %forward.4.init_ref, bf16[32,2048]{1,0:T(8,128)(2,1)S(1)} %get-tuple-element.84.refs_0_.refs_9_, ...), custom_call_target="tpu_custom_call" | custom-call | flops 2684354560 | bytes 20971520 | tf_op jit(solution)/shard_map/forward/pallas_call | solution.py:209
  79.3 10.3 %all_to_all.10 = f32[8,16,128]{2,1,0:T(8,128)S(1)} all-to-all(f32[8,16,128]{2,1,0:T(8,128)} %bitcast.32), channel_id=1, replica_groups=mesh['grp'=2,'freq'=8,'src'=2] {'freq'}, dimensions={0} | all-to-all | bytes 131072 | tf_op jit(solution)/shard_map/all_to_all | solution.py:387
  90.5 7.8 %adjoint.6 = (bf16[32,2048]{1,0:T(8,128)(2,1)S(1)}, bf16[32,2048]{1,0:T(8,128)(2,1)S(1)}, bf16[32,2048]{1,0:T(8,128)(2,1)S(1)}, bf16[32,2048]{1,0:T(8,128)(2,1)S...) custom-call(s32[1]{0:T(128)} %bitcast.1.turn_ref.turn, ...), custom_call_target="tpu_custom_call" | custom-call | flops 2684354560 | bytes 20971520 | tf_op jit(solution)/shard_map/adjoint/pallas_call | solution.py:120
  99.5 3.3 %collective-permute-start.17 = (bf16[32,2048]{1,0:T(8,128)(2,1)S(1)}, bf16[32,2048]{1,0:T(8,128)(2,1)S(1)}, u32[]{:S(2)}, u32[]{:S(2)}) collective-permute-start(bf16[32,2048]{1,0:T(8,128)(2,1)S(1)} %get-tuple-element.98), channel_id=1, source_target_pairs={{0,8},{2,10},{4,12},{6,14},{8,0},{10,2},{12,4},{14,6},{1,9},{3,11}... | collective-permute-start | bytes 393224 | tf_op jit(solution)/shard_map/ppermute | solution.py:382
  102.8 7.7 %adjoint.7 = (bf16[32,2048]{1,0:T(8,128)(2,1)S(1)}, bf16[32,2048]{1,0:T(8,128)(2,1)S(1)}, bf16[32,2048]{1,0:T(8,128)(2,1)S(1)}, bf16[32,2048]{1,0:T(8,128)(2,1)S(1)}) custom-call(s32[1]{0:T(128)} %bitcast.1.turn_ref.turn, bf16[2,8,320,4096]{3,2,1,0:T(8,128)(2,1)} %k_hbm.11, bf16[8,16,640]{2,1,0:T(8,128)(2,1)S(1)} %get-tuple-element.92.refs_0_), custom_call_target="tpu_custom_call" | custom-call | flops 2684354560 | bytes 20971520 | tf_op jit(solution)/shard_map/adjoint/pallas_call | solution.py:120
  112.8 2.8 %collective-permute-start.20 = (bf16[32,2048]{1,0:T(8,128)(2,1)S(1)}, bf16[32,2048]{1,0:T(8,128)(2,1)S(1)}, u32[]{:S(2)}, u32[]{:S(2)}) collective-permute-start(bf16[32,2048]{1,0:T(8,128)(2,1)S(1)} %get-tuple-element.101), channel_id=1, source_target_pairs={{0,12},{2,14},{4,8},{6,10},{8,4},{10,6},{12,0},{14,2},{1,13},{3,15... | collective-permute-start | bytes 393224 | tf_op jit(solution)/shard_map/ppermute | solution.py:382
  115.8 6.7 %collective-permute-done.19 = bf16[32,2048]{1,0:T(8,128)(2,1)S(1)} collective-permute-done((bf16[32,2048]{1,0:T(8,128)(2,1)S(1)}, bf16[32,2048]{1,0:T(8,128)(2,1)S(1)}, u32[]{:S(2)}, u32[]{:S(2)}) %collective-permute-start.19) | collective-permute-done | bytes 131104 | tf_op jit(solution)/shard_map/ppermute | solution.py:382
  129.5 4.6 %collective-permute-done.21.refs_1_ = bf16[128,2048]{1,0:T(8,128)(2,1)S(1)} collective-permute-done((bf16[128,2048]{1,0:T(8,128)(2,1)S(1)}, bf16[128,2048]{1,0:T(8,128)(2,1)S(1)}, u32[]{:S(2)}, u32[]{:S(2)}) %collective-permute-start.21) | collective-permute-done | bytes 524320 | tf_op jit(solution)/shard_map/ppermute | solution.py:382
  134.5 3.0 %collective-permute-start.26 = (bf16[32,2048]{1,0:T(8,128)(2,1)S(1)}, bf16[32,2048]{1,0:T(8,128)(2,1)S(1)}, u32[]{:S(2)}, u32[]{:S(2)}) collective-permute-start(bf16[32,2048]{1,0:T(8,128)(2,1)S(1)} %get-tuple-element.113), channel_id=1, source_target_pairs={{0,4},{2,6},{4,0},{6,2},{8,12},{10,14},{12,8},{14,10},{1,5},{3,7},... | collective-permute-start | bytes 393224 | tf_op jit(solution)/shard_map/ppermute | solution.py:382
  140.0 8.5 %forward.6.init_ref = f32[136,320]{1,0:T(8,128)S(1)} custom-call(s32[1]{0:T(128)} %bitcast.1.turn_ref.turn, bf16[2,8,320,4096]{3,2,1,0:T(8,128)(2,1)} %k_hbm.11, f32[8,128]{1,0:T(8,128)S(1)} %get-tuple-element.104.al, bf16[32,2048]{1,0:T(8,128)(2,1)S(1)} %get-tuple-element.109.rest_0_.refs_5_, bf16[32,2048]{1,0:T(8,128)(2,1)S(1)} %collective-permute-done.24.rest_1_.refs_6_, ...), custom_call_target="tpu_custom_call" | custom-call | flops 2684354560 | bytes 20971520 | tf_op jit(solution)/shard_map/forward/pallas_call | solution.py:209
  149.8 8.5 %forward.7.own_ref = f32[136,320]{1,0:T(8,128)S(1)} custom-call(s32[1]{0:T(128)} %bitcast.1.turn_ref.turn, bf16[2,8,320,4096]{3,2,1,0:T(8,128)(2,1)} %k_hbm.11, f32[8,128]{1,0:T(8,128)S(1)} %get-tuple-element.102.al_ref, f32[136,320]{1,0:T(8,128)S(1)} %forward.6.init_ref, bf16[32,2048]{1,0:T(8,128)(2,1)S(1)} %get-tuple-element.112.refs_0_.refs_13_, ...), custom_call_target="tpu_custom_call" | custom-call | flops 2684354560 | bytes 20971520 | tf_op jit(solution)/shard_map/forward/pallas_call | solution.py:209
  162.3 3.8 %all-to-all-start.1 = ((f32[8,16,128]{2,1,0:T(8,128)}), f32[8,16,128]{2,1,0:T(8,128)S(1)}, u32[]{:S(2)}, u32[]{:S(2)}) async-start(f32[8,16,128]{2,1,0:T(8,128)} %bitcast.31), calls=%async_computation.1 | async-start | bytes 131072 | tf_op jit(solution)/shard_map/all_to_all | solution.py:387
  166.1 6.8 %all-to-all-done.1 = f32[8,16,128]{2,1,0:T(8,128)S(1)} async-done(((f32[8,16,128]{2,1,0:T(8,128)}), f32[8,16,128]{2,1,0:T(8,128)S(1)}, u32[]{:S(2)}, u32[]{:S(2)}) %all-to-all-start.1) | async-done | bytes 65568 | tf_op jit(solution)/shard_map/all_to_all | solution.py:387
  173.9 3.6 %finish.1 = (f32[2,8,8,4096]{3,2,1,0:T(8,128)}, f32[2,8,8,160]{3,2,1,0:T(8,128)}) custom-call(s32[3]{0:T(128)S(1)} %pad_add_fusion.place_ref, f32[128,128]{1,0:T(8,128)S(1)} %bitcast.30, f32[128,320]{1,0:T(8,128)S(1)} %copy-done.5, f32[2,8,8,320]{3,2,1,0:T(8,128)S(1)} %get-tuple-element.118.r_ref, f32[8,128]{1,0:T(8,128)S(1)} %get-tuple-element.119.refs_0_, ...), custom_call_target="tpu_custom_call" | custom-call | tf_op jit(solution)/shard_map/finish/pallas_call | solution.py:362
  (101 shorter events, 38.1 us)
Async XLA Ops:
  9.5 15.0 %collective-permute-start.1 = (bf16[32,2048]{1,0:T(8,128)(2,1)S(1)}, bf16[32,2048]{1,0:T(8,128)(2,1)S(1)}, u32[]{:S(2)}, u32[]{:S(2)}) collective-permute-start(bf16[32,2048]{1,0:T(8,128)(2,1)S(1)} %get-tuple-element.69), channel_id=1, source_target_pairs={{0,4},{2,6},{4,0},{6,2},{8,12},{10,14},{12,8},{14,10},{1,5},{3,7},... | collective-permute-start | bytes 393224 | tf_op jit(solution)/shard_map/ppermute | solution.py:382
  12.6 13.0 %collective-permute-start.2 = (bf16[32,2048]{1,0:T(8,128)(2,1)S(1)}, bf16[32,2048]{1,0:T(8,128)(2,1)S(1)}, u32[]{:S(2)}, u32[]{:S(2)}) collective-permute-start(bf16[32,2048]{1,0:T(8,128)(2,1)S(1)} %get-tuple-element.70), channel_id=1, source_target_pairs={{0,8},{2,10},{4,12},{6,14},{8,0},{10,2},{12,4},{14,6},{1,9},{3,11}... | collective-permute-start | bytes 393224 | tf_op jit(solution)/shard_map/ppermute | solution.py:382
  15.2 10.5 %collective-permute-start.3 = (bf16[32,2048]{1,0:T(8,128)(2,1)S(1)}, bf16[32,2048]{1,0:T(8,128)(2,1)S(1)}, u32[]{:S(2)}, u32[]{:S(2)}) collective-permute-start(bf16[32,2048]{1,0:T(8,128)(2,1)S(1)} %get-tuple-element.63), channel_id=1, source_target_pairs={{0,12},{2,14},{4,8},{6,10},{8,4},{10,6},{12,0},{14,2},{1,13},{3,15... | collective-permute-start | bytes 393224 | tf_op jit(solution)/shard_map/ppermute | solution.py:382
  25.7 14.5 %collective-permute-start.7 = (bf16[128,2048]{1,0:T(8,128)(2,1)S(1)}, bf16[128,2048]{1,0:T(8,128)(2,1)S(1)}, u32[]{:S(2)}, u32[]{:S(2)}) collective-permute-start(bf16[128,2048]{1,0:T(8,128)(2,1)S(1)} %constant_dynamic-update-slice_fusion.refs_0_), channel_id=1, source_target_pairs={{0,2},{2,0},{4,6},{6,4},{8,10},{10,8},{12,14},{14,12},{1,3},{3,1},... | collective-permute-start | bytes 1572872 | tf_op jit(solution)/shard_map/ppermute | solution.py:382
  27.3 11.5 %collective-permute-start.4 = (bf16[32,2048]{1,0:T(8,128)(2,1)S(1)}, bf16[32,2048]{1,0:T(8,128)(2,1)S(1)}, u32[]{:S(2)}, u32[]{:S(2)}) collective-permute-start(bf16[32,2048]{1,0:T(8,128)(2,1)S(1)} %get-tuple-element.71), channel_id=1, source_target_pairs={{0,8},{2,10},{4,12},{6,14},{8,0},{10,2},{12,4},{14,6},{1,9},{3,11}... | collective-permute-start | bytes 393224 | tf_op jit(solution)/shard_map/ppermute | solution.py:382
  38.9 12.4 %collective-permute-start.6 = (bf16[128,2048]{1,0:T(8,128)(2,1)S(1)}, bf16[128,2048]{1,0:T(8,128)(2,1)S(1)}, u32[]{:S(2)}, u32[]{:S(2)}) collective-permute-start(bf16[128,2048]{1,0:T(8,128)(2,1)S(1)} %constant_dynamic-update-slice_fusion.4.refs_0_), channel_id=1, source_target_pairs={{0,2},{2,0},{4,6},{6,4},{8,10},{10,8},{12,14},{14,12},{1,3},{3,1},... | collective-permute-start | bytes 1572872 | tf_op jit(solution)/shard_map/ppermute | solution.py:382
  40.7 14.4 %collective-permute-start.8 = (bf16[32,2048]{1,0:T(8,128)(2,1)S(1)}, bf16[32,2048]{1,0:T(8,128)(2,1)S(1)}, u32[]{:S(2)}, u32[]{:S(2)}) collective-permute-start(bf16[32,2048]{1,0:T(8,128)(2,1)S(1)} %get-tuple-element.79), channel_id=1, source_target_pairs={{0,8},{2,10},{4,12},{6,14},{8,0},{10,2},{12,4},{14,6},{1,9},{3,11}... | collective-permute-start | bytes 393224 | tf_op jit(solution)/shard_map/ppermute | solution.py:382
  43.2 13.4 %collective-permute-start.9 = (bf16[32,2048]{1,0:T(8,128)(2,1)S(1)}, bf16[32,2048]{1,0:T(8,128)(2,1)S(1)}, u32[]{:S(2)}, u32[]{:S(2)}) collective-permute-start(bf16[32,2048]{1,0:T(8,128)(2,1)S(1)} %get-tuple-element.82), channel_id=1, source_target_pairs={{0,4},{2,6},{4,0},{6,2},{8,12},{10,14},{12,8},{14,10},{1,5},{3,7},... | collective-permute-start | bytes 393224 | tf_op jit(solution)/shard_map/ppermute | solution.py:382
  43.3 13.3 %collective-permute-start.10 = (bf16[32,2048]{1,0:T(8,128)(2,1)S(1)}, bf16[32,2048]{1,0:T(8,128)(2,1)S(1)}, u32[]{:S(2)}, u32[]{:S(2)}) collective-permute-start(bf16[32,2048]{1,0:T(8,128)(2,1)S(1)} %get-tuple-element.83), channel_id=1, source_target_pairs={{0,12},{2,14},{4,8},{6,10},{8,4},{10,6},{12,0},{14,2},{1,13},{3,15... | collective-permute-start | bytes 393224 | tf_op jit(solution)/shard_map/ppermute | solution.py:382
  51.7 13.6 %collective-permute-start.11 = (bf16[32,2048]{1,0:T(8,128)(2,1)S(1)}, bf16[32,2048]{1,0:T(8,128)(2,1)S(1)}, u32[]{:S(2)}, u32[]{:S(2)}) collective-permute-start(bf16[32,2048]{1,0:T(8,128)(2,1)S(1)} %get-tuple-element.85), channel_id=1, source_target_pairs={{0,4},{2,6},{4,0},{6,2},{8,12},{10,14},{12,8},{14,10},{1,5},{3,7},... | collective-permute-start | bytes 393224 | tf_op jit(solution)/shard_map/ppermute | solution.py:382
  55.1 10.2 %collective-permute-start.13 = (bf16[32,2048]{1,0:T(8,128)(2,1)S(1)}, bf16[32,2048]{1,0:T(8,128)(2,1)S(1)}, u32[]{:S(2)}, u32[]{:S(2)}) collective-permute-start(bf16[32,2048]{1,0:T(8,128)(2,1)S(1)} %get-tuple-element.80), channel_id=1, source_target_pairs={{0,12},{2,14},{4,8},{6,10},{8,4},{10,6},{12,0},{14,2},{1,13},{3,15... | collective-permute-start | bytes 393224 | tf_op jit(solution)/shard_map/ppermute | solution.py:382
  56.0 10.8 %collective-permute-start.12 = (bf16[32,2048]{1,0:T(8,128)(2,1)S(1)}, bf16[32,2048]{1,0:T(8,128)(2,1)S(1)}, u32[]{:S(2)}, u32[]{:S(2)}) collective-permute-start(bf16[32,2048]{1,0:T(8,128)(2,1)S(1)} %get-tuple-element.87), channel_id=1, source_target_pairs={{0,8},{2,10},{4,12},{6,14},{8,0},{10,2},{12,4},{14,6},{1,9},{3,11}... | collective-permute-start | bytes 393224 | tf_op jit(solution)/shard_map/ppermute | solution.py:382
  98.4 13.1 %collective-permute-start.18 = (bf16[32,2048]{1,0:T(8,128)(2,1)S(1)}, bf16[32,2048]{1,0:T(8,128)(2,1)S(1)}, u32[]{:S(2)}, u32[]{:S(2)}) collective-permute-start(bf16[32,2048]{1,0:T(8,128)(2,1)S(1)} %get-tuple-element.91), channel_id=1, source_target_pairs={{0,12},{2,14},{4,8},{6,10},{8,4},{10,6},{12,0},{14,2},{1,13},{3,15... | collective-permute-start | bytes 393224 | tf_op jit(solution)/shard_map/ppermute | solution.py:382
  99.0 11.7 %collective-permute-start.16 = (bf16[32,2048]{1,0:T(8,128)(2,1)S(1)}, bf16[32,2048]{1,0:T(8,128)(2,1)S(1)}, u32[]{:S(2)}, u32[]{:S(2)}) collective-permute-start(bf16[32,2048]{1,0:T(8,128)(2,1)S(1)} %get-tuple-element.97), channel_id=1, source_target_pairs={{0,4},{2,6},{4,0},{6,2},{8,12},{10,14},{12,8},{14,10},{1,5},{3,7},... | collective-permute-start | bytes 393224 | tf_op jit(solution)/shard_map/ppermute | solution.py:382
  99.5 12.0 %collective-permute-start.17 = (bf16[32,2048]{1,0:T(8,128)(2,1)S(1)}, bf16[32,2048]{1,0:T(8,128)(2,1)S(1)}, u32[]{:S(2)}, u32[]{:S(2)}) collective-permute-start(bf16[32,2048]{1,0:T(8,128)(2,1)S(1)} %get-tuple-element.98), channel_id=1, source_target_pairs={{0,8},{2,10},{4,12},{6,14},{8,0},{10,2},{12,4},{14,6},{1,9},{3,11}... | collective-permute-start | bytes 393224 | tf_op jit(solution)/shard_map/ppermute | solution.py:382
  111.5 13.1 %collective-permute-start.22 = (bf16[128,2048]{1,0:T(8,128)(2,1)S(1)}, bf16[128,2048]{1,0:T(8,128)(2,1)S(1)}, u32[]{:S(2)}, u32[]{:S(2)}) collective-permute-start(bf16[128,2048]{1,0:T(8,128)(2,1)S(1)} %constant_dynamic-update-slice_fusion.8.refs_0_), channel_id=1, source_target_pairs={{0,2},{2,0},{4,6},{6,4},{8,10},{10,8},{12,14},{14,12},{1,3},{3,1},... | collective-permute-start | bytes 1572872 | tf_op jit(solution)/shard_map/ppermute | solution.py:382
  112.1 10.4 %collective-permute-start.19 = (bf16[32,2048]{1,0:T(8,128)(2,1)S(1)}, bf16[32,2048]{1,0:T(8,128)(2,1)S(1)}, u32[]{:S(2)}, u32[]{:S(2)}) collective-permute-start(bf16[32,2048]{1,0:T(8,128)(2,1)S(1)} %get-tuple-element.99), channel_id=1, source_target_pairs={{0,8},{2,10},{4,12},{6,14},{8,0},{10,2},{12,4},{14,6},{1,9},{3,11}... | collective-permute-start | bytes 393224 | tf_op jit(solution)/shard_map/ppermute | solution.py:382
  122.5 11.6 %collective-permute-start.21 = (bf16[128,2048]{1,0:T(8,128)(2,1)S(1)}, bf16[128,2048]{1,0:T(8,128)(2,1)S(1)}, u32[]{:S(2)}, u32[]{:S(2)}) collective-permute-start(bf16[128,2048]{1,0:T(8,128)(2,1)S(1)} %constant_dynamic-update-slice_fusion.12.refs_0_), channel_id=1, source_target_pairs={{0,2},{2,0},{4,6},{6,4},{8,10},{10,8},{12,14},{14,12},{1,3},{3,1},... | collective-permute-start | bytes 1572872 | tf_op jit(solution)/shard_map/ppermute | solution.py:382
  125.0 12.5 %collective-permute-start.23 = (bf16[32,2048]{1,0:T(8,128)(2,1)S(1)}, bf16[32,2048]{1,0:T(8,128)(2,1)S(1)}, u32[]{:S(2)}, u32[]{:S(2)}) collective-permute-start(bf16[32,2048]{1,0:T(8,128)(2,1)S(1)} %get-tuple-element.107), channel_id=1, source_target_pairs={{0,8},{2,10},{4,12},{6,14},{8,0},{10,2},{12,4},{14,6},{1,9},{3,11}... | collective-permute-start | bytes 393224 | tf_op jit(solution)/shard_map/ppermute | solution.py:382
  127.1 12.9 %collective-permute-start.24 = (bf16[32,2048]{1,0:T(8,128)(2,1)S(1)}, bf16[32,2048]{1,0:T(8,128)(2,1)S(1)}, u32[]{:S(2)}, u32[]{:S(2)}) collective-permute-start(bf16[32,2048]{1,0:T(8,128)(2,1)S(1)} %get-tuple-element.110), channel_id=1, source_target_pairs={{0,4},{2,6},{4,0},{6,2},{8,12},{10,14},{12,8},{14,10},{1,5},{3,7},... | collective-permute-start | bytes 393224 | tf_op jit(solution)/shard_map/ppermute | solution.py:382
  128.6 11.4 %collective-permute-start.25 = (bf16[32,2048]{1,0:T(8,128)(2,1)S(1)}, bf16[32,2048]{1,0:T(8,128)(2,1)S(1)}, u32[]{:S(2)}, u32[]{:S(2)}) collective-permute-start(bf16[32,2048]{1,0:T(8,128)(2,1)S(1)} %get-tuple-element.111), channel_id=1, source_target_pairs={{0,12},{2,14},{4,8},{6,10},{8,4},{10,6},{12,0},{14,2},{1,13},{3,15... | collective-permute-start | bytes 393224 | tf_op jit(solution)/shard_map/ppermute | solution.py:382
  134.5 14.0 %collective-permute-start.26 = (bf16[32,2048]{1,0:T(8,128)(2,1)S(1)}, bf16[32,2048]{1,0:T(8,128)(2,1)S(1)}, u32[]{:S(2)}, u32[]{:S(2)}) collective-permute-start(bf16[32,2048]{1,0:T(8,128)(2,1)S(1)} %get-tuple-element.113), channel_id=1, source_target_pairs={{0,4},{2,6},{4,0},{6,2},{8,12},{10,14},{12,8},{14,10},{1,5},{3,7},... | collective-permute-start | bytes 393224 | tf_op jit(solution)/shard_map/ppermute | solution.py:382
  137.6 11.0 %collective-permute-start.28 = (bf16[32,2048]{1,0:T(8,128)(2,1)S(1)}, bf16[32,2048]{1,0:T(8,128)(2,1)S(1)}, u32[]{:S(2)}, u32[]{:S(2)}) collective-permute-start(bf16[32,2048]{1,0:T(8,128)(2,1)S(1)} %get-tuple-element.108), channel_id=1, source_target_pairs={{0,12},{2,14},{4,8},{6,10},{8,4},{10,6},{12,0},{14,2},{1,13},{3,15... | collective-permute-start | bytes 393224 | tf_op jit(solution)/shard_map/ppermute | solution.py:382
  162.3 10.7 %all-to-all-start.1 = ((f32[8,16,128]{2,1,0:T(8,128)}), f32[8,16,128]{2,1,0:T(8,128)S(1)}, u32[]{:S(2)}, u32[]{:S(2)}) async-start(f32[8,16,128]{2,1,0:T(8,128)} %bitcast.31), calls=%async_computation.1 | async-start | bytes 131072 | tf_op jit(solution)/shard_map/all_to_all | solution.py:387
  (18 other events, 152.5 us)

commit v7 on v6

--- a/solution.py
+++ b/solution.py
@@ -281,9 +281,9 @@
         squares = jnp.concatenate([squares, jnp.zeros((8, pad), F32)], 1)
     curvature = sum(squares[:, j : j + LANES] for j in range(0, receivers + pad, LANES))
     alignment = own_ref[size:, :LANES] + got_ref[size:, :LANES]
-    for at in range(0, sums_ref.shape[0], 16):
-        sums_ref[at : at + 8] = alignment
-        sums_ref[at + 8 : at + 16] = curvature
+    both = jnp.concatenate([alignment[:4] + alignment[4:], curvature[:4] + curvature[4:]], 0)
+    for at in range(0, sums_ref.shape[0], 8):
+        sums_ref[at : at + 8] = both
 
 
 def merge(own, got, count):
@@ -292,7 +292,7 @@
         merge_body,
         in_specs=[in_vmem()] * 2,
         out_specs=[in_vmem()] * 2,
-        out_shape=[jax.ShapeDtypeStruct((size - 8, receivers), F32), jax.ShapeDtypeStruct((16 * count, LANES), F32)],
+        out_shape=[jax.ShapeDtypeStruct((size - 8, receivers), F32), jax.ShapeDtypeStruct((8 * count, LANES), F32)],
         name="merge",
     )(own, got)
 
@@ -310,8 +310,8 @@
 
 
 def step_length(s_ref):
-    sums = sum(s_ref[at : at + 16] for at in range(0, s_ref.shape[0], 16))
-    return jnp.sum(sums[0:8], keepdims=True) / jnp.sum(sums[8:16], keepdims=True)
+    sums = sum(s_ref[at : at + 8] for at in range(0, s_ref.shape[0], 8))
+    return jnp.sum(sums[0:4], keepdims=True) / jnp.sum(sums[4:8], keepdims=True)
 
 
 def finish_body(place_ref, s_ref, p_ref, r_ref, *refs, spans, pieces):
@@ -475,7 +475,7 @@
             stage, ins = "rest", [then(lhs, gradient[-1])]
             gradients.append(gradient)
             if gathered and mode == "relay":
-                gradient = list(gradient[:2]) + [then(x, gathered[-1][0]) for x in gradient[2:]]
+                gradient = list(gradient[:2]) + [then(x, gathered[-1][0]) for x in gradient[2:3]] + list(gradient[3:])
             gathered.append(pair_up(scatter(gradient, mode), mode))
         for n, (_, _, mode) in enumerate(parts):
             got = gathered[n]
@@ -493,7 +493,7 @@
             fields[-1].append(field)
         got = swap(image) if src_count == 2 else lax.psum(image, "src") - image
         projected, sums = merge(image, got, count)
-        sums = exchange(sums, 16)
+        sums = exchange(sums, 8)
     spans = [(base, width) for base, width, _ in parts]
     turns = [turn_of(mode) for _, _, mode in parts]
     core = lax.axis_index("src").reshape(1).astype(jnp.int32)

time: 178 us -> 177 us (level)
  starting transfers between devices: 46.9 us -> 43.2 us
  waiting for transfers between devices: 39.8 us -> 43.1 us
    ppermute x28, starting transfers between devices: 43 us -> 39.1 us  [send(): lax.ppermute(x, 'freq', [(i, i ^ hop) for i in range(lax.axis_size('freq'...]
    ppermute x28, waiting for transfers between devices: 30.1 us -> 33.6 us  [send(): lax.ppermute(x, 'freq', [(i, i ^ hop) for i in range(lax.axis_size('freq'...]
  transfers between devices with their start and end apart: 31 -> 31, of which waited for: 13 -> 11; matrix products, arithmetic and copies ran while one was open for 1% -> 1% of each run, Pallas kernels for 19% -> 19%
where the time goes in v7:
time: 177 us
  Pallas kernels  74.2 us (42%)
  starting transfers between devices  43.2 us (24%)
  waiting for transfers between devices  43.1 us (24%)
  blocking collectives  9.93 us (6%)
  local copies, waits for them, and re-layouts  4.79 us (3%)
    ppermute x28, starting transfers between devices, send(): lax.ppermute(x, 'freq', [(i, i ^ hop) for i in range(lax.axis_size('freq'...  39.1 us
    pallas_call x4, Pallas kernels, forward(): pl.pallas_call(body, in_specs=specs + [in_vmem()] * (len(start) + pieces)...  34.1 us
    ppermute x28, waiting for transfers between devices, send(): lax.ppermute(x, 'freq', [(i, i ^ hop) for i in range(lax.axis_size('freq'...  33.6 us
    pallas_call x4, Pallas kernels, adjoint(): pl.pallas_call(functools.partial(adjoint_body, pieces=pieces, points=poin...  31.2 us
    all_to_all x1, blocking collectives, exchange(): lax.all_to_all(x.reshape(-1, rows, width), 'freq', 0, 0, tiled=True)  9.93 us
    all_to_all x1, waiting for transfers between devices, exchange(): lax.all_to_all(x.reshape(-1, rows, width), 'freq', 0, 0, tiled=True)  6.61 us
    unnamed x34, local copies, waits for them, and re-layouts  4.31 us
    all_to_all x1, starting transfers between devices, exchange(): lax.all_to_all(x.reshape(-1, rows, width), 'freq', 0, 0, tiled=True)  3.93 us
  transfers between devices with their start and end apart: 31, of which 11 were waited for; matrix products, arithmetic and copies ran while one was open for 1% of the time, Pallas kernels for 19%

profile of v7, /device:TPU:0, one launch (start us, length us, event | category | flops | bytes accessed | tf_op | source)
XLA Modules:
  0.0 176.7 jit_solution(17084680108584287853)
XLA Ops:
  1.6 7.9 %adjoint.4 = (bf16[32,2048]{1,0:T(8,128)(2,1)S(1)}, bf16[32,2048]{1,0:T(8,128)(2,1)S(1)}, bf16[32,2048]{1,0:T(8,128)(2,1)S(1)}, bf16[32,2048]{1,0:T(8,128)(2,1)S(1)}, bf16[8,16,640]{2,1,0:T(8,128)(2,1)S(1)}) custom-call(s32[1]{0:T(128)} %bitcast.1.turn_ref.turn, bf16[2,8,320,4096]{3,2,1,0:T(8,128)(2,1)} %k_hbm.11, f32[2,8,8,320]{3,2,1,0:T(8,128)S(1)} %bitcast.27), custom_call_target="tpu_custom_call" | custom-call | flops 2684354560 | bytes 20971520 | tf_op jit(solution)/shard_map/adjoint/pallas_call | solution.py:120
  9.5 3.1 %collective-permute-start.1 = (bf16[32,2048]{1,0:T(8,128)(2,1)S(1)}, bf16[32,2048]{1,0:T(8,128)(2,1)S(1)}, u32[]{:S(2)}, u32[]{:S(2)}) collective-permute-start(bf16[32,2048]{1,0:T(8,128)(2,1)S(1)} %get-tuple-element.67), channel_id=1, source_target_pairs={{0,4},{2,6},{4,0},{6,2},{8,12},{10,14},{12,8},{14,10},{1,5},{3,7},... | collective-permute-start | bytes 393224 | tf_op jit(solution)/shard_map/ppermute | solution.py:382
  12.6 2.6 %collective-permute-start.2 = (bf16[32,2048]{1,0:T(8,128)(2,1)S(1)}, bf16[32,2048]{1,0:T(8,128)(2,1)S(1)}, u32[]{:S(2)}, u32[]{:S(2)}) collective-permute-start(bf16[32,2048]{1,0:T(8,128)(2,1)S(1)} %get-tuple-element.68), channel_id=1, source_target_pairs={{0,8},{2,10},{4,12},{6,14},{8,0},{10,2},{12,4},{14,6},{1,9},{3,11}... | collective-permute-start | bytes 393224 | tf_op jit(solution)/shard_map/ppermute | solution.py:382
  15.2 7.7 %adjoint.5 = (bf16[32,2048]{1,0:T(8,128)(2,1)S(1)}, bf16[32,2048]{1,0:T(8,128)(2,1)S(1)}, bf16[32,2048]{1,0:T(8,128)(2,1)S(1)}, bf16[32,2048]{1,0:T(8,128)(2,1)S(1)}) custom-call(s32[1]{0:T(128)} %bitcast.1.turn_ref.turn, bf16[2,8,320,4096]{3,2,1,0:T(8,128)(2,1)} %k_hbm.11, bf16[8,16,640]{2,1,0:T(8,128)(2,1)S(1)} %get-tuple-element.62.refs_0_), custom_call_target="tpu_custom_call" | custom-call | flops 2684354560 | bytes 20971520 | tf_op jit(solution)/shard_map/adjoint/pallas_call | solution.py:120
  23.9 3.0 %collective-permute-start.5 = (bf16[32,2048]{1,0:T(8,128)(2,1)S(1)}, bf16[32,2048]{1,0:T(8,128)(2,1)S(1)}, u32[]{:S(2)}, u32[]{:S(2)}) collective-permute-start(bf16[32,2048]{1,0:T(8,128)(2,1)S(1)} %get-tuple-element.70), channel_id=1, source_target_pairs={{0,12},{2,14},{4,8},{6,10},{8,4},{10,6},{12,0},{14,2},{1,13},{3,15... | collective-permute-start | bytes 393224 | tf_op jit(solution)/shard_map/ppermute | solution.py:382
  30.1 8.1 %collective-permute-done.4 = bf16[32,2048]{1,0:T(8,128)(2,1)S(1)} collective-permute-done((bf16[32,2048]{1,0:T(8,128)(2,1)S(1)}, bf16[32,2048]{1,0:T(8,128)(2,1)S(1)}, u32[]{:S(2)}, u32[]{:S(2)}) %collective-permute-start.4) | collective-permute-done | bytes 131104 | tf_op jit(solution)/shard_map/ppermute | solution.py:382
  45.3 6.8 %collective-permute-done.6.refs_1_ = bf16[128,2048]{1,0:T(8,128)(2,1)S(1)} collective-permute-done((bf16[128,2048]{1,0:T(8,128)(2,1)S(1)}, bf16[128,2048]{1,0:T(8,128)(2,1)S(1)}, u32[]{:S(2)}, u32[]{:S(2)}) %collective-permute-start.6) | collective-permute-done | bytes 524320 | tf_op jit(solution)/shard_map/ppermute | solution.py:382
  56.1 8.6 %forward.4.init_ref = f32[136,320]{1,0:T(8,128)S(1)} custom-call(s32[1]{0:T(128)} %bitcast.1.turn_ref.turn, bf16[2,8,320,4096]{3,2,1,0:T(8,128)(2,1)} %k_hbm.11, f32[8,128]{1,0:T(8,128)S(1)} %get-tuple-element.73.al, bf16[32,2048]{1,0:T(8,128)(2,1)S(1)} %get-tuple-element.78.rest_0_.refs_1_, bf16[32,2048]{1,0:T(8,128)(2,1)S(1)} %collective-permute-done.9.rest_1_.refs_2_, ...), custom_call_target="tpu_custom_call" | custom-call | flops 2684354560 | bytes 20971520 | tf_op jit(solution)/shard_map/forward/pallas_call | solution.py:209
  66.7 8.5 %forward.5.own_ref = f32[136,320]{1,0:T(8,128)S(1)} custom-call(s32[1]{0:T(128)} %bitcast.1.turn_ref.turn, bf16[2,8,320,4096]{3,2,1,0:T(8,128)(2,1)} %k_hbm.11, f32[8,128]{1,0:T(8,128)S(1)} %get-tuple-element.71.al_ref, f32[136,320]{1,0:T(8,128)S(1)} %forward.4.init_ref, bf16[32,2048]{1,0:T(8,128)(2,1)S(1)} %get-tuple-element.81.refs_0_.refs_9_, ...), custom_call_target="tpu_custom_call" | custom-call | flops 2684354560 | bytes 20971520 | tf_op jit(solution)/shard_map/forward/pallas_call | solution.py:209
  79.2 9.9 %all_to_all.10 = f32[8,8,128]{2,1,0:T(8,128)S(1)} all-to-all(f32[8,8,128]{2,1,0:T(8,128)} %bitcast.32), channel_id=1, replica_groups=mesh['grp'=2,'freq'=8,'src'=2] {'freq'}, dimensions={0} | all-to-all | bytes 65536 | tf_op jit(solution)/shard_map/all_to_all | solution.py:387
  90.0 7.8 %adjoint.6 = (bf16[32,2048]{1,0:T(8,128)(2,1)S(1)}, bf16[32,2048]{1,0:T(8,128)(2,1)S(1)}, bf16[32,2048]{1,0:T(8,128)(2,1)S(1)}, bf16[32,2048]{1,0:T(8,128)(2,1)S...) custom-call(s32[1]{0:T(128)} %bitcast.1.turn_ref.turn, ...), custom_call_target="tpu_custom_call" | custom-call | flops 2684354560 | bytes 20971520 | tf_op jit(solution)/shard_map/adjoint/pallas_call | solution.py:120
  99.0 3.3 %collective-permute-start.17 = (bf16[32,2048]{1,0:T(8,128)(2,1)S(1)}, bf16[32,2048]{1,0:T(8,128)(2,1)S(1)}, u32[]{:S(2)}, u32[]{:S(2)}) collective-permute-start(bf16[32,2048]{1,0:T(8,128)(2,1)S(1)} %get-tuple-element.95), channel_id=1, source_target_pairs={{0,8},{2,10},{4,12},{6,14},{8,0},{10,2},{12,4},{14,6},{1,9},{3,11}... | collective-permute-start | bytes 393224 | tf_op jit(solution)/shard_map/ppermute | solution.py:382
  102.3 7.7 %adjoint.7 = (bf16[32,2048]{1,0:T(8,128)(2,1)S(1)}, bf16[32,2048]{1,0:T(8,128)(2,1)S(1)}, bf16[32,2048]{1,0:T(8,128)(2,1)S(1)}, bf16[32,2048]{1,0:T(8,128)(2,1)S(1)}) custom-call(s32[1]{0:T(128)} %bitcast.1.turn_ref.turn, bf16[2,8,320,4096]{3,2,1,0:T(8,128)(2,1)} %k_hbm.11, bf16[8,16,640]{2,1,0:T(8,128)(2,1)S(1)} %get-tuple-element.89.refs_0_), custom_call_target="tpu_custom_call" | custom-call | flops 2684354560 | bytes 20971520 | tf_op jit(solution)/shard_map/adjoint/pallas_call | solution.py:120
  112.2 2.0 %collective-permute-start.19 = (bf16[32,2048]{1,0:T(8,128)(2,1)S(1)}, bf16[32,2048]{1,0:T(8,128)(2,1)S(1)}, u32[]{:S(2)}, u32[]{:S(2)}) collective-permute-start(bf16[32,2048]{1,0:T(8,128)(2,1)S(1)} %get-tuple-element.96), channel_id=1, source_target_pairs={{0,8},{2,10},{4,12},{6,14},{8,0},{10,2},{12,4},{14,6},{1,9},{3,11}... | collective-permute-start | bytes 393224 | tf_op jit(solution)/shard_map/ppermute | solution.py:382
  114.3 2.8 %collective-permute-done.15 = bf16[32,2048]{1,0:T(8,128)(2,1)S(1)} collective-permute-done((bf16[32,2048]{1,0:T(8,128)(2,1)S(1)}, bf16[32,2048]{1,0:T(8,128)(2,1)S(1)}, u32[]{:S(2)}, u32[]{:S(2)}) %collective-permute-start.15) | collective-permute-done | bytes 131104 | tf_op jit(solution)/shard_map/ppermute | solution.py:382
  117.0 6.2 %collective-permute-done.19 = bf16[32,2048]{1,0:T(8,128)(2,1)S(1)} collective-permute-done((bf16[32,2048]{1,0:T(8,128)(2,1)S(1)}, bf16[32,2048]{1,0:T(8,128)(2,1)S(1)}, u32[]{:S(2)}, u32[]{:S(2)}) %collective-permute-start.19) | collective-permute-done | bytes 131104 | tf_op jit(solution)/shard_map/ppermute | solution.py:382
  124.5 2.5 %collective-permute-start.23 = (bf16[32,2048]{1,0:T(8,128)(2,1)S(1)}, bf16[32,2048]{1,0:T(8,128)(2,1)S(1)}, u32[]{:S(2)}, u32[]{:S(2)}) collective-permute-start(bf16[32,2048]{1,0:T(8,128)(2,1)S(1)} %get-tuple-element.103), channel_id=1, source_target_pairs={{0,8},{2,10},{4,12},{6,14},{8,0},{10,2},{12,4},{14,6},{1,9},{3,11}... | collective-permute-start | bytes 393224 | tf_op jit(solution)/shard_map/ppermute | solution.py:382
  129.0 6.2 %collective-permute-done.21.refs_1_ = bf16[128,2048]{1,0:T(8,128)(2,1)S(1)} collective-permute-done((bf16[128,2048]{1,0:T(8,128)(2,1)S(1)}, bf16[128,2048]{1,0:T(8,128)(2,1)S(1)}, u32[]{:S(2)}, u32[]{:S(2)}) %collective-permute-start.21) | collective-permute-done | bytes 524320 | tf_op jit(solution)/shard_map/ppermute | solution.py:382
  135.8 2.7 %collective-permute-start.28 = (bf16[32,2048]{1,0:T(8,128)(2,1)S(1)}, bf16[32,2048]{1,0:T(8,128)(2,1)S(1)}, u32[]{:S(2)}, u32[]{:S(2)}) collective-permute-start(bf16[32,2048]{1,0:T(8,128)(2,1)S(1)} %get-tuple-element.104), channel_id=1, source_target_pairs={{0,12},{2,14},{4,8},{6,10},{8,4},{10,6},{12,0},{14,2},{1,13},{3,15... | collective-permute-start | bytes 393224 | tf_op jit(solution)/shard_map/ppermute | solution.py:382
  139.2 8.5 %forward.6.init_ref = f32[136,320]{1,0:T(8,128)S(1)} custom-call(s32[1]{0:T(128)} %bitcast.1.turn_ref.turn, bf16[2,8,320,4096]{3,2,1,0:T(8,128)(2,1)} %k_hbm.11, f32[8,128]{1,0:T(8,128)S(1)} %get-tuple-element.100.al, bf16[32,2048]{1,0:T(8,128)(2,1)S(1)} %get-tuple-element.105.rest_0_.refs_5_, bf16[32,2048]{1,0:T(8,128)(2,1)S(1)} %collective-permute-done.24.rest_1_.refs_6_, ...), custom_call_target="tpu_custom_call" | custom-call | flops 2684354560 | bytes 20971520 | tf_op jit(solution)/shard_map/forward/pallas_call | solution.py:209
  149.1 8.5 %forward.7.own_ref = f32[136,320]{1,0:T(8,128)S(1)} custom-call(s32[1]{0:T(128)} %bitcast.1.turn_ref.turn, bf16[2,8,320,4096]{3,2,1,0:T(8,128)(2,1)} %k_hbm.11, f32[8,128]{1,0:T(8,128)S(1)} %get-tuple-element.98.al_ref, f32[136,320]{1,0:T(8,128)S(1)} %forward.6.init_ref, bf16[32,2048]{1,0:T(8,128)(2,1)S(1)} %get-tuple-element.108.refs_0_.refs_13_, ...), custom_call_target="tpu_custom_call" | custom-call | flops 2684354560 | bytes 20971520 | tf_op jit(solution)/shard_map/forward/pallas_call | solution.py:209
  161.6 3.9 %all-to-all-start.1 = ((f32[8,8,128]{2,1,0:T(8,128)}), f32[8,8,128]{2,1,0:T(8,128)S(1)}, u32[]{:S(2)}, u32[]{:S(2)}) async-start(f32[8,8,128]{2,1,0:T(8,128)} %bitcast.31), calls=%async_computation.1 | async-start | bytes 65536 | tf_op jit(solution)/shard_map/all_to_all | solution.py:387
  165.6 6.6 %all-to-all-done.1 = f32[8,8,128]{2,1,0:T(8,128)S(1)} async-done(((f32[8,8,128]{2,1,0:T(8,128)}), f32[8,8,128]{2,1,0:T(8,128)S(1)}, u32[]{:S(2)}, u32[]{:S(2)}) %all-to-all-start.1) | async-done | bytes 32800 | tf_op jit(solution)/shard_map/all_to_all | solution.py:387
  173.1 3.6 %finish.1 = (f32[2,8,8,4096]{3,2,1,0:T(8,128)}, f32[2,8,8,160]{3,2,1,0:T(8,128)}) custom-call(s32[3]{0:T(128)S(1)} %pad_add_fusion.place_ref, f32[64,128]{1,0:T(8,128)S(1)} %bitcast.29, f32[128,320]{1,0:T(8,128)S(1)} %copy-done.5, f32[2,8,8,320]{3,2,1,0:T(8,128)S(1)} %get-tuple-element.114.r_ref, f32[8,128]{1,0:T(8,128)S(1)} %get-tuple-element.115.refs_0_, ...), custom_call_target="tpu_custom_call" | custom-call | tf_op jit(solution)/shard_map/finish/pallas_call | solution.py:362
  (101 shorter events, 36.9 us)
Async XLA Ops:
  9.5 18.0 %collective-permute-start.1 = (bf16[32,2048]{1,0:T(8,128)(2,1)S(1)}, bf16[32,2048]{1,0:T(8,128)(2,1)S(1)}, u32[]{:S(2)}, u32[]{:S(2)}) collective-permute-start(bf16[32,2048]{1,0:T(8,128)(2,1)S(1)} %get-tuple-element.67), channel_id=1, source_target_pairs={{0,4},{2,6},{4,0},{6,2},{8,12},{10,14},{12,8},{14,10},{1,5},{3,7},... | collective-permute-start | bytes 393224 | tf_op jit(solution)/shard_map/ppermute | solution.py:382
  12.6 15.0 %collective-permute-start.2 = (bf16[32,2048]{1,0:T(8,128)(2,1)S(1)}, bf16[32,2048]{1,0:T(8,128)(2,1)S(1)}, u32[]{:S(2)}, u32[]{:S(2)}) collective-permute-start(bf16[32,2048]{1,0:T(8,128)(2,1)S(1)} %get-tuple-element.68), channel_id=1, source_target_pairs={{0,8},{2,10},{4,12},{6,14},{8,0},{10,2},{12,4},{14,6},{1,9},{3,11}... | collective-permute-start | bytes 393224 | tf_op jit(solution)/shard_map/ppermute | solution.py:382
  15.2 12.4 %collective-permute-start.3 = (bf16[32,2048]{1,0:T(8,128)(2,1)S(1)}, bf16[32,2048]{1,0:T(8,128)(2,1)S(1)}, u32[]{:S(2)}, u32[]{:S(2)}) collective-permute-start(bf16[32,2048]{1,0:T(8,128)(2,1)S(1)} %get-tuple-element.61), channel_id=1, source_target_pairs={{0,12},{2,14},{4,8},{6,10},{8,4},{10,6},{12,0},{14,2},{1,13},{3,15... | collective-permute-start | bytes 393224 | tf_op jit(solution)/shard_map/ppermute | solution.py:382
  23.9 14.3 %collective-permute-start.5 = (bf16[32,2048]{1,0:T(8,128)(2,1)S(1)}, bf16[32,2048]{1,0:T(8,128)(2,1)S(1)}, u32[]{:S(2)}, u32[]{:S(2)}) collective-permute-start(bf16[32,2048]{1,0:T(8,128)(2,1)S(1)} %get-tuple-element.70), channel_id=1, source_target_pairs={{0,12},{2,14},{4,8},{6,10},{8,4},{10,6},{12,0},{14,2},{1,13},{3,15... | collective-permute-start | bytes 393224 | tf_op jit(solution)/shard_map/ppermute | solution.py:382
  27.7 12.6 %collective-permute-start.7 = (bf16[128,2048]{1,0:T(8,128)(2,1)S(1)}, bf16[128,2048]{1,0:T(8,128)(2,1)S(1)}, u32[]{:S(2)}, u32[]{:S(2)}) collective-permute-start(bf16[128,2048]{1,0:T(8,128)(2,1)S(1)} %constant_dynamic-update-slice_fusion.refs_0_), channel_id=1, source_target_pairs={{0,2},{2,0},{4,6},{6,4},{8,10},{10,8},{12,14},{14,12},{1,3},{3,1},... | collective-permute-start | bytes 1572872 | tf_op jit(solution)/shard_map/ppermute | solution.py:382
  38.3 13.8 %collective-permute-start.6 = (bf16[128,2048]{1,0:T(8,128)(2,1)S(1)}, bf16[128,2048]{1,0:T(8,128)(2,1)S(1)}, u32[]{:S(2)}, u32[]{:S(2)}) collective-permute-start(bf16[128,2048]{1,0:T(8,128)(2,1)S(1)} %constant_dynamic-update-slice_fusion.4.refs_0_), channel_id=1, source_target_pairs={{0,2},{2,0},{4,6},{6,4},{8,10},{10,8},{12,14},{14,12},{1,3},{3,1},... | collective-permute-start | bytes 1572872 | tf_op jit(solution)/shard_map/ppermute | solution.py:382
  40.7 12.1 %collective-permute-start.8 = (bf16[32,2048]{1,0:T(8,128)(2,1)S(1)}, bf16[32,2048]{1,0:T(8,128)(2,1)S(1)}, u32[]{:S(2)}, u32[]{:S(2)}) collective-permute-start(bf16[32,2048]{1,0:T(8,128)(2,1)S(1)} %get-tuple-element.76), channel_id=1, source_target_pairs={{0,8},{2,10},{4,12},{6,14},{8,0},{10,2},{12,4},{14,6},{1,9},{3,11}... | collective-permute-start | bytes 393224 | tf_op jit(solution)/shard_map/ppermute | solution.py:382
  42.7 13.4 %collective-permute-start.9 = (bf16[32,2048]{1,0:T(8,128)(2,1)S(1)}, bf16[32,2048]{1,0:T(8,128)(2,1)S(1)}, u32[]{:S(2)}, u32[]{:S(2)}) collective-permute-start(bf16[32,2048]{1,0:T(8,128)(2,1)S(1)} %get-tuple-element.79), channel_id=1, source_target_pairs={{0,4},{2,6},{4,0},{6,2},{8,12},{10,14},{12,8},{14,10},{1,5},{3,7},... | collective-permute-start | bytes 393224 | tf_op jit(solution)/shard_map/ppermute | solution.py:382
  43.9 12.2 %collective-permute-start.10 = (bf16[32,2048]{1,0:T(8,128)(2,1)S(1)}, bf16[32,2048]{1,0:T(8,128)(2,1)S(1)}, u32[]{:S(2)}, u32[]{:S(2)}) collective-permute-start(bf16[32,2048]{1,0:T(8,128)(2,1)S(1)} %get-tuple-element.80), channel_id=1, source_target_pairs={{0,12},{2,14},{4,8},{6,10},{8,4},{10,6},{12,0},{14,2},{1,13},{3,15... | collective-permute-start | bytes 393224 | tf_op jit(solution)/shard_map/ppermute | solution.py:382
  52.5 12.1 %collective-permute-start.11 = (bf16[32,2048]{1,0:T(8,128)(2,1)S(1)}, bf16[32,2048]{1,0:T(8,128)(2,1)S(1)}, u32[]{:S(2)}, u32[]{:S(2)}) collective-permute-start(bf16[32,2048]{1,0:T(8,128)(2,1)S(1)} %get-tuple-element.82), channel_id=1, source_target_pairs={{0,4},{2,6},{4,0},{6,2},{8,12},{10,14},{12,8},{14,10},{1,5},{3,7},... | collective-permute-start | bytes 393224 | tf_op jit(solution)/shard_map/ppermute | solution.py:382
  52.8 11.9 %collective-permute-start.13 = (bf16[32,2048]{1,0:T(8,128)(2,1)S(1)}, bf16[32,2048]{1,0:T(8,128)(2,1)S(1)}, u32[]{:S(2)}, u32[]{:S(2)}) collective-permute-start(bf16[32,2048]{1,0:T(8,128)(2,1)S(1)} %get-tuple-element.77), channel_id=1, source_target_pairs={{0,12},{2,14},{4,8},{6,10},{8,4},{10,6},{12,0},{14,2},{1,13},{3,15... | collective-permute-start | bytes 393224 | tf_op jit(solution)/shard_map/ppermute | solution.py:382
  54.5 12.1 %collective-permute-start.12 = (bf16[32,2048]{1,0:T(8,128)(2,1)S(1)}, bf16[32,2048]{1,0:T(8,128)(2,1)S(1)}, u32[]{:S(2)}, u32[]{:S(2)}) collective-permute-start(bf16[32,2048]{1,0:T(8,128)(2,1)S(1)} %get-tuple-element.84), channel_id=1, source_target_pairs={{0,8},{2,10},{4,12},{6,14},{8,0},{10,2},{12,4},{14,6},{1,9},{3,11}... | collective-permute-start | bytes 393224 | tf_op jit(solution)/shard_map/ppermute | solution.py:382
  97.8 13.8 %collective-permute-start.18 = (bf16[32,2048]{1,0:T(8,128)(2,1)S(1)}, bf16[32,2048]{1,0:T(8,128)(2,1)S(1)}, u32[]{:S(2)}, u32[]{:S(2)}) collective-permute-start(bf16[32,2048]{1,0:T(8,128)(2,1)S(1)} %get-tuple-element.88), channel_id=1, source_target_pairs={{0,12},{2,14},{4,8},{6,10},{8,4},{10,6},{12,0},{14,2},{1,13},{3,15... | collective-permute-start | bytes 393224 | tf_op jit(solution)/shard_map/ppermute | solution.py:382
  98.5 13.2 %collective-permute-start.16 = (bf16[32,2048]{1,0:T(8,128)(2,1)S(1)}, bf16[32,2048]{1,0:T(8,128)(2,1)S(1)}, u32[]{:S(2)}, u32[]{:S(2)}) collective-permute-start(bf16[32,2048]{1,0:T(8,128)(2,1)S(1)} %get-tuple-element.94), channel_id=1, source_target_pairs={{0,4},{2,6},{4,0},{6,2},{8,12},{10,14},{12,8},{14,10},{1,5},{3,7},... | collective-permute-start | bytes 393224 | tf_op jit(solution)/shard_map/ppermute | solution.py:382
  99.0 12.7 %collective-permute-start.17 = (bf16[32,2048]{1,0:T(8,128)(2,1)S(1)}, bf16[32,2048]{1,0:T(8,128)(2,1)S(1)}, u32[]{:S(2)}, u32[]{:S(2)}) collective-permute-start(bf16[32,2048]{1,0:T(8,128)(2,1)S(1)} %get-tuple-element.95), channel_id=1, source_target_pairs={{0,8},{2,10},{4,12},{6,14},{8,0},{10,2},{12,4},{14,6},{1,9},{3,11}... | collective-permute-start | bytes 393224 | tf_op jit(solution)/shard_map/ppermute | solution.py:382
  110.1 13.2 %collective-permute-start.20 = (bf16[32,2048]{1,0:T(8,128)(2,1)S(1)}, bf16[32,2048]{1,0:T(8,128)(2,1)S(1)}, u32[]{:S(2)}, u32[]{:S(2)}) collective-permute-start(bf16[32,2048]{1,0:T(8,128)(2,1)S(1)} %get-tuple-element.97), channel_id=1, source_target_pairs={{0,12},{2,14},{4,8},{6,10},{8,4},{10,6},{12,0},{14,2},{1,13},{3,15... | collective-permute-start | bytes 393224 | tf_op jit(solution)/shard_map/ppermute | solution.py:382
  111.7 12.4 %collective-permute-start.22 = (bf16[128,2048]{1,0:T(8,128)(2,1)S(1)}, bf16[128,2048]{1,0:T(8,128)(2,1)S(1)}, u32[]{:S(2)}, u32[]{:S(2)}) collective-permute-start(bf16[128,2048]{1,0:T(8,128)(2,1)S(1)} %constant_dynamic-update-slice_fusion.8.refs_0_), channel_id=1, source_target_pairs={{0,2},{2,0},{4,6},{6,4},{8,10},{10,8},{12,14},{14,12},{1,3},{3,1},... | collective-permute-start | bytes 1572872 | tf_op jit(solution)/shard_map/ppermute | solution.py:382
  112.2 11.0 %collective-permute-start.19 = (bf16[32,2048]{1,0:T(8,128)(2,1)S(1)}, bf16[32,2048]{1,0:T(8,128)(2,1)S(1)}, u32[]{:S(2)}, u32[]{:S(2)}) collective-permute-start(bf16[32,2048]{1,0:T(8,128)(2,1)S(1)} %get-tuple-element.96), channel_id=1, source_target_pairs={{0,8},{2,10},{4,12},{6,14},{8,0},{10,2},{12,4},{14,6},{1,9},{3,11}... | collective-permute-start | bytes 393224 | tf_op jit(solution)/shard_map/ppermute | solution.py:382
  123.3 11.9 %collective-permute-start.21 = (bf16[128,2048]{1,0:T(8,128)(2,1)S(1)}, bf16[128,2048]{1,0:T(8,128)(2,1)S(1)}, u32[]{:S(2)}, u32[]{:S(2)}) collective-permute-start(bf16[128,2048]{1,0:T(8,128)(2,1)S(1)} %constant_dynamic-update-slice_fusion.12.refs_0_), channel_id=1, source_target_pairs={{0,2},{2,0},{4,6},{6,4},{8,10},{10,8},{12,14},{14,12},{1,3},{3,1},... | collective-permute-start | bytes 1572872 | tf_op jit(solution)/shard_map/ppermute | solution.py:382
  124.5 11.3 %collective-permute-start.23 = (bf16[32,2048]{1,0:T(8,128)(2,1)S(1)}, bf16[32,2048]{1,0:T(8,128)(2,1)S(1)}, u32[]{:S(2)}, u32[]{:S(2)}) collective-permute-start(bf16[32,2048]{1,0:T(8,128)(2,1)S(1)} %get-tuple-element.103), channel_id=1, source_target_pairs={{0,8},{2,10},{4,12},{6,14},{8,0},{10,2},{12,4},{14,6},{1,9},{3,11}... | collective-permute-start | bytes 393224 | tf_op jit(solution)/shard_map/ppermute | solution.py:382
  127.0 12.2 %collective-permute-start.24 = (bf16[32,2048]{1,0:T(8,128)(2,1)S(1)}, bf16[32,2048]{1,0:T(8,128)(2,1)S(1)}, u32[]{:S(2)}, u32[]{:S(2)}) collective-permute-start(bf16[32,2048]{1,0:T(8,128)(2,1)S(1)} %get-tuple-element.106), channel_id=1, source_target_pairs={{0,4},{2,6},{4,0},{6,2},{8,12},{10,14},{12,8},{14,10},{1,5},{3,7},... | collective-permute-start | bytes 393224 | tf_op jit(solution)/shard_map/ppermute | solution.py:382
  127.3 11.9 %collective-permute-start.25 = (bf16[32,2048]{1,0:T(8,128)(2,1)S(1)}, bf16[32,2048]{1,0:T(8,128)(2,1)S(1)}, u32[]{:S(2)}, u32[]{:S(2)}) collective-permute-start(bf16[32,2048]{1,0:T(8,128)(2,1)S(1)} %get-tuple-element.107), channel_id=1, source_target_pairs={{0,12},{2,14},{4,8},{6,10},{8,4},{10,6},{12,0},{14,2},{1,13},{3,15... | collective-permute-start | bytes 393224 | tf_op jit(solution)/shard_map/ppermute | solution.py:382
  135.7 12.1 %collective-permute-start.26 = (bf16[32,2048]{1,0:T(8,128)(2,1)S(1)}, bf16[32,2048]{1,0:T(8,128)(2,1)S(1)}, u32[]{:S(2)}, u32[]{:S(2)}) collective-permute-start(bf16[32,2048]{1,0:T(8,128)(2,1)S(1)} %get-tuple-element.109), channel_id=1, source_target_pairs={{0,4},{2,6},{4,0},{6,2},{8,12},{10,14},{12,8},{14,10},{1,5},{3,7},... | collective-permute-start | bytes 393224 | tf_op jit(solution)/shard_map/ppermute | solution.py:382
  135.8 12.0 %collective-permute-start.28 = (bf16[32,2048]{1,0:T(8,128)(2,1)S(1)}, bf16[32,2048]{1,0:T(8,128)(2,1)S(1)}, u32[]{:S(2)}, u32[]{:S(2)}) collective-permute-start(bf16[32,2048]{1,0:T(8,128)(2,1)S(1)} %get-tuple-element.104), channel_id=1, source_target_pairs={{0,12},{2,14},{4,8},{6,10},{8,4},{10,6},{12,0},{14,2},{1,13},{3,15... | collective-permute-start | bytes 393224 | tf_op jit(solution)/shard_map/ppermute | solution.py:382
  (18 other events, 164.0 us)
